TPU v7x, 32 devices: a whole 2x2x4 slice. The times are simulated.
32 devices in a mesh: dp: 8 (over y, x, core), mp: 4 (over z).
Axes of the slice: x: 2, y: 2, z: 4, core: 2. Of those that a mesh axis runs over, the one named last changes fastest.
Arguments:
- prefix_tokens: bfloat16 [16, 560, 2048], P('dp', 'mp'), may hold values from -6 to 6
- action_tokens: bfloat16 [16, 48, 1024], P('dp', 'mp'), may hold values from -6 to 6
- block_ids: int32 [16, 608], P('dp'), may hold values from 0 to 2, as said below
- live_dims: int32 [16, 32], P('dp'), may hold values from 0 to 1, as said below
- hidden_counts: int32 [4], replicated, may hold values from 256 to 2048, as said below
- pre_attn_gain: float32 [2048], replicated, may hold values from 0.5 to 1.5
- pre_mlp_gain: float32 [2048], replicated, may hold values from 0.5 to 1.5
- act_attn_gain: float32 [1024], replicated, may hold values from 0.5 to 1.5
- act_mlp_gain: float32 [1024], replicated, may hold values from 0.5 to 1.5
- pre_query: bfloat16 [2048, 2048], P(('dp', 'mp')), may hold values from -0.125 to 0.125
- pre_keyval: bfloat16 [2048, 512], P(('dp', 'mp')), may hold values from -0.125 to 0.125
- pre_output: bfloat16 [2048, 2048], P(('dp', 'mp')), may hold values from -3 to 3
- act_query: bfloat16 [1024, 2048], P(('dp', 'mp')), may hold values from -0.1875 to 0.1875
- act_keyval: bfloat16 [1024, 512], P(('dp', 'mp')), may hold values from -0.1875 to 0.1875
- act_output: bfloat16 [2048, 1024], P(('dp', 'mp')), may hold values from -3 to 3
- pre_gate: bfloat16 [2048, 16384], P('dp', 'mp'), may hold values from -0.125 to 0.125
- pre_up: bfloat16 [2048, 16384], P('dp', 'mp'), may hold values from -0.125 to 0.125
- pre_down: bfloat16 [16384, 2048], P('mp', 'dp'), may hold values from -0.046875 to 0.046875
- act_gate: bfloat16 [1024, 8192], P('dp', 'mp'), may hold values from -0.1875 to 0.1875
- act_up: bfloat16 [1024, 8192], P('dp', 'mp'), may hold values from -0.1875 to 0.1875
- act_down: bfloat16 [8192, 1024], P('mp', 'dp'), may hold values from -0.09375 to 0.09375
- action_head: bfloat16 [1024, 32], replicated, may hold values from -0.5 to 0.5
- prefix_cot: bfloat16 [16, 560, 2048], P('dp', 'mp'), may hold values from -6 to 6
- pred_cot: float32 [16, 48, 32], P('dp', 'mp'), may hold values from -6 to 6
Outputs:
- prefix_out: bfloat16 [16, 560, 2048], P('dp', 'mp')
- action_pred: float32 [16, 48, 32], P('dp', 'mp')
- prefix_grad: float32 [16, 560, 2048], P('dp', 'mp')
- action_grad: float32 [16, 48, 1024], P('dp', 'mp')
- grad_pre_attn_gain: float32 [2048], P(('dp', 'mp'))
- grad_pre_mlp_gain: float32 [2048], P(('dp', 'mp'))
- grad_act_attn_gain: float32 [1024], P(('dp', 'mp'))
- grad_act_mlp_gain: float32 [1024], P(('dp', 'mp'))
- grad_pre_query: float32 [2048, 2048], P(('dp', 'mp'))
- grad_pre_keyval: float32 [2048, 512], P(('dp', 'mp'))
- grad_pre_output: float32 [2048, 2048], P(('dp', 'mp'))
- grad_act_query: float32 [1024, 2048], P(('dp', 'mp'))
- grad_act_keyval: float32 [1024, 512], P(('dp', 'mp'))
- grad_act_output: float32 [2048, 1024], P(('dp', 'mp'))
- grad_pre_gate: float32 [2048, 16384], P('dp', 'mp')
- grad_pre_up: float32 [2048, 16384], P('dp', 'mp')
- grad_pre_down: float32 [16384, 2048], P('mp', 'dp')
- grad_act_gate: float32 [1024, 8192], P('dp', 'mp')
- grad_act_up: float32 [1024, 8192], P('dp', 'mp')
- grad_act_down: float32 [8192, 1024], P('mp', 'dp')
- grad_action_head: float32 [1024, 32], P(('dp', 'mp'))
Inputs may be any that keep to these rules, and one draw needn't show every extreme that they name: `block_ids`: along each item: 0 from its first position up to a split inside the prefix, 1 for the rest of its first 560 positions, 2 for its 48 action positions. `live_dims`: each row is 1 on its leading 7 to 18 entries and 0 after; some row has 18 ones and another 7. `hidden_counts`: multiples of 256 that sum to 4096; exactly one equals 2048.
All inputs are finite; a program needn't handle non-finite values.
Results may differ from a plain program's by a relative error of at most 0.018.
Values may be sent and summed in bfloat16 or wider, within the bound.
No kernel may reach another device: no remote copies, remote signals or barrier semaphores. Data moves between devices by JAX's collectives and lax.ppermute only.
A program may use at most 320 MiB of HBM per device.

v0:
```python
import jax
import jax.numpy as jnp
from jax import lax
from jax.sharding import PartitionSpec as P

NORM_EPS = 1e-06
ROPE_BASE = 10000.0
MASKED = -1e30


def rms_norm(values, gain_vec):
    return (
        values * lax.rsqrt(jnp.mean(values * values, axis=-1, keepdims=True) + NORM_EPS) * gain_vec
    )


def rope_tables(positions, head_dim):
    half_dim = head_dim // 2
    inverse = ROPE_BASE ** (-2.0 * jnp.arange(half_dim).astype(jnp.float32) / head_dim)
    angles = positions.astype(jnp.float32)[:, None] * inverse[None, :]
    return (jnp.cos(angles), jnp.sin(angles))


def rotate(values, cosine_tab, sine_tab):
    half_dim = values.shape[-1] // 2
    lower_half = values[..., :half_dim]
    upper_half = values[..., half_dim:]
    return jnp.concatenate(
        [
            lower_half * cosine_tab - upper_half * sine_tab,
            upper_half * cosine_tab + lower_half * sine_tab,
        ],
        axis=-1,
    )


def geglu(gate_pre, upward, live_mask):
    return jax.nn.gelu(gate_pre, approximate=True) * upward * live_mask


def project(rows, weight):
    return jnp.einsum("ird,dc->irc", rows, weight, preferred_element_type=jnp.float32)


def project_back(grads, weight):
    return jnp.einsum("irc,dc->ird", grads, weight, preferred_element_type=jnp.float32)


def outer_sum(rows, grads):
    return jnp.einsum("ird,irc->dc", rows, grads, preferred_element_type=jnp.float32)


def geglu_back(gate_val, up_val, live_mask, hidden_back):

    def unit_fn(gate_in, up_in):
        return geglu(gate_in, up_in, live_mask)

    gate_back, up_back = jax.vjp(unit_fn, gate_val, up_val)[1](hidden_back)
    return (gate_back.astype(jnp.bfloat16), up_back.astype(jnp.bfloat16))


def shards(
    prefix_tokens,
    action_tokens,
    block_ids,
    live_dims,
    hidden_counts,
    pre_attn_gain,
    pre_mlp_gain,
    act_attn_gain,
    act_mlp_gain,
    pre_query,
    pre_keyval,
    pre_output,
    act_query,
    act_keyval,
    act_output,
    pre_gate,
    pre_up,
    pre_down,
    act_gate,
    act_up,
    act_down,
    action_head,
    prefix_cot,
    pred_cot,
):
    groups = lax.axis_size("mp")
    member = lax.axis_index("mp")
    n_items, pre_rows, model_width = prefix_tokens.shape
    act_rows = action_tokens.shape[1]
    pre_len = pre_rows * groups
    head_dim = pre_keyval.shape[1] // 2
    head_count = pre_query.shape[1] // head_dim
    local_len = pre_rows + act_rows
    scale = head_dim ** (-0.5)
    local_pos = jnp.concatenate(
        [
            member * pre_rows + jnp.arange(pre_rows),
            pre_len + member * act_rows + jnp.arange(act_rows),
        ]
    )
    cosine_tab, sine_tab = rope_tables(local_pos, head_dim)
    local_blocks = jnp.concatenate(
        [
            lax.dynamic_slice_in_dim(block_ids, member * pre_rows, pre_rows, 1),
            lax.dynamic_slice_in_dim(block_ids, pre_len + member * act_rows, act_rows, 1),
        ],
        axis=1,
    )
    allowed = block_ids[:, None, None, :] <= local_blocks[:, None, :, None]
    attn_local = (pre_query, pre_keyval, pre_output, act_query, act_keyval, act_output)
    attn_full = (
        lax.all_gather(attn_local[0], ("dp", "mp"), axis=0, tiled=True),
        lax.all_gather(attn_local[1], ("dp", "mp"), axis=0, tiled=True),
        lax.all_gather(attn_local[2], ("dp", "mp"), axis=0, tiled=True),
        lax.all_gather(attn_local[3], ("dp", "mp"), axis=0, tiled=True),
        lax.all_gather(attn_local[4], ("dp", "mp"), axis=0, tiled=True),
        lax.all_gather(attn_local[5], ("dp", "mp"), axis=0, tiled=True),
    )
    pre_x = prefix_tokens.astype(jnp.float32)
    act_x = action_tokens.astype(jnp.float32)
    pre_normed = rms_norm(pre_x, pre_attn_gain).astype(jnp.bfloat16)
    act_normed = rms_norm(act_x, act_attn_gain).astype(jnp.bfloat16)
    query_raw = jnp.concatenate(
        [project(pre_normed, attn_full[0]), project(act_normed, attn_full[3])], axis=1
    )
    query_rows = rotate(
        query_raw.reshape(n_items, local_len, head_count, head_dim),
        cosine_tab[:, None, :],
        sine_tab[:, None, :],
    ).astype(jnp.bfloat16)
    keyval_raw = jnp.concatenate(
        [project(pre_normed, attn_full[1]), project(act_normed, attn_full[4])], axis=1
    )
    keyval_rows = jnp.concatenate(
        [rotate(keyval_raw[..., :head_dim], cosine_tab, sine_tab), keyval_raw[..., head_dim:]],
        axis=-1,
    ).astype(jnp.bfloat16)
    pre_keys, act_keys = (
        lax.all_gather(keyval_rows[:, :pre_rows], "mp", axis=1, tiled=True),
        lax.all_gather(keyval_rows[:, pre_rows:], "mp", axis=1, tiled=True),
    )
    all_keyval = jnp.concatenate([pre_keys, act_keys], axis=1)
    key_rows = all_keyval[..., :head_dim]
    value_rows = all_keyval[..., head_dim:]
    scores = (
        jnp.einsum("iqhd,ikd->ihqk", query_rows, key_rows, preferred_element_type=jnp.float32)
        * scale
    )
    probs = jax.nn.softmax(jnp.where(allowed, scores, MASKED), axis=-1)
    probs_low = probs.astype(jnp.bfloat16)
    attended = jnp.einsum(
        "ihqk,ikd->iqhd", probs_low, value_rows, preferred_element_type=jnp.float32
    )
    attended = attended.astype(jnp.bfloat16).reshape(n_items, local_len, head_count * head_dim)
    pre_mid = pre_x + project(attended[:, :pre_rows], attn_full[2])
    act_mid = act_x + project(attended[:, pre_rows:], attn_full[5])
    pre_second = rms_norm(pre_mid, pre_mlp_gain).astype(jnp.bfloat16)
    act_second = rms_norm(act_mid, act_mlp_gain).astype(jnp.bfloat16)
    pre_gathered, act_gathered = (
        lax.all_gather(pre_second, "mp", axis=1, tiled=True),
        lax.all_gather(act_second, "mp", axis=1, tiled=True),
    )
    mlp_local = (pre_gate, pre_up, pre_down, act_gate, act_up, act_down)
    mlp_full = (
        lax.all_gather(mlp_local[0], "dp", axis=0, tiled=True),
        lax.all_gather(mlp_local[1], "dp", axis=0, tiled=True),
        lax.all_gather(mlp_local[2], "dp", axis=1, tiled=True),
        lax.all_gather(mlp_local[3], "dp", axis=0, tiled=True),
        lax.all_gather(mlp_local[4], "dp", axis=0, tiled=True),
        lax.all_gather(mlp_local[5], "dp", axis=1, tiled=True),
    )
    slot_count = lax.dynamic_index_in_dim(hidden_counts, member, keepdims=False)
    slot_live = (jnp.arange(act_gate.shape[1]) < slot_count).astype(jnp.float32)
    pre_gate_val = project(pre_gathered, mlp_full[0])
    pre_up_val = project(pre_gathered, mlp_full[1])
    pre_hidden = geglu(pre_gate_val, pre_up_val, 1.0).astype(jnp.bfloat16)
    act_gate_val = project(act_gathered, mlp_full[3])
    act_up_val = project(act_gathered, mlp_full[4])
    act_hidden = geglu(act_gate_val, act_up_val, slot_live).astype(jnp.bfloat16)
    pre_sums, act_sums = (
        lax.psum_scatter(
            project(pre_hidden, mlp_full[2]).astype(jnp.bfloat16),
            "mp",
            scatter_dimension=1,
            tiled=True,
        ).astype(jnp.float32),
        lax.psum_scatter(
            project(act_hidden, mlp_full[5]).astype(jnp.bfloat16),
            "mp",
            scatter_dimension=1,
            tiled=True,
        ).astype(jnp.float32),
    )
    pre_final = pre_mid + pre_sums
    act_final = act_mid + act_sums
    prefix_out = pre_final.astype(jnp.bfloat16)
    act_final_low = act_final.astype(jnp.bfloat16)
    live_mask = live_dims[:, None, :].astype(jnp.float32)
    action_pred = project(act_final_low, action_head) * live_mask
    pred_back = (pred_cot * live_mask).astype(jnp.bfloat16)
    grad_head = outer_sum(act_final_low, pred_back)
    act_final_back = project_back(pred_back, action_head)
    pre_grad_rows, act_grad_rows = (
        lax.all_gather(prefix_cot, "mp", axis=1, tiled=True),
        lax.all_gather(act_final_back.astype(jnp.bfloat16), "mp", axis=1, tiled=True),
    )
    mlp_back = (
        lax.all_gather(mlp_local[0], "dp", axis=0, tiled=True),
        lax.all_gather(mlp_local[1], "dp", axis=0, tiled=True),
        lax.all_gather(mlp_local[2], "dp", axis=1, tiled=True),
        lax.all_gather(mlp_local[3], "dp", axis=0, tiled=True),
        lax.all_gather(mlp_local[4], "dp", axis=0, tiled=True),
        lax.all_gather(mlp_local[5], "dp", axis=1, tiled=True),
    )
    grad_pre_down = outer_sum(pre_hidden, pre_grad_rows)
    grad_act_down = outer_sum(act_hidden, act_grad_rows)
    pre_gate_back, pre_up_back = geglu_back(
        pre_gate_val, pre_up_val, 1.0, project_back(pre_grad_rows, mlp_back[2])
    )
    act_gate_back, act_up_back = geglu_back(
        act_gate_val, act_up_val, slot_live, project_back(act_grad_rows, mlp_back[5])
    )
    grad_pre_gate = outer_sum(pre_gathered, pre_gate_back)
    grad_pre_up = outer_sum(pre_gathered, pre_up_back)
    grad_act_gate = outer_sum(act_gathered, act_gate_back)
    grad_act_up = outer_sum(act_gathered, act_up_back)
    pre_second_part = project_back(pre_gate_back, mlp_back[0]) + project_back(
        pre_up_back, mlp_back[1]
    )
    act_second_part = project_back(act_gate_back, mlp_back[3]) + project_back(
        act_up_back, mlp_back[4]
    )
    mlp_reduced = (
        lax.psum_scatter(
            grad_pre_gate.astype(jnp.bfloat16), "dp", scatter_dimension=0, tiled=True
        ).astype(jnp.float32),
        lax.psum_scatter(
            grad_pre_up.astype(jnp.bfloat16), "dp", scatter_dimension=0, tiled=True
        ).astype(jnp.float32),
        lax.psum_scatter(
            grad_pre_down.astype(jnp.bfloat16), "dp", scatter_dimension=1, tiled=True
        ).astype(jnp.float32),
        lax.psum_scatter(
            grad_act_gate.astype(jnp.bfloat16), "dp", scatter_dimension=0, tiled=True
        ).astype(jnp.float32),
        lax.psum_scatter(
            grad_act_up.astype(jnp.bfloat16), "dp", scatter_dimension=0, tiled=True
        ).astype(jnp.float32),
        lax.psum_scatter(
            grad_act_down.astype(jnp.bfloat16), "dp", scatter_dimension=1, tiled=True
        ).astype(jnp.float32),
    )
    pre_second_back, act_second_back = (
        lax.psum_scatter(pre_second_part, "mp", scatter_dimension=1, tiled=True),
        lax.psum_scatter(act_second_part, "mp", scatter_dimension=1, tiled=True),
    )
    pre_mid_part, grad_pre_mlp_gain = jax.vjp(rms_norm, pre_mid, pre_mlp_gain)[1](pre_second_back)
    act_mid_part, grad_act_mlp_gain = jax.vjp(rms_norm, act_mid, act_mlp_gain)[1](act_second_back)
    pre_mid_grad = prefix_cot.astype(jnp.float32) + pre_mid_part
    act_mid_grad = act_final_back + act_mid_part
    attn_back = (
        lax.all_gather(attn_local[0], ("dp", "mp"), axis=0, tiled=True),
        lax.all_gather(attn_local[1], ("dp", "mp"), axis=0, tiled=True),
        lax.all_gather(attn_local[2], ("dp", "mp"), axis=0, tiled=True),
        lax.all_gather(attn_local[3], ("dp", "mp"), axis=0, tiled=True),
        lax.all_gather(attn_local[4], ("dp", "mp"), axis=0, tiled=True),
        lax.all_gather(attn_local[5], ("dp", "mp"), axis=0, tiled=True),
    )
    pre_out_back = pre_mid_grad.astype(jnp.bfloat16)
    act_out_back = act_mid_grad.astype(jnp.bfloat16)
    grad_pre_output = outer_sum(attended[:, :pre_rows], pre_out_back)
    grad_act_output = outer_sum(attended[:, pre_rows:], act_out_back)
    attended_back = (
        jnp.concatenate(
            [project_back(pre_out_back, attn_back[2]), project_back(act_out_back, attn_back[5])],
            axis=1,
        )
        .astype(jnp.bfloat16)
        .reshape(n_items, local_len, head_count, head_dim)
    )
    probs_back = jnp.einsum(
        "iqhd,ikd->ihqk", attended_back, value_rows, preferred_element_type=jnp.float32
    )
    value_back = jnp.einsum(
        "ihqk,iqhd->ikd", probs_low, attended_back, preferred_element_type=jnp.float32
    )
    scores_back = (
        probs * (probs_back - jnp.sum(probs * probs_back, axis=-1, keepdims=True))
    ).astype(jnp.bfloat16)
    query_back = (
        jnp.einsum("ihqk,ikd->iqhd", scores_back, key_rows, preferred_element_type=jnp.float32)
        * scale
    )
    key_back = (
        jnp.einsum("ihqk,iqhd->ikd", scores_back, query_rows, preferred_element_type=jnp.float32)
        * scale
    )
    keyval_back = jnp.concatenate([key_back, value_back], axis=-1)
    pre_kv_back, act_kv_back = (
        lax.psum_scatter(
            keyval_back[:, :pre_len].astype(jnp.bfloat16), "mp", scatter_dimension=1, tiled=True
        ).astype(jnp.float32),
        lax.psum_scatter(
            keyval_back[:, pre_len:].astype(jnp.bfloat16), "mp", scatter_dimension=1, tiled=True
        ).astype(jnp.float32),
    )
    own_kv_back = jnp.concatenate([pre_kv_back, act_kv_back], axis=1)
    keyval_low = jnp.concatenate(
        [rotate(own_kv_back[..., :head_dim], cosine_tab, -sine_tab), own_kv_back[..., head_dim:]],
        axis=-1,
    ).astype(jnp.bfloat16)
    query_low = rotate(query_back, cosine_tab[:, None, :], -sine_tab[:, None, :])
    query_low = query_low.reshape(n_items, local_len, head_count * head_dim).astype(jnp.bfloat16)
    grad_pre_query = outer_sum(pre_normed, query_low[:, :pre_rows])
    grad_pre_keyval = outer_sum(pre_normed, keyval_low[:, :pre_rows])
    grad_act_query = outer_sum(act_normed, query_low[:, pre_rows:])
    grad_act_keyval = outer_sum(act_normed, keyval_low[:, pre_rows:])
    pre_normed_back = project_back(query_low[:, :pre_rows], attn_back[0]) + project_back(
        keyval_low[:, :pre_rows], attn_back[1]
    )
    act_normed_back = project_back(query_low[:, pre_rows:], attn_back[3]) + project_back(
        keyval_low[:, pre_rows:], attn_back[4]
    )
    pre_x_part, grad_pre_attn_gain = jax.vjp(rms_norm, pre_x, pre_attn_gain)[1](pre_normed_back)
    act_x_part, grad_act_attn_gain = jax.vjp(rms_norm, act_x, act_attn_gain)[1](act_normed_back)
    prefix_grad = pre_mid_grad + pre_x_part
    action_grad = act_mid_grad + act_x_part
    attn_reduced = (
        lax.psum_scatter(grad_pre_attn_gain, ("dp", "mp"), scatter_dimension=0, tiled=True),
        lax.psum_scatter(grad_pre_mlp_gain, ("dp", "mp"), scatter_dimension=0, tiled=True),
        lax.psum_scatter(grad_act_attn_gain, ("dp", "mp"), scatter_dimension=0, tiled=True),
        lax.psum_scatter(grad_act_mlp_gain, ("dp", "mp"), scatter_dimension=0, tiled=True),
        lax.psum_scatter(grad_pre_query, ("dp", "mp"), scatter_dimension=0, tiled=True),
        lax.psum_scatter(grad_pre_keyval, ("dp", "mp"), scatter_dimension=0, tiled=True),
        lax.psum_scatter(grad_pre_output, ("dp", "mp"), scatter_dimension=0, tiled=True),
        lax.psum_scatter(grad_act_query, ("dp", "mp"), scatter_dimension=0, tiled=True),
        lax.psum_scatter(grad_act_keyval, ("dp", "mp"), scatter_dimension=0, tiled=True),
        lax.psum_scatter(grad_act_output, ("dp", "mp"), scatter_dimension=0, tiled=True),
        lax.psum_scatter(grad_head, ("dp", "mp"), scatter_dimension=0, tiled=True),
    )
    return (
        prefix_out,
        action_pred,
        prefix_grad,
        action_grad,
        attn_reduced[0],
        attn_reduced[1],
        attn_reduced[2],
        attn_reduced[3],
        attn_reduced[4],
        attn_reduced[5],
        attn_reduced[6],
        attn_reduced[7],
        attn_reduced[8],
        attn_reduced[9],
        mlp_reduced[0],
        mlp_reduced[1],
        mlp_reduced[2],
        mlp_reduced[3],
        mlp_reduced[4],
        mlp_reduced[5],
        attn_reduced[10],
    )


def solution(mesh):
    in_specs = (
        P("dp", "mp", None),
        P("dp", "mp", None),
        P("dp", None),
        P("dp", None),
        P(),
        P(),
        P(),
        P(),
        P(),
        P(("dp", "mp"), None),
        P(("dp", "mp"), None),
        P(("dp", "mp"), None),
        P(("dp", "mp"), None),
        P(("dp", "mp"), None),
        P(("dp", "mp"), None),
        P("dp", "mp"),
        P("dp", "mp"),
        P("mp", "dp"),
        P("dp", "mp"),
        P("dp", "mp"),
        P("mp", "dp"),
        P(),
        P("dp", "mp", None),
        P("dp", "mp", None),
    )
    out_specs = (
        P("dp", "mp", None),
        P("dp", "mp", None),
        P("dp", "mp", None),
        P("dp", "mp", None),
        P(("dp", "mp")),
        P(("dp", "mp")),
        P(("dp", "mp")),
        P(("dp", "mp")),
        P(("dp", "mp"), None),
        P(("dp", "mp"), None),
        P(("dp", "mp"), None),
        P(("dp", "mp"), None),
        P(("dp", "mp"), None),
        P(("dp", "mp"), None),
        P("dp", "mp"),
        P("dp", "mp"),
        P("mp", "dp"),
        P("dp", "mp"),
        P("dp", "mp"),
        P("mp", "dp"),
        P(("dp", "mp"), None),
    )
    return jax.shard_map(shards, mesh=mesh, in_specs=in_specs, out_specs=out_specs, check_vma=False)
```

profile of v0, /device:TPU:0, one launch (start us, length us, event | category | flops | bytes accessed | tf_op | source)
XLA Modules:
  0.0 3761.1 jit_solution(17438975461930933890)
XLA Ops:
  12.8 54.8 %all-gather.18.cloned.1.call-done = bf16[1024,512]{1,0:T(8,128)(2,1)} async-done(((bf16[32,512]{1,0:T(8,128)(2,1)}), bf16[1024,512]{1,0:T(8,128)(2,1)}) %all-gather.18.cloned.1.call-update) | async-done | bytes 1048592 | tf_op jit(solution)/shard_map/all_gather | solution.py:118
  69.1 56.8 %all-gather.16.cloned.1.call-done = bf16[2048,512]{1,0:T(8,128)(2,1)} async-done(((bf16[64,512]{1,0:T(8,128)(2,1)}), bf16[2048,512]{1,0:T(8,128)(2,1)}) %all-gather.16.cloned.1.call-update) | async-done | bytes 2097168 | tf_op jit(solution)/shard_map/all_gather | solution.py:115
  160.9 63.1 %all-gather.24.cloned.1.call-done = bf16[1024,2048]{1,0:T(8,128)(2,1)} async-done(((bf16[32,2048]{1,0:T(8,128)(2,1)}), bf16[1024,2048]{1,0:T(8,128)(2,1)}) %all-gather.24.cloned.1.call-update) | async-done | bytes 4194320 | tf_op jit(solution)/shard_map/all_gather | solution.py:117
  227.1 75.7 %all-gather.22.cloned.1.call-done = bf16[2048,2048]{1,0:T(8,128)(2,1)} async-done(((bf16[64,2048]{1,0:T(8,128)(2,1)}), bf16[2048,2048]{1,0:T(8,128)(2,1)}) %all-gather.22.cloned.1.call-update) | async-done | bytes 8388624 | tf_op jit(solution)/shard_map/all_gather | solution.py:114
  318.7 62.9 %all-gather.26.cloned.1.call-done = bf16[2048,2048]{1,0:T(8,128)(2,1)} async-done(((bf16[64,2048]{1,0:T(8,128)(2,1)}), bf16[2048,2048]{1,0:T(8,128)(2,1)}) %all-gather.26.cloned.1.call-update) | async-done | bytes 8388624 | tf_op jit(solution)/shard_map/all_gather | solution.py:116
  423.1 61.5 %all-gather.36.cloned.1.call-done = bf16[2048,1024]{1,0:T(8,128)(2,1)} async-done(((bf16[64,1024]{1,0:T(8,128)(2,1)}), bf16[2048,1024]{1,0:T(8,128)(2,1)}) %all-gather.36.cloned.1.call-update) | async-done | bytes 4194320 | tf_op jit(solution)/shard_map/all_gather | solution.py:119
  524.8 35.5 all-gather.38.cloned.1.call-done
  569.8 80.0 %all-gather.28.cloned.1.call-done = bf16[2,560,2048]{2,0,1:T(2,128)(2,1)} async-done(((bf16[2,140,2048]{2,0,1:T(2,128)(2,1)}), bf16[2,560,2048]{2,0,1:T(2,128)(2,1)}) %all-gather.28.cloned.1.call-update) | async-done | bytes 4587536 | tf_op jit(solution)/shard_map/all_gather | solution.py:162
  649.7 90.1 %all-gather.32.cloned.1.call-done = bf16[2048,4096]{1,0:T(8,128)(2,1)} async-done(((bf16[256,4096]{1,0:T(8,128)(2,1)}), bf16[2048,4096]{1,0:T(8,128)(2,1)}) %all-gather.32.cloned.1.call-update) | async-done | bytes 16777232 | tf_op jit(solution)/shard_map/all_gather | solution.py:168
  739.9 28.7 fusion.14
  768.6 60.1 %all-gather.44.cloned.1.call-done = bf16[2,560,2048]{2,0,1:T(2,128)(2,1)} async-done(((bf16[2,140,2048]{2,0,1:T(2,128)(2,1)}), bf16[2,560,2048]{2,0,1:T(2,128)(2,1)}) %all-gather.44.cloned.1.call-update) | async-done | bytes 4587536 | tf_op jit(solution)/shard_map/all_gather | solution.py:206
  828.7 93.4 %all-gather.34.cloned.1.call-done = bf16[4096,2048]{1,0:T(8,128)(2,1)} async-done(((bf16[4096,256]{1,0:T(8,128)(2,1)}), bf16[4096,2048]{1,0:T(8,128)(2,1)}) %all-gather.34.cloned.1.call-update) | async-done | bytes 16777232 | tf_op jit(solution)/shard_map/all_gather | solution.py:169
  950.8 62.9 %all-gather.30.cloned.1.call-done = bf16[2048,4096]{1,0:T(8,128)(2,1)} async-done(((bf16[256,4096]{1,0:T(8,128)(2,1)}), bf16[2048,4096]{1,0:T(8,128)(2,1)}) %all-gather.30.cloned.1.call-update) | async-done | bytes 16777232 | tf_op jit(solution)/shard_map/all_gather | solution.py:167
  1013.7 46.8 %fusion.7 = (bf16[2,560,4096]{2,1,0:T(8,128)(2,1)}, bf16[2,560,4096]{2,1,0:T(8,128)(2,1)}, bf16[2,560,4096]{2,1,0:T(8,128)(2,1)}) fusion(f32[2,560,4096]{2,1,0:T(8,128)} %fusion.8, f32[2,560,4096]{2,1,0:T(8,128)} %fusion.14, bf16[2048,4096]{1,0:T(8,128)(2,1)} %all-gather.30.cloned.1.call-done, bf16[2,560,2048]{2,0,1:T(2,128)(2,1)} %all-gather.28.cloned.1.call-done), kind=kOutput, calls=%fused_computation.12 | convolution fusion | flops 18909757440 | bytes 85590016 | tf_op jit(solution)/shard_map/ird,dc->irc/dot_general | solution.py:42
  1164.3 288.0 %all-reduce.16.cloned.1.call-done = (f32[2,560,2048]{2,0,1:T(2,128)}, f32[2,48,1024]{2,0,1:T(2,128)}) async-done(((f32[2,560,2048]{2,0,1:T(2,128)}, f32[2,48,1024]{2,0,1:T(2,128)}), (f32[2,560,2048]{2,0,1:T(2,128)}, f32[2,48,1024]{2,0,1:T(2,128)})) %all-reduce.16.cloned.1.call-update) | async-done | bytes 9568272
  1510.9 40.2 %bitcast_convert_fusion.2 = bf16[2048,4096]{1,0:T(8,128)(2,1)} fusion(bf16[2,560,4096]{2,1,0:T(8,128)(2,1)} %get-tuple-element.102, bf16[2,560,2048]{2,0,1:T(2,128)(2,1)} %all-gather.28.cloned.1.call-done), kind=kOutput, calls=%fused_computation.3 | convolution fusion | flops 18798870528 | bytes 30539776 | tf_op jit(solution)/shard_map/ird,irc->dc/dot_general | solution.py:50
  1551.1 40.4 %bitcast_convert_fusion.1 = bf16[2048,4096]{1,0:T(8,128)(2,1)} fusion(bf16[2,560,4096]{2,1,0:T(8,128)(2,1)} %get-tuple-element.103, bf16[2,560,2048]{2,0,1:T(2,128)(2,1)} %all-gather.28.cloned.1.call-done), kind=kOutput, calls=%fused_computation.2 | convolution fusion | flops 18798870528 | bytes 30539776 | tf_op jit(solution)/shard_map/ird,irc->dc/dot_general | solution.py:50
  1591.6 30.2 bitcast_convert_fusion
  1621.9 81.7 %all-reduce.18.cloned.1.call-done = (bf16[2,560,2048]{2,0,1:T(2,128)(2,1)}, bf16[2,48,1024]{2,0,1:T(2,128)(2,1)}, bf16[2,560,512]{2,0,1:T(2,128)(2,1)}, bf16[2,48,512]{2,0,1:T(2,128)(2,1)}) async-done(((bf16[2,560,2048]{2,0,1:T(2,128)(2,1)}, bf16[2,48,1024]{2,0,1:T(2,128)(2,1)}, bf16[2,560,512]{2,0,1:T(2,128)(2,1)}, bf16[2,48,512]{2,0,1:T(2,128)(2,1)}), (bf16[2,560,2048]{2,0,1:T(2,128)(2,1)}, ...) | async-done | bytes 6029328
  1761.2 52.1 %reduce-scatter.34.cloned.1.call-done = bf16[128,2048]{1,0:T(8,128)(2,1)} async-done(((bf16[1024,2048]{1,0:T(8,128)(2,1)}), bf16[128,2048]{1,0:T(8,128)(2,1)}) %reduce-scatter.34.cloned.1.call-update) | async-done | bytes 524304 | tf_op jit(solution)/shard_map/reduce_scatter | solution.py:245
  1815.4 53.4 %reduce-scatter.36.cloned.1.call-done = bf16[128,2048]{1,0:T(8,128)(2,1)} async-done(((bf16[1024,2048]{1,0:T(8,128)(2,1)}), bf16[128,2048]{1,0:T(8,128)(2,1)}) %reduce-scatter.36.cloned.1.call-update) | async-done | bytes 524304 | tf_op jit(solution)/shard_map/reduce_scatter | solution.py:248
  1892.2 39.9 %all-reduce.10 = (f32[2048]{0:T(1024)S(1)}, f32[2048]{0:T(1024)S(1)}, f32[1024]{0:T(1024)S(1)}, f32[1024]{0:T(1024)S(1)}) all-reduce(f32[2048]{0:T(1024)S(1)} %get-tuple-element.86, f32[2048]{0:T(1024)S(1)} %copy-done.60, f32[1024]{0:T(1024)S(1)} %get-tuple-element.90, ...), channel_id=8, replica_groups=mesh['dp'=8,'mp'=4] {'dp','mp'}, use_global_device_ids=true, to_apply=%region_18.19.clone | all-reduce | flops 6144 | bytes 49152
  1934.4 54.6 %reduce-scatter.28.cloned.1.call-done = bf16[256,4096]{1,0:T(8,128)(2,1)} async-done(((bf16[2048,4096]{1,0:T(8,128)(2,1)}), bf16[256,4096]{1,0:T(8,128)(2,1)}) %reduce-scatter.28.cloned.1.call-update) | async-done | bytes 2097168 | tf_op jit(solution)/shard_map/reduce_scatter | solution.py:236
  1993.2 115.5 %reduce-scatter.30.cloned.1.call-done = bf16[256,4096]{1,0:T(8,128)(2,1)} async-done(((bf16[2048,4096]{1,0:T(8,128)(2,1)}), bf16[256,4096]{1,0:T(8,128)(2,1)}) %reduce-scatter.30.cloned.1.call-update) | async-done | bytes 2097168 | tf_op jit(solution)/shard_map/reduce_scatter | solution.py:239
  2112.7 115.4 %reduce-scatter.32.cloned.1.call-done = bf16[4096,256]{1,0:T(8,128)(2,1)} async-done(((bf16[4096,2048]{1,0:T(8,128)(2,1)}), bf16[4096,256]{1,0:T(8,128)(2,1)}) %reduce-scatter.32.cloned.1.call-update) | async-done | bytes 2097168 | tf_op jit(solution)/shard_map/reduce_scatter | solution.py:242
  2232.1 132.8 %reduce-scatter.38.cloned.1.call-done = f32[32,32]{1,0:T(8,128)} async-done(((f32[1024,32]{1,0:T(8,128)}), f32[32,32]{1,0:T(8,128)}) %reduce-scatter.38.cloned.1.call-update) | async-done | bytes 4112 | tf_op jit(solution)/shard_map/reduce_scatter | solution.py:341
  2364.9 137.5 %reduce-scatter.24.cloned.1.call-done = f32[32,512]{1,0:T(8,128)} async-done(((f32[1024,512]{1,0:T(8,128)}), f32[32,512]{1,0:T(8,128)}) %reduce-scatter.24.cloned.1.call-update) | async-done | bytes 65552 | tf_op jit(solution)/shard_map/reduce_scatter | solution.py:339
  2502.4 148.4 %reduce-scatter.18.cloned.1.call-done = f32[64,512]{1,0:T(8,128)} async-done(((f32[2048,512]{1,0:T(8,128)}), f32[64,512]{1,0:T(8,128)}) %reduce-scatter.18.cloned.1.call-update) | async-done | bytes 131088 | tf_op jit(solution)/shard_map/reduce_scatter | solution.py:336
  2650.8 187.2 %reduce-scatter.22.cloned.1.call-done = f32[32,2048]{1,0:T(8,128)} async-done(((f32[1024,2048]{1,0:T(8,128)}), f32[32,2048]{1,0:T(8,128)}) %reduce-scatter.22.cloned.1.call-update) | async-done | bytes 262160 | tf_op jit(solution)/shard_map/reduce_scatter | solution.py:338
  2838.0 186.4 %reduce-scatter.26.cloned.1.call-done = f32[64,1024]{1,0:T(8,128)} async-done(((f32[2048,1024]{1,0:T(8,128)}), f32[64,1024]{1,0:T(8,128)}) %reduce-scatter.26.cloned.1.call-update) | async-done | bytes 262160 | tf_op jit(solution)/shard_map/reduce_scatter | solution.py:340
  3024.3 364.8 %reduce-scatter.16.cloned.1.call-done = f32[64,2048]{1,0:T(8,128)} async-done(((f32[2048,2048]{1,0:T(8,128)}), f32[64,2048]{1,0:T(8,128)}) %reduce-scatter.16.cloned.1.call-update) | async-done | bytes 524304 | tf_op jit(solution)/shard_map/reduce_scatter | solution.py:335
  3389.1 364.9 %reduce-scatter.20.cloned.1.call-done = f32[64,2048]{1,0:T(8,128)} async-done(((f32[2048,2048]{1,0:T(8,128)}), f32[64,2048]{1,0:T(8,128)}) %reduce-scatter.20.cloned.1.call-update) | async-done | bytes 524304 | tf_op jit(solution)/shard_map/reduce_scatter | solution.py:337
  (385 shorter events, 438.2 us)
Async XLA Ops:
  7.2 386.5 %copy-start = (bf16[1024,32]{0,1:T(8,128)(2,1)S(1)}, bf16[1024,32]{0,1:T(8,128)(2,1)}, u32[]{:S(2)}) copy-start(bf16[1024,32]{0,1:T(8,128)(2,1)} %param.45) | copy-start | bytes 196612
  7.2 60.3 %all-gather.18.cloned.1.call-start = ((), (), s32[]{:S(2)}) async-start(), calls=%async_computation.14 | async-start | bytes 1081344 | tf_op jit(solution)/shard_map/all_gather | solution.py:118
  8.0 118.0 %all-gather.16.cloned.1.call-start = ((), (), s32[]{:S(2)}) async-start(), calls=%async_computation.13 | async-start | bytes 2162688 | tf_op jit(solution)/shard_map/all_gather | solution.py:115
  8.7 150.8 %all-gather.20.cloned.1.call-start = ((), (), s32[]{:S(2)}) async-start(), calls=%async_computation.15 | async-start | bytes 1433600 | tf_op jit(solution)/shard_map/all_gather | solution.py:141
  129.7 94.3 %all-gather.24.cloned.1.call-start = ((), (), s32[]{:S(2)}) async-start(), calls=%async_computation.17 | async-start | bytes 4325376 | tf_op jit(solution)/shard_map/all_gather | solution.py:117
  130.3 172.5 %all-gather.22.cloned.1.call-start = ((), (), s32[]{:S(2)}) async-start(), calls=%async_computation.16 | async-start | bytes 8650752 | tf_op jit(solution)/shard_map/all_gather | solution.py:114
  130.9 250.7 %all-gather.26.cloned.1.call-start = ((), (), s32[]{:S(2)}) async-start(), calls=%async_computation.18 | async-start | bytes 8650752 | tf_op jit(solution)/shard_map/all_gather | solution.py:116
  131.5 288.0 %all-gather.42.cloned.1.call-start = ((), (), s32[]{:S(2)}) async-start(), calls=%async_computation.26 | async-start | bytes 4718592 | tf_op jit(solution)/shard_map/all_gather | solution.py:172
  132.2 352.4 %all-gather.36.cloned.1.call-start = ((), (), s32[]{:S(2)}) async-start(), calls=%async_computation.23 | async-start | bytes 4325376 | tf_op jit(solution)/shard_map/all_gather | solution.py:119
  133.0 388.9 %all-gather.40.cloned.1.call-start = ((), (), s32[]{:S(2)}) async-start(), calls=%async_computation.25 | async-start | bytes 4718592 | tf_op jit(solution)/shard_map/all_gather | solution.py:171
  133.7 426.6 %all-gather.38.cloned.1.call-start = ((), (), s32[]{:S(2)}) async-start(), calls=%async_computation.24 | async-start | bytes 4718592 | tf_op jit(solution)/shard_map/all_gather | solution.py:170
  134.3 515.5 %all-gather.28.cloned.1.call-start = ((), (), s32[]{:S(2)}) async-start(), calls=%async_computation.19 | async-start | bytes 5734400 | tf_op jit(solution)/shard_map/all_gather | solution.py:162
  391.0 348.8 %all-gather.32.cloned.1.call-start = ((), (), s32[]{:S(2)}) async-start(), calls=%async_computation.21 | async-start | bytes 18874368 | tf_op jit(solution)/shard_map/all_gather | solution.py:168
  391.7 437.1 %all-gather.44.cloned.1.call-start = ((), (), s32[]{:S(2)}) async-start(), calls=%async_computation.27 | async-start | bytes 5734400 | tf_op jit(solution)/shard_map/all_gather | solution.py:206
  392.4 529.7 %all-gather.34.cloned.1.call-start = ((), (), s32[]{:S(2)}) async-start(), calls=%async_computation.22 | async-start | bytes 18874368 | tf_op jit(solution)/shard_map/all_gather | solution.py:169
  393.0 620.7 %all-gather.30.cloned.1.call-start = ((), (), s32[]{:S(2)}) async-start(), calls=%async_computation.20 | async-start | bytes 18874368 | tf_op jit(solution)/shard_map/all_gather | solution.py:167
  393.6 1058.7 %all-reduce.16.cloned.1.call-start = ((), (), s32[]{:S(2)}) async-start(), calls=%async_computation.41 | async-start | bytes 19136512
  1122.6 581.1 %all-reduce.18.cloned.1.call-start = ((), (), s32[]{:S(2)}) async-start(), calls=%async_computation.42 | async-start | bytes 12058624
  1155.1 298.8 %copy-start.49 = (f32[2,12,1024]{2,1,0:T(8,128)S(1)}, f32[2,12,1024]{2,1,0:T(8,128)}, u32[]{:S(2)}) copy-start(f32[2,12,1024]{2,1,0:T(8,128)} %get-tuple-element.128) | copy-start | bytes 294916
  1489.1 269.8 %reduce-scatter.40.cloned.1.call-start = ((), (), s32[]{:S(2)}) async-start(), calls=%async_computation.40 | async-start | bytes 4718592
  1501.2 312.1 %reduce-scatter.34.cloned.1.call-start = ((), (), s32[]{:S(2)}) async-start(), calls=%async_computation.37 | async-start | bytes 4718592 | tf_op jit(solution)/shard_map/reduce_scatter | solution.py:245
  1506.4 362.4 %reduce-scatter.36.cloned.1.call-start = ((), (), s32[]{:S(2)}) async-start(), calls=%async_computation.38 | async-start | bytes 4718592 | tf_op jit(solution)/shard_map/reduce_scatter | solution.py:248
  1510.8 478.3 %reduce-scatter.28.cloned.1.call-start = ((), (), s32[]{:S(2)}) async-start(), calls=%async_computation.34 | async-start | bytes 18874368 | tf_op jit(solution)/shard_map/reduce_scatter | solution.py:236
  1551.0 557.6 %reduce-scatter.30.cloned.1.call-start = ((), (), s32[]{:S(2)}) async-start(), calls=%async_computation.35 | async-start | bytes 18874368 | tf_op jit(solution)/shard_map/reduce_scatter | solution.py:239
  1591.5 636.6 %reduce-scatter.32.cloned.1.call-start = ((), (), s32[]{:S(2)}) async-start(), calls=%async_computation.36 | async-start | bytes 18874368 | tf_op jit(solution)/shard_map/reduce_scatter | solution.py:242
  1621.8 743.1 %reduce-scatter.38.cloned.1.call-start = ((), (), s32[]{:S(2)}) async-start(), calls=%async_computation.39 | async-start | bytes 540672 | tf_op jit(solution)/shard_map/reduce_scatter | solution.py:341
  1711.5 790.9 %reduce-scatter.24.cloned.1.call-start = ((), (), s32[]{:S(2)}) async-start(), calls=%async_computation.32 | async-start | bytes 2162688 | tf_op jit(solution)/shard_map/reduce_scatter | solution.py:339
  1715.8 934.9 %reduce-scatter.18.cloned.1.call-start = ((), (), s32[]{:S(2)}) async-start(), calls=%async_computation.29 | async-start | bytes 4325376 | tf_op jit(solution)/shard_map/reduce_scatter | solution.py:336
  1722.6 1115.3 %reduce-scatter.22.cloned.1.call-start = ((), (), s32[]{:S(2)}) async-start(), calls=%async_computation.31 | async-start | bytes 8650752 | tf_op jit(solution)/shard_map/reduce_scatter | solution.py:338
  1731.5 1292.8 %reduce-scatter.26.cloned.1.call-start = ((), (), s32[]{:S(2)}) async-start(), calls=%async_computation.33 | async-start | bytes 8650752 | tf_op jit(solution)/shard_map/reduce_scatter | solution.py:340
  1737.4 1651.7 %reduce-scatter.16.cloned.1.call-start = ((), (), s32[]{:S(2)}) async-start(), calls=%async_computation.28 | async-start | bytes 17301504 | tf_op jit(solution)/shard_map/reduce_scatter | solution.py:335
  1748.5 2005.5 %reduce-scatter.20.cloned.1.call-start = ((), (), s32[]{:S(2)}) async-start(), calls=%async_computation.30 | async-start | bytes 17301504 | tf_op jit(solution)/shard_map/reduce_scatter | solution.py:337
  (88 other events, 3798.3 us)
Sparse Core Ops, SparseCore 0:
  11.0 56.4 all-gather.17
  70.5 55.4 all-gather.15
  129.8 29.5 all-gather.19
  162.3 61.6 all-gather.23
  226.8 75.9 all-gather.21
  305.5 75.9 all-gather.25
  383.4 36.0 all-gather.41
  422.5 62.0 all-gather.35
  486.5 35.2 all-gather.39
  523.6 36.7 all-gather.37
  562.5 87.2 all-gather.27
  651.5 88.3 all-gather.31
  741.4 87.2 all-gather.43
  830.4 91.5 all-gather.33
  923.8 89.8 all-gather.29
  1122.7 329.5 all-reduce.15
  1489.2 214.3 all-reduce.17
  1707.8 50.1 reduce-scatter.39
  1762.0 51.3 reduce-scatter.33
  1817.5 51.2 reduce-scatter.35
  1872.4 116.6 reduce-scatter.27
  1992.6 115.9 reduce-scatter.29
  2112.2 115.9 reduce-scatter.31
  2230.8 133.9 reduce-scatter.37
  2367.8 134.5 reduce-scatter.23
  2505.1 145.6 reduce-scatter.17
  2653.5 184.4 reduce-scatter.21
  2840.8 183.4 reduce-scatter.25
  3027.2 361.8 reduce-scatter.15
  3391.8 362.1 reduce-scatter.19
where the time goes:
time: 3770 us; the launch traced here: 3760 us
  waiting for transfers between devices  3130 us (83%)
  matrix products  414 us (11%)
  blocking collectives  81.3 us (2%)
  local copies, waits for them, and re-layouts  78.4 us (2%)
  other arithmetic  40.8 us (1%)
    unnamed x33, waiting for transfers between devices  378 us
    reduce_scatter x1, waiting for transfers between devices, shards(): lax.psum_scatter(grad_pre_output, ('dp', 'mp'), scatter_dimension=0, tile...  365 us
    reduce_scatter x1, waiting for transfers between devices, shards(): lax.psum_scatter(grad_pre_query, ('dp', 'mp'), scatter_dimension=0, tiled...  365 us
    reduce_scatter x1, waiting for transfers between devices, shards(): lax.psum_scatter(grad_act_query, ('dp', 'mp'), scatter_dimension=0, tiled...  187 us
    reduce_scatter x1, waiting for transfers between devices, shards(): lax.psum_scatter(grad_act_output, ('dp', 'mp'), scatter_dimension=0, tile...  186 us
    dot_general x13, matrix products, outer_sum(): jnp.einsum('ird,irc->dc', rows, grads, preferred_element_type=jnp.float32)  161 us
    reduce_scatter x1, waiting for transfers between devices, shards(): lax.psum_scatter(grad_pre_keyval, ('dp', 'mp'), scatter_dimension=0, tile...  148 us
    reduce_scatter x1, waiting for transfers between devices, shards(): lax.psum_scatter(grad_act_keyval, ('dp', 'mp'), scatter_dimension=0, tile...  137 us
  transfers between devices with their start and end apart: 30, of which 29 were waited for; matrix products, arithmetic and copies ran while one was open for 10% of the time, Pallas kernels for 0%

commit v1 on v0

v1 whole, which is shorter than its diff:
```python
import jax
import jax.numpy as jnp
from jax import lax
from jax.experimental import pallas as pl
from jax.experimental.pallas import tpu as pltpu
from jax.sharding import PartitionSpec as P

NORM_EPS = 1e-06
ROPE_BASE = 10000.0
MASKED = -1e30
F32 = jnp.float32
BF16 = jnp.bfloat16


def hop(value, bit):
    size = lax.axis_size("dp")
    return lax.ppermute(value, "dp", [(d, d ^ bit) for d in range(size)])


def ring_up(value):
    size = lax.axis_size("mp")
    return lax.ppermute(value, "mp", [(d, (d + 1) % size) for d in range(size)])


def ring_down(value):
    size = lax.axis_size("mp")
    return lax.ppermute(value, "mp", [(d, (d - 1) % size) for d in range(size)])


def ring_gather(value):
    out = [value]
    for _ in range(lax.axis_size("mp") - 1):
        out.append(ring_up(out[-1]))
    return out


def ring_scatter(parts):
    total = parts[-1].astype(BF16)
    for part in parts[-2::-1]:
        total = ring_down(total.astype(BF16)).astype(F32) + part.astype(F32)
    return total


def chip_order(size):
    return sorted(range(1, size), key=lambda c: (bin(c).count("1"), c))


def rel_blocks():
    size = lax.axis_size("dp")
    place = jnp.arange(size, dtype=jnp.int32)
    half = size // 2
    rel = (place % half) * 2 + place // half
    return jnp.bitwise_xor(rel, lax.axis_index("dp").astype(jnp.int32))


def dp_gather(shard):
    chips = lax.axis_size("dp") // 2
    half = shard.shape[0] // 2
    got = {0: [shard]}

    def top(c):
        return got[c][0] if len(got[c]) == 2 else got[c][0][:half]

    def bottom(c):
        return got[c][1] if len(got[c]) == 2 else got[c][0][half:]

    for c in chip_order(chips):
        high, low = 1 << (c.bit_length() - 1), c & -c
        if high == low:
            got[c] = [hop(shard, 2 * high)]
        else:
            got[c] = [hop(top(c ^ high), 2 * high), hop(bottom(c ^ low), 2 * low)]
    own = [piece for c in range(chips) for piece in got[c]]
    return own + [hop(piece, 1) for piece in own]


def dp_scatter(own, other):
    chips = lax.axis_size("dp") // 2
    rows = own.shape[0] // chips
    half = rows // 2
    other = hop(other, 1)

    def term(start):
        cut = slice(start, start + half)
        return own[cut].astype(F32) + other[cut].astype(F32)

    acc = {c: [term(c * rows), term(c * rows + half)] for c in range(chips)}
    for c in reversed(chip_order(chips)):
        high, low = 1 << (c.bit_length() - 1), c & -c
        up, down = (piece.astype(BF16) for piece in acc[c])
        acc[c ^ high][0] = acc[c ^ high][0] + hop(up, 2 * high).astype(F32)
        acc[c ^ low][1] = acc[c ^ low][1] + hop(down, 2 * low).astype(F32)
    return jnp.concatenate(acc[0], axis=0)


def _copy_block(_, src, dst):
    dst[...] = src[...]


def permute_columns(values, order, inverse=False):
    count = order.shape[0]
    rows, width = values.shape
    block = width // count
    if block % 128:
        hit = order[:, None] == jnp.arange(count, dtype=order.dtype)[None, :]
        places = jnp.arange(count, dtype=order.dtype)
        back = jnp.sum(jnp.where(hit, places[:, None], 0), axis=0) if inverse else order
        split = values.reshape(rows, count, block)
        cuts = [lax.dynamic_slice_in_dim(split, back[g], 1, 1) for g in range(count)]
        return jnp.concatenate(cuts, axis=1).reshape(rows, width)
    here = pl.BlockSpec((rows, block), lambda g, idx: (0, g))
    there = pl.BlockSpec((rows, block), lambda g, idx: (0, idx[g]))
    return pl.pallas_call(
        _copy_block,
        grid_spec=pltpu.PrefetchScalarGridSpec(
            num_scalar_prefetch=1,
            grid=(count,),
            in_specs=[here if inverse else there],
            out_specs=there if inverse else here,
        ),
        out_shape=jax.ShapeDtypeStruct(values.shape, values.dtype),
    )(order, values)


def inverse_rms(values):
    return lax.rsqrt(jnp.mean(values * values, axis=-1, keepdims=True) + NORM_EPS)


def rms_norm(values, gain_vec):
    return values * inverse_rms(values) * gain_vec


def rms_back(values, gain_vec, grads):
    inverse = inverse_rms(values)
    unit = values * inverse
    scaled = gain_vec * grads
    mean = jnp.mean(unit * scaled, axis=-1, keepdims=True)
    return inverse * (scaled - unit * mean), jnp.sum(grads * unit, axis=0)


def rope_tables(positions, head_dim):
    half_dim = head_dim // 2
    inverse = ROPE_BASE ** (-2.0 * jnp.arange(half_dim).astype(F32) / head_dim)
    angles = positions.astype(F32)[:, None] * inverse[None, :]
    return (jnp.cos(angles), jnp.sin(angles))


def rotate(values, cosine_tab, sine_tab):
    half_dim = values.shape[-1] // 2
    lower_half = values[..., :half_dim]
    upper_half = values[..., half_dim:]
    return jnp.concatenate(
        [
            lower_half * cosine_tab - upper_half * sine_tab,
            upper_half * cosine_tab + lower_half * sine_tab,
        ],
        axis=-1,
    )


def mm(left, right):
    return lax.dot_general(left, right, (((1,), (0,)), ((), ())), preferred_element_type=F32)


def mm_nt(left, right):
    return lax.dot_general(left, right, (((1,), (1,)), ((), ())), preferred_element_type=F32)


def mm_tn(left, right):
    return lax.dot_general(left, right, (((0,), (0,)), ((), ())), preferred_element_type=F32)


def geglu(gate_val, up_val, live_mask):
    return jax.nn.gelu(gate_val, approximate=True) * up_val * live_mask


def feed_forward(rows, cot_rows, gate, up, down_t, live_mask):
    gate_val = mm(rows, gate)
    up_val = mm(rows, up)
    hidden_back = mm(cot_rows, down_t)
    hidden, pull = jax.vjp(lambda g, u: geglu(g, u, live_mask), gate_val, up_val)
    gate_back, up_back = pull(hidden_back)
    return hidden.astype(BF16), gate_back.astype(BF16), up_back.astype(BF16)


def shards(
    prefix_tokens,
    action_tokens,
    block_ids,
    live_dims,
    hidden_counts,
    pre_attn_gain,
    pre_mlp_gain,
    act_attn_gain,
    act_mlp_gain,
    pre_query,
    pre_keyval,
    pre_output,
    act_query,
    act_keyval,
    act_output,
    pre_gate,
    pre_up,
    pre_down,
    act_gate,
    act_up,
    act_down,
    action_head,
    prefix_cot,
    pred_cot,
):
    groups = lax.axis_size("mp")
    ways = lax.axis_size("dp")
    member = lax.axis_index("mp")
    items, pre_rows, width = prefix_tokens.shape
    act_rows, act_width = action_tokens.shape[1:]
    pre_len = pre_rows * groups
    head_dim = pre_keyval.shape[1] // 2
    query_width = pre_query.shape[1]
    heads = query_width // head_dim
    local_len = pre_rows + act_rows
    scale = head_dim ** (-0.5)
    order = rel_blocks()

    pre_part, act_part, out_part = pre_query.shape[0], act_query.shape[0], pre_output.shape[0]
    qkv_own = jnp.concatenate(
        [
            jnp.concatenate([pre_query, pre_keyval], axis=1),
            jnp.concatenate([act_query, act_keyval], axis=1),
        ],
        axis=0,
    )
    out_own = jnp.concatenate([pre_output, act_output], axis=1)

    def in_place(pieces):
        size = pieces[0].shape[0]
        twice = jnp.concatenate(pieces[::-1] * 2, axis=0)
        return lax.dynamic_slice_in_dim(twice, (groups - 1 - member) * size, groups * size, 0)

    qkv_ring = ring_gather(qkv_own)
    out_ring = ring_gather(out_own)
    qkv_block = jnp.concatenate(
        [
            in_place([piece[:pre_part] for piece in qkv_ring]),
            in_place([piece[pre_part:] for piece in qkv_ring]),
        ],
        axis=0,
    )
    pre_block = groups * pre_part
    out_block = in_place(out_ring)
    qkv_pieces = dp_gather(qkv_block)
    out_full = jnp.concatenate(dp_gather(out_block), axis=0)
    qkv_all = jnp.concatenate(qkv_pieces, axis=0).reshape(ways, -1, qkv_own.shape[1])
    pre_qkv = qkv_all[:, :pre_block].reshape(width, -1)
    act_qkv = qkv_all[:, pre_block:].reshape(act_width, -1)
    pre_out_w = out_full[:, :width]
    act_out_w = out_full[:, width:]

    gate_full = jnp.concatenate(dp_gather(pre_gate), axis=0)
    up_full = jnp.concatenate(dp_gather(pre_up), axis=0)
    down_full = jnp.concatenate(dp_gather(pre_down.T), axis=0)
    act_stack = jnp.concatenate([act_gate, act_up, act_down.T], axis=0)
    act_all = jnp.concatenate(dp_gather(act_stack), axis=0).reshape(ways, 3, -1, act_gate.shape[1])
    act_gate_full, act_up_full, act_down_full = (
        act_all[:, n].reshape(act_width, -1) for n in range(3)
    )

    pre_flat = prefix_tokens.reshape(items * pre_rows, width)
    act_flat = action_tokens.reshape(items * act_rows, act_width)
    cot_flat = prefix_cot.reshape(items * pre_rows, width)
    pre_x = pre_flat.astype(F32)
    act_x = act_flat.astype(F32)
    live_mask = live_dims[:, None, :].astype(F32)
    pred_back = (pred_cot * live_mask).astype(BF16).reshape(items * act_rows, -1)
    act_final_back = mm_nt(pred_back, action_head)
    cot_rel = permute_columns(cot_flat, order)
    act_cot_rel = permute_columns(act_final_back.astype(BF16), order)
    cot_all = jnp.concatenate(ring_gather(cot_rel), axis=0)
    act_cot_all = jnp.concatenate(ring_gather(act_cot_rel), axis=0)

    local_pos = jnp.concatenate(
        [
            member * pre_rows + jnp.arange(pre_rows),
            pre_len + member * act_rows + jnp.arange(act_rows),
        ]
    )
    cosine_tab, sine_tab = rope_tables(local_pos, head_dim)

    def blocks_of(which):
        return jnp.concatenate(
            [
                lax.dynamic_slice_in_dim(block_ids, which * pre_rows, pre_rows, 1),
                lax.dynamic_slice_in_dim(block_ids, pre_len + which * act_rows, act_rows, 1),
            ],
            axis=1,
        )

    local_blocks = blocks_of(member)
    key_blocks = jnp.concatenate(
        [blocks_of((member - r) % groups) for r in range(groups)], axis=1
    )
    allowed = key_blocks[:, None, None, :] <= local_blocks[:, None, :, None]

    def join(pre_part_rows, act_part_rows):
        return jnp.concatenate(
            [
                pre_part_rows.reshape(items, pre_rows, -1),
                act_part_rows.reshape(items, act_rows, -1),
            ],
            axis=1,
        )

    def part(joined):
        flat = joined.shape[-1]
        return (
            joined[:, :pre_rows].reshape(items * pre_rows, flat),
            joined[:, pre_rows:].reshape(items * act_rows, flat),
        )

    pre_normed = permute_columns(rms_norm(pre_x, pre_attn_gain).astype(BF16), order)
    act_normed = permute_columns(rms_norm(act_x, act_attn_gain).astype(BF16), order)
    keyval_raw = join(mm(pre_normed, pre_qkv[:, query_width:]), mm(act_normed, act_qkv[:, query_width:]))
    keyval_rows = jnp.concatenate(
        [rotate(keyval_raw[..., :head_dim], cosine_tab, sine_tab), keyval_raw[..., head_dim:]],
        axis=-1,
    ).astype(BF16)
    all_keyval = jnp.concatenate(ring_gather(keyval_rows), axis=1)
    key_rows = all_keyval[..., :head_dim]
    value_rows = all_keyval[..., head_dim:]
    query_raw = join(mm(pre_normed, pre_qkv[:, :query_width]), mm(act_normed, act_qkv[:, :query_width]))
    query_rows = rotate(
        query_raw.reshape(items, local_len, heads, head_dim),
        cosine_tab[:, None, :],
        sine_tab[:, None, :],
    ).astype(BF16)
    scores = (
        jnp.einsum("iqhd,ikd->ihqk", query_rows, key_rows, preferred_element_type=F32) * scale
    )
    probs = jax.nn.softmax(jnp.where(allowed, scores, MASKED), axis=-1)
    probs_low = probs.astype(BF16)
    attended = jnp.einsum("ihqk,ikd->iqhd", probs_low, value_rows, preferred_element_type=F32)
    attended = attended.astype(BF16).reshape(items, local_len, query_width)
    pre_att, act_att = (permute_columns(rows, order) for rows in part(attended))
    pre_mid = pre_x + mm(pre_att, pre_out_w)
    act_mid = act_x + mm(act_att, act_out_w)

    pre_second = permute_columns(rms_norm(pre_mid, pre_mlp_gain).astype(BF16), order)
    act_second = permute_columns(rms_norm(act_mid, act_mlp_gain).astype(BF16), order)
    pre_all = jnp.concatenate(ring_gather(pre_second), axis=0)
    act_all_rows = jnp.concatenate(ring_gather(act_second), axis=0)
    slot_count = lax.dynamic_index_in_dim(hidden_counts, member, keepdims=False)
    slot_live = (jnp.arange(act_gate.shape[1]) < slot_count).astype(F32)

    pre_hidden, pre_gate_back, pre_up_back = feed_forward(
        pre_all, cot_all, gate_full, up_full, down_full, 1.0
    )
    act_hidden, act_gate_back, act_up_back = feed_forward(
        act_all_rows, act_cot_all, act_gate_full, act_up_full, act_down_full, slot_live
    )

    def weight_grad(rows, grads):
        half = rows.shape[1] // 2
        return (
            mm_tn(rows[:, :half], grads).astype(BF16),
            mm_tn(rows[:, half:], grads).astype(BF16),
        )

    grad_pre_gate = dp_scatter(*weight_grad(pre_all, pre_gate_back))
    pre_second_part = mm_nt(pre_gate_back, gate_full) + mm_nt(pre_up_back, up_full)
    act_second_part = mm_nt(act_gate_back, act_gate_full) + mm_nt(act_up_back, act_up_full)
    grad_pre_up = dp_scatter(*weight_grad(pre_all, pre_up_back))
    grad_pre_down = dp_scatter(*weight_grad(cot_all, pre_hidden)).T
    act_terms = [
        weight_grad(act_all_rows, act_gate_back),
        weight_grad(act_all_rows, act_up_back),
        weight_grad(act_cot_all, act_hidden),
    ]

    def act_stacked(which):
        parts = [term[which].reshape(ways // 2, -1, act_gate.shape[1]) for term in act_terms]
        return jnp.concatenate(parts, axis=1).reshape(-1, act_gate.shape[1])

    grad_act = dp_scatter(act_stacked(0), act_stacked(1)).reshape(3, -1, act_gate.shape[1])
    grad_act_gate, grad_act_up, grad_act_down = grad_act[0], grad_act[1], grad_act[2].T

    def row_sums(partial):
        count = partial.shape[0] // groups
        return ring_scatter([partial[r * count : (r + 1) * count] for r in range(groups)])

    pre_second_back = permute_columns(row_sums(pre_second_part), order, True)
    act_second_back = permute_columns(row_sums(act_second_part), order, True)
    pre_sums = permute_columns(row_sums(mm_nt(pre_hidden, down_full)), order, True)
    act_sums = permute_columns(row_sums(mm_nt(act_hidden, act_down_full)), order, True)

    prefix_out = (pre_mid + pre_sums).astype(BF16).reshape(prefix_tokens.shape)
    act_final_low = (act_mid + act_sums).astype(BF16)
    action_pred = mm(act_final_low, action_head).reshape(pred_cot.shape) * live_mask
    grad_head = mm_tn(act_final_low, pred_back)

    pre_mid_part, grad_pre_mlp_gain = rms_back(pre_mid, pre_mlp_gain, pre_second_back)
    act_mid_part, grad_act_mlp_gain = rms_back(act_mid, act_mlp_gain, act_second_back)
    pre_mid_grad = cot_flat.astype(F32) + pre_mid_part
    act_mid_grad = act_final_back + act_mid_part
    pre_out_back = pre_mid_grad.astype(BF16)
    act_out_back = act_mid_grad.astype(BF16)
    out_half = query_width // 2
    out_own_grad, out_other_grad = (
        jnp.concatenate(
            [mm_tn(pre_att[:, cut], pre_out_back), mm_tn(act_att[:, cut], act_out_back)], axis=1
        ).astype(BF16)
        for cut in (slice(0, out_half), slice(out_half, None))
    )
    grad_out = dp_scatter(out_own_grad, out_other_grad)
    attended_back = join(
        permute_columns(mm_nt(pre_out_back, pre_out_w).astype(BF16), order, True),
        permute_columns(mm_nt(act_out_back, act_out_w).astype(BF16), order, True),
    ).reshape(items, local_len, heads, head_dim)
    probs_back = jnp.einsum(
        "iqhd,ikd->ihqk", attended_back, value_rows, preferred_element_type=F32
    )
    value_back = jnp.einsum(
        "ihqk,iqhd->ikd", probs_low, attended_back, preferred_element_type=F32
    )
    scores_back = (
        probs * (probs_back - jnp.sum(probs * probs_back, axis=-1, keepdims=True))
    ).astype(BF16)
    key_back = (
        jnp.einsum("ihqk,iqhd->ikd", scores_back, query_rows, preferred_element_type=F32) * scale
    )
    query_back = (
        jnp.einsum("ihqk,ikd->iqhd", scores_back, key_rows, preferred_element_type=F32) * scale
    )
    keyval_back = jnp.concatenate([key_back, value_back], axis=-1).astype(BF16)
    own_kv_back = ring_scatter(
        [keyval_back[:, r * local_len : (r + 1) * local_len] for r in range(groups)]
    )
    keyval_low = jnp.concatenate(
        [rotate(own_kv_back[..., :head_dim], cosine_tab, -sine_tab), own_kv_back[..., head_dim:]],
        axis=-1,
    ).astype(BF16)
    query_low = rotate(query_back, cosine_tab[:, None, :], -sine_tab[:, None, :])
    query_low = query_low.reshape(items, local_len, query_width).astype(BF16)
    pre_back, act_back = part(jnp.concatenate([query_low, keyval_low], axis=-1))

    def qkv_term(which):
        pre_half, act_half = width // 2, act_width // 2
        pre_grad = mm_tn(pre_normed[:, which * pre_half : (which + 1) * pre_half], pre_back)
        act_grad = mm_tn(act_normed[:, which * act_half : (which + 1) * act_half], act_back)
        parts = [
            grad.astype(BF16).reshape(ways // 2, -1, grad.shape[1]) for grad in (pre_grad, act_grad)
        ]
        return jnp.concatenate(parts, axis=1).reshape(-1, pre_back.shape[1])

    grad_qkv = dp_scatter(qkv_term(0), qkv_term(1))

    def for_members(block):
        size = block.shape[0] // groups
        return [
            lax.dynamic_slice_in_dim(block, ((member - r) % groups) * size, size, 0)
            for r in range(groups)
        ]

    grad_out = ring_scatter(for_members(grad_out))
    grad_qkv = ring_scatter(
        [
            jnp.concatenate([upper, lower], axis=0)
            for upper, lower in zip(
                for_members(grad_qkv[:pre_block]), for_members(grad_qkv[pre_block:])
            )
        ]
    )
    pre_normed_back = permute_columns(mm_nt(pre_back, pre_qkv), order, True)
    act_normed_back = permute_columns(mm_nt(act_back, act_qkv), order, True)
    pre_x_part, grad_pre_attn_gain = rms_back(pre_x, pre_attn_gain, pre_normed_back)
    act_x_part, grad_act_attn_gain = rms_back(act_x, act_attn_gain, act_normed_back)
    prefix_grad = (pre_mid_grad + pre_x_part).reshape(prefix_tokens.shape)
    action_grad = (act_mid_grad + act_x_part).reshape(action_tokens.shape)

    devices = ways * groups
    small = jnp.concatenate(
        [
            value.reshape(devices, -1)
            for value in (
                grad_pre_attn_gain,
                grad_pre_mlp_gain,
                grad_act_attn_gain,
                grad_act_mlp_gain,
                grad_head,
            )
        ],
        axis=1,
    )
    bit = 1
    while bit < ways:
        small = small + hop(small, bit)
        bit *= 2
    mine = lax.axis_index("dp") * groups
    terms = [
        lax.dynamic_slice_in_dim(small, mine + (member - r) % groups, 1, 0) for r in range(groups)
    ]
    total = terms[-1]
    for term in terms[-2::-1]:
        total = ring_down(total) + term
    sizes = [width // devices] * 2 + [act_width // devices] * 2
    gains, start = [], 0
    for size in sizes:
        gains.append(total[0, start : start + size])
        start += size
    grad_head = total[0, start:].reshape(act_width // devices, -1)

    return (
        prefix_out,
        action_pred,
        prefix_grad,
        action_grad,
        *gains,
        grad_qkv[:pre_part, :query_width],
        grad_qkv[:pre_part, query_width:],
        grad_out[:, :width],
        grad_qkv[pre_part:, :query_width],
        grad_qkv[pre_part:, query_width:],
        grad_out[:, width:],
        grad_pre_gate,
        grad_pre_up,
        grad_pre_down,
        grad_act_gate,
        grad_act_up,
        grad_act_down,
        grad_head,
    )


def solution(mesh):
    rows = P("dp", "mp", None)
    both = P(("dp", "mp"), None)
    wide = P("dp", "mp")
    tall = P("mp", "dp")
    in_specs = (
        (rows, rows, P("dp", None), P("dp", None))
        + (P(),) * 5
        + (both,) * 6
        + (wide, wide, tall, wide, wide, tall, P(), rows, rows)
    )
    out_specs = (
        (rows,) * 4
        + (P(("dp", "mp")),) * 4
        + (both,) * 6
        + (wide, wide, tall, wide, wide, tall, both)
    )
    return jax.shard_map(shards, mesh=mesh, in_specs=in_specs, out_specs=out_specs, check_vma=False)
```

time: 3770 us -> 1860 us (0.49)
  waiting for transfers between devices: 3130 us -> 843 us
  other arithmetic: 40.8 us -> 202 us
  local copies, waits for them, and re-layouts: 78.4 us -> 204 us
  starting transfers between devices: 1.41 us -> 123 us
  Pallas kernels: 0 us -> 87.7 us
  blocking collectives: 81.3 us -> 0 us
    reduce_scatter x12 -> x0, waiting for transfers between devices: 1910 us -> none  [the longest x1 365 us: shards(): lax.psum_scatter(grad_pre_output, ('dp', 'mp'), scatter_dimension=0, tile...]
    ppermute x0 -> x144, waiting for transfers between devices: none -> 843 us  [the longest x99 647 us: hop(): return lax.ppermute(value, 'dp', [(d, d ^ bit) for d in range(size)])]
    all_gather x15 -> x0, waiting for transfers between devices: 837 us -> none  [the longest x1 93.4 us: shards(): lax.all_gather(mlp_local[2], 'dp', axis=1, tiled=True)]
    unnamed x33 -> x0, waiting for transfers between devices: 378 us -> none
    ppermute x0 -> x144, starting transfers between devices: none -> 123 us  [the longest x99 64.7 us: hop(): return lax.ppermute(value, 'dp', [(d, d ^ bit) for d in range(size)])]
    unnamed x199 -> x392, local copies, waits for them, and re-layouts: 44.5 us -> 135 us
    pallas_call x0 -> x16, Pallas kernels: none -> 87.7 us  [permute_columns(): pl.pallas_call(_copy_block, grid_spec=pltpu.PrefetchScalarGridSpec(num_sc...]
    concatenate x5 -> x21, other arithmetic: 3.38 us -> 62 us  [the longest x2 13.5 us: act_stacked(): return jnp.concatenate(parts, axis=1).reshape(-1, act_gate.shape[1])]
  transfers between devices with their start and end apart: 30 -> 144, of which waited for: 29 -> 61; matrix products, arithmetic and copies ran while one was open for 10% -> 41% of each run, Pallas kernels for 0% -> 4%
where the time goes in v1:
time: 1860 us; the launch traced here: 1840 us
  waiting for transfers between devices  843 us (45%)
  matrix products  380 us (20%)
  local copies, waits for them, and re-layouts  204 us (11%)
  other arithmetic  202 us (11%)
  starting transfers between devices  123 us (7%)
  Pallas kernels  87.7 us (5%)
    ppermute x99, waiting for transfers between devices, hop(): return lax.ppermute(value, 'dp', [(d, d ^ bit) for d in range(size)])  647 us
    unnamed x392, local copies, waits for them, and re-layouts  135 us
    dot_general x21, matrix products, mm_tn(): lax.dot_general(left, right, (((0,), (0,)), ((), ())), preferred_element_...  134 us
    dot_general x13, matrix products, mm(): lax.dot_general(left, right, (((1,), (0,)), ((), ())), preferred_element_...  124 us
    dot_general x11, matrix products, mm_nt(): lax.dot_general(left, right, (((1,), (1,)), ((), ())), preferred_element_...  106 us
    ppermute x24, waiting for transfers between devices, ring_down(): return lax.ppermute(value, 'mp', [(d, (d - 1) % size) for d in range(size)])  99.1 us
    ppermute x21, waiting for transfers between devices, ring_up(): return lax.ppermute(value, 'mp', [(d, (d + 1) % size) for d in range(size)])  96.7 us
    pallas_call x16, Pallas kernels, permute_columns(): pl.pallas_call(_copy_block, grid_spec=pltpu.PrefetchScalarGridSpec(num_sc...  87.7 us
  transfers between devices with their start and end apart: 144, of which 61 were waited for; matrix products, arithmetic and copies ran while one was open for 41% of the time, Pallas kernels for 4%

profile of v1, /device:TPU:0, one launch (start us, length us, event | category | flops | bytes accessed | tf_op | source)
XLA Modules:
  0.0 1842.0 jit_solution(10964233832634113379)
XLA Ops:
  109.8 58.1 %collective-permute-done.63 = bf16[384,2048]{1,0:T(8,128)(2,1)S(1)} collective-permute-done((bf16[384,2048]{1,0:T(8,128)(2,1)}, bf16[384,2048]{1,0:T(8,128)(2,1)S(1)}, u32[]{:S(2)}, u32[]{:S(2)}) %collective-permute-start.63) | collective-permute-done | bytes 1572896 | tf_op jit(solution)/shard_map/ppermute | solution.py:17
  184.9 31.8 %collective-permute-done.40 = bf16[256,4096]{1,0:T(8,128)(2,1)S(1)} collective-permute-done((bf16[256,4096]{1,0:T(8,128)(2,1)}, bf16[256,4096]{1,0:T(8,128)(2,1)S(1)}, u32[]{:S(2)}, u32[]{:S(2)}) %collective-permute-start.40) | collective-permute-done | bytes 2097184 | tf_op jit(solution)/shard_map/ppermute | solution.py:17
  229.8 31.9 %collective-permute-done.31 = bf16[256,4096]{1,0:T(8,128)(2,1)} collective-permute-done((bf16[256,4096]{1,0:T(8,128)(2,1)}, bf16[256,4096]{1,0:T(8,128)(2,1)}, u32[]{:S(2)}, u32[]{:S(2)}) %collective-permute-start.31) | collective-permute-done | bytes 2097184 | tf_op jit(solution)/shard_map/ppermute | solution.py:17
  285.8 26.4 %collective-permute-done.19 = bf16[256,3072]{1,0:T(8,128)(2,1)S(1)} collective-permute-done((bf16[256,3072]{1,0:T(8,128)(2,1)}, bf16[256,3072]{1,0:T(8,128)(2,1)S(1)}, u32[]{:S(2)}, u32[]{:S(2)}) %collective-permute-start.19) | collective-permute-done | bytes 1572896 | tf_op jit(solution)/shard_map/ppermute | solution.py:17
  315.3 19.4 %collective-permute-done.50 = bf16[128,4096]{0,1:T(8,128)(2,1)S(1)} collective-permute-done((bf16[128,4096]{0,1:T(8,128)(2,1)}, bf16[128,4096]{0,1:T(8,128)(2,1)S(1)}, u32[]{:S(2)}, u32[]{:S(2)}) %collective-permute-start.50) | collective-permute-done | bytes 1048608 | tf_op jit(solution)/shard_map/ppermute | solution.py:17
  337.4 16.8 collective-permute-done.41
  404.8 18.8 %collective-permute-done.77 = bf16[280,2048]{1,0:T(8,128)(2,1)} collective-permute-done((bf16[280,2048]{1,0:T(8,128)(2,1)}, bf16[280,2048]{1,0:T(8,128)(2,1)}, u32[]{:S(2)}, u32[]{:S(2)}) %collective-permute-start.77) | collective-permute-done | bytes 1146912 | tf_op jit(solution)/shard_map/ppermute | solution.py:22
  468.1 25.9 %fusion.148 = f32[1120,4096]{1,0:T(8,128)} fusion(bf16[2048,4096]{0,1:T(8,128)(2,1)} %constant_dynamic-update-slice_fusion.59, bf16[280,2048]{1,0:T(8,128)(2,1)} %collective-permute-done.77, bf16[280,2048]{1,0:T(8,128)(2,1)} %collective-permute-done.76, bf16[280,2048]{1,0:T(8,128)(2,1)} %copy-done.60, bf16[280,2048]{1,0:T(8,128)(2,1)} %shard_map.399), kind=kOutput, calls=%fused_computation.493 | convolution fusion | flops 18808832000 | bytes 39714816 | tf_op jit(solution)/shard_map/dot_general | solution.py:162
  750.9 24.7 %fusion.149 = f32[1120,4096]{1,0:T(8,128)} fusion(bf16[2048,4096]{1,0:T(8,128)(2,1)} %constant_dynamic-update-slice_fusion.49, bf16[280,2048]{1,0:T(8,128)(2,1)} %collective-permute-done.29, bf16[280,2048]{1,0:T(8,128)(2,1)} %collective-permute-done.28, bf16[280,2048]{1,0:T(8,128)(2,1)S(1)} %copy-done.63, bf16[280,2048]{1,0:T(8,128)(2,1)S(1)} %copy-done.33), kind=kOutput, calls=%fused_computation.494 | convolution fusion | flops 18808832000 | bytes 39714816 | tf_op jit(solution)/shard_map/dot_general | solution.py:162
  775.6 47.4 %fusion.7 = (bf16[1120,4096]{1,0:T(8,128)(2,1)}, bf16[1120,4096]{1,0:T(8,128)(2,1)}, bf16[1120,4096]{1,0:T(8,128)(2,1)}) fusion(f32[1120,4096]{1,0:T(8,128)} %fusion.148, f32[1120,4096]{1,0:T(8,128)} %fusion.149, bf16[2048,4096]{1,0:T(8,128)(2,1)} %constant_dynamic-update-slice_fusion.39, bf16[280,2048]{1,0:T(8,128)(2,1)} %collective-permute-done.29, ...), kind=kOutput, calls=%fused_computation.9 | convolution fusion | flops 18928107520 | bytes 85590016 | tf_op jit(solution)/shard_map/dot_general | solution.py:162
  823.1 16.7 convolution_convert_fusion.4
  839.8 16.9 convolution_convert_fusion.5
  856.7 28.6 %fusion.157 = f32[1120,2048]{1,0:T(8,128)} fusion(bf16[1120,4096]{1,0:T(8,128)(2,1)} %get-tuple-element.141, bf16[2048,4096]{1,0:T(8,128)(2,1)S(1)} %bitcast.222), kind=kOutput, calls=%fused_computation.502 | convolution fusion | flops 18790481920 | bytes 35127296 | tf_op jit(solution)/shard_map/dot_general | solution.py:166
  885.3 17.0 convolution_convert_fusion.2
  902.2 25.6 %convolution_add_fusion = f32[1120,2048]{1,0:T(8,128)S(1)} fusion(f32[1120,2048]{1,0:T(8,128)} %fusion.157, bf16[1120,4096]{1,0:T(8,128)(2,1)} %get-tuple-element.140, bf16[2048,4096]{1,0:T(8,128)(2,1)} %constant_dynamic-update-slice_fusion.39), kind=kOutput, calls=%fused_computation.20 | convolution fusion | flops 18792775680 | bytes 44302336 | tf_op jit(solution)/shard_map/dot_general | solution.py:166
  929.0 22.9 %fusion.154 = f32[1120,2048]{1,0:T(8,128)S(1)} fusion(bf16[1120,4096]{1,0:T(8,128)(2,1)} %get-tuple-element.142, bf16[2048,4096]{0,1:T(8,128)(2,1)} %constant_dynamic-update-slice_fusion.59), kind=kOutput, calls=%fused_computation.499 | convolution fusion | flops 18790481920 | bytes 35127296 | tf_op jit(solution)/shard_map/dot_general | solution.py:166
  952.0 19.7 %convolution_convert_fusion.3 = bf16[1024,4096]{1,0:T(8,128)(2,1)} fusion(bf16[1120,4096]{1,0:T(8,128)(2,1)} %get-tuple-element.141, bf16[1120,2048]{1,0:T(8,128)(2,1)} %pad_maximum_fusion.5), kind=kOutput, calls=%fused_computation.35 | convolution fusion | flops 9399435264 | bytes 19857408 | tf_op jit(solution)/shard_map/dot_general | solution.py:170
  975.8 17.2 convolution_convert_fusion
  1005.0 20.8 %collective-permute-done.79 = bf16[280,2048]{1,0:T(8,128)(2,1)} collective-permute-done((bf16[280,2048]{1,0:T(8,128)(2,1)}, bf16[280,2048]{1,0:T(8,128)(2,1)}, u32[]{:S(2)}, u32[]{:S(2)}) %collective-permute-start.79) | collective-permute-done | bytes 1146912 | tf_op jit(solution)/shard_map/ppermute | solution.py:27
  1030.0 16.8 convolution_convert_fusion.1
  1056.7 18.3 collective-permute-done.80
  1323.6 15.3 collective-permute-done.118
  1341.2 42.5 %collective-permute-done.125 = bf16[128,4096]{1,0:T(8,128)(2,1)S(1)} collective-permute-done((bf16[128,4096]{1,0:T(8,128)(2,1)S(1)}, bf16[128,4096]{1,0:T(8,128)(2,1)S(1)}, u32[]{:S(2)}, u32[]{:S(2)}) %collective-permute-start.125) | collective-permute-done | bytes 1048608 | tf_op jit(solution)/shard_map/ppermute | solution.py:17
  1387.0 19.2 %collective-permute-done.132 = bf16[128,4096]{1,0:T(8,128)(2,1)S(1)} collective-permute-done((bf16[128,4096]{1,0:T(8,128)(2,1)S(1)}, bf16[128,4096]{1,0:T(8,128)(2,1)S(1)}, u32[]{:S(2)}, u32[]{:S(2)}) %collective-permute-start.132) | collective-permute-done | bytes 1048608 | tf_op jit(solution)/shard_map/ppermute | solution.py:17
  1414.5 17.9 collective-permute-done.119
  1461.3 31.1 %collective-permute-done.110 = bf16[128,3072]{1,0:T(8,128)(2,1)S(1)} collective-permute-done((bf16[128,3072]{1,0:T(8,128)(2,1)}, bf16[128,3072]{1,0:T(8,128)(2,1)S(1)}, u32[]{:S(2)}, u32[]{:S(2)}) %collective-permute-start.110) | collective-permute-done | bytes 786464 | tf_op jit(solution)/shard_map/ppermute | solution.py:17
  1540.1 39.4 %collective-permute-done.120 = bf16[128,4096]{1,0:T(8,128)(2,1)S(1)} collective-permute-done((bf16[128,4096]{1,0:T(8,128)(2,1)S(1)}, bf16[128,4096]{1,0:T(8,128)(2,1)S(1)}, u32[]{:S(2)}, u32[]{:S(2)}) %collective-permute-start.120) | collective-permute-done | bytes 1048608 | tf_op jit(solution)/shard_map/ppermute | solution.py:17
  1589.5 35.0 %collective-permute-done.127 = bf16[128,4096]{1,0:T(8,128)(2,1)} collective-permute-done((bf16[128,4096]{1,0:T(8,128)(2,1)S(1)}, bf16[128,4096]{1,0:T(8,128)(2,1)}, u32[]{:S(2)}, u32[]{:S(2)}) %collective-permute-start.127) | collective-permute-done | bytes 1048608 | tf_op jit(solution)/shard_map/ppermute | solution.py:17
  1640.1 26.6 %collective-permute-done.134 = bf16[128,4096]{1,0:T(8,128)(2,1)S(1)} collective-permute-done((bf16[128,4096]{1,0:T(8,128)(2,1)S(1)}, bf16[128,4096]{1,0:T(8,128)(2,1)S(1)}, u32[]{:S(2)}, u32[]{:S(2)}) %collective-permute-start.134) | collective-permute-done | bytes 1048608 | tf_op jit(solution)/shard_map/ppermute | solution.py:17
  1672.3 19.2 %collective-permute-done.98 = bf16[192,2560]{1,0:T(8,128)(2,1)S(1)} collective-permute-done((bf16[192,2560]{1,0:T(8,128)(2,1)S(1)}, bf16[192,2560]{1,0:T(8,128)(2,1)S(1)}, u32[]{:S(2)}, u32[]{:S(2)}) %collective-permute-start.98) | collective-permute-done | bytes 983072 | tf_op jit(solution)/shard_map/ppermute | solution.py:17
  1695.2 18.7 %collective-permute-done.121 = bf16[128,4096]{1,0:T(8,128)(2,1)S(1)} collective-permute-done((bf16[128,4096]{1,0:T(8,128)(2,1)S(1)}, bf16[128,4096]{1,0:T(8,128)(2,1)S(1)}, u32[]{:S(2)}, u32[]{:S(2)}) %collective-permute-start.121) | collective-permute-done | bytes 1048608 | tf_op jit(solution)/shard_map/ppermute | solution.py:17
  1718.8 35.6 %collective-permute-done.97 = bf16[192,2560]{1,0:T(8,128)(2,1)S(1)} collective-permute-done((bf16[192,2560]{1,0:T(8,128)(2,1)S(1)}, bf16[192,2560]{1,0:T(8,128)(2,1)S(1)}, u32[]{:S(2)}, u32[]{:S(2)}) %collective-permute-start.97) | collective-permute-done | bytes 983072 | tf_op jit(solution)/shard_map/ppermute | solution.py:17
  (925 shorter events, 1016.3 us)
Async XLA Ops:
  0.7 173.4 %collective-permute-start.48 = (bf16[256,4096]{0,1:T(8,128)(2,1)}, bf16[256,4096]{0,1:T(8,128)(2,1)}, u32[]{:S(2)}, u32[]{:S(2)}) collective-permute-start(bf16[256,4096]{0,1:T(8,128)(2,1)} %bitcast.214), channel_id=1, source_target_pairs={{0,8},{4,12},{8,0},{12,4},{16,24},{20,28},{24,16},{28,20},{1,9},{5... | collective-permute-start | bytes 6291464 | tf_op jit(solution)/shard_map/ppermute | solution.py:17
  3.7 174.9 %collective-permute-start.49 = (bf16[256,4096]{0,1:T(8,128)(2,1)}, bf16[256,4096]{0,1:T(8,128)(2,1)}, u32[]{:S(2)}, u32[]{:S(2)}) collective-permute-start(bf16[256,4096]{0,1:T(8,128)(2,1)} %bitcast.215), channel_id=1, source_target_pairs={{0,16},{4,20},{8,24},{12,28},{16,0},{20,4},{24,8},{28,12},{1,17},{... | collective-permute-start | bytes 6291464 | tf_op jit(solution)/shard_map/ppermute | solution.py:17
  91.4 90.3 %collective-permute-start.39 = (bf16[256,4096]{1,0:T(8,128)(2,1)}, bf16[256,4096]{1,0:T(8,128)(2,1)S(1)}, u32[]{:S(2)}, u32[]{:S(2)}) collective-permute-start(bf16[256,4096]{1,0:T(8,128)(2,1)} %param.40), channel_id=1, source_target_pairs={{0,8},{4,12},{8,0},{12,4},{16,24},{20,28},{24,16},{28,20},{1,9},{5... | collective-permute-start | bytes 6291464 | tf_op jit(solution)/shard_map/ppermute | solution.py:17
  92.6 75.3 %collective-permute-start.63 = (bf16[384,2048]{1,0:T(8,128)(2,1)}, bf16[384,2048]{1,0:T(8,128)(2,1)S(1)}, u32[]{:S(2)}, u32[]{:S(2)}) collective-permute-start(bf16[384,2048]{1,0:T(8,128)(2,1)} %pad_maximum_fusion.10), channel_id=1, source_target_pairs={{0,8},{4,12},{8,0},{12,4},{16,24},{20,28},{24,16},{28,20},{1,9},{5... | collective-permute-start | bytes 4718600 | tf_op jit(solution)/shard_map/ppermute | solution.py:17
  104.7 66.3 %collective-permute-start.64 = (bf16[384,2048]{1,0:T(8,128)(2,1)}, bf16[384,2048]{1,0:T(8,128)(2,1)S(1)}, u32[]{:S(2)}, u32[]{:S(2)}) collective-permute-start(bf16[384,2048]{1,0:T(8,128)(2,1)} %pad_maximum_fusion.10), channel_id=1, source_target_pairs={{0,16},{4,20},{8,24},{12,28},{16,0},{20,4},{24,8},{28,12},{1,17},{... | collective-permute-start | bytes 4718600 | tf_op jit(solution)/shard_map/ppermute | solution.py:17
  174.1 87.6 %collective-permute-start.31 = (bf16[256,4096]{1,0:T(8,128)(2,1)}, bf16[256,4096]{1,0:T(8,128)(2,1)}, u32[]{:S(2)}, u32[]{:S(2)}) collective-permute-start(bf16[256,4096]{1,0:T(8,128)(2,1)} %param.39), channel_id=1, source_target_pairs={{0,16},{4,20},{8,24},{12,28},{16,0},{20,4},{24,8},{28,12},{1,17},{... | collective-permute-start | bytes 6291464 | tf_op jit(solution)/shard_map/ppermute | solution.py:17
  178.6 103.4 %collective-permute-start.67 = (bf16[384,2048]{1,0:T(8,128)(2,1)}, bf16[384,2048]{1,0:T(8,128)(2,1)}, u32[]{:S(2)}, u32[]{:S(2)}) collective-permute-start(bf16[384,2048]{1,0:T(8,128)(2,1)} %pad_maximum_fusion.10), channel_id=1, source_target_pairs={{0,4},{4,0},{8,12},{12,8},{16,20},{20,16},{24,28},{28,24},{1,5},{5... | collective-permute-start | bytes 4718600 | tf_op jit(solution)/shard_map/ppermute | solution.py:17
  181.7 103.2 %collective-permute-start.18 = (bf16[256,3072]{1,0:T(8,128)(2,1)}, bf16[256,3072]{1,0:T(8,128)(2,1)S(1)}, u32[]{:S(2)}, u32[]{:S(2)}) collective-permute-start(bf16[256,3072]{1,0:T(8,128)(2,1)} %get-tuple-element.135), channel_id=1, source_target_pairs={{0,8},{4,12},{8,0},{12,4},{16,24},{20,28},{24,16},{28,20},{1,9},{5... | collective-permute-start | bytes 4718600 | tf_op jit(solution)/shard_map/ppermute | solution.py:17
  216.7 61.9 %collective-permute-start.65 = (bf16[192,2048]{1,0:T(8,128)(2,1)}, bf16[192,2048]{1,0:T(8,128)(2,1)}, u32[]{:S(2)}, u32[]{:S(2)}) collective-permute-start(bf16[192,2048]{1,0:T(8,128)(2,1)} %slice.831), channel_id=1, source_target_pairs={{0,16},{4,20},{8,24},{12,28},{16,0},{20,4},{24,8},{28,12},{1,17},{... | collective-permute-start | bytes 2359304 | tf_op jit(solution)/shard_map/ppermute | solution.py:17
  278.6 78.8 %collective-permute-start.52 = (bf16[256,4096]{0,1:T(8,128)(2,1)}, bf16[256,4096]{0,1:T(8,128)(2,1)}, u32[]{:S(2)}, u32[]{:S(2)}) collective-permute-start(bf16[256,4096]{0,1:T(8,128)(2,1)} %bitcast.216), channel_id=1, source_target_pairs={{0,4},{4,0},{8,12},{12,8},{16,20},{20,16},{24,28},{28,24},{1,5},{5... | collective-permute-start | bytes 6291464 | tf_op jit(solution)/shard_map/ppermute | solution.py:17
  282.0 73.5 %collective-permute-start.75 = (bf16[280,2048]{1,0:T(8,128)(2,1)S(1)}, bf16[280,2048]{1,0:T(8,128)(2,1)S(1)}, u32[]{:S(2)}, u32[]{:S(2)}) collective-permute-start(bf16[280,2048]{1,0:T(8,128)(2,1)S(1)} %copy-done.31), channel_id=1, source_target_pairs={{0,1},{1,2},{2,3},{3,0},{4,5},{5,6},{6,7},{7,4},{8,9},{9,10},{10,1... | collective-permute-start | bytes 3440648 | tf_op jit(solution)/shard_map/ppermute | solution.py:22
  387.6 69.5 %collective-permute-start.22 = (bf16[256,3072]{1,0:T(8,128)(2,1)}, bf16[256,3072]{1,0:T(8,128)(2,1)}, u32[]{:S(2)}, u32[]{:S(2)}) collective-permute-start(bf16[256,3072]{1,0:T(8,128)(2,1)} %get-tuple-element.135), channel_id=1, source_target_pairs={{0,4},{4,0},{8,12},{12,8},{16,20},{20,16},{24,28},{28,24},{1,5},{5... | collective-permute-start | bytes 4718600 | tf_op jit(solution)/shard_map/ppermute | solution.py:17
  393.6 66.6 %collective-permute-start.53 = (bf16[256,4096]{0,1:T(8,128)(2,1)}, bf16[256,4096]{0,1:T(8,128)(2,1)}, u32[]{:S(2)}, u32[]{:S(2)}) collective-permute-start(bf16[256,4096]{0,1:T(8,128)(2,1)} %collective-permute-done.48), channel_id=1, source_target_pairs={{0,4},{4,0},{8,12},{12,8},{16,20},{20,16},{24,28},{28,24},{1,5},{5... | collective-permute-start | bytes 6291464 | tf_op jit(solution)/shard_map/ppermute | solution.py:17
  453.2 85.5 %collective-permute-start.7 = (bf16[384,2560]{1,0:T(8,128)(2,1)}, bf16[384,2560]{1,0:T(8,128)(2,1)}, u32[]{:S(2)}, u32[]{:S(2)}) collective-permute-start(bf16[384,2560]{1,0:T(8,128)(2,1)} %pad_maximum_fusion.9), channel_id=1, source_target_pairs={{0,4},{4,0},{8,12},{12,8},{16,20},{20,16},{24,28},{28,24},{1,5},{5... | collective-permute-start | bytes 5898248 | tf_op jit(solution)/shard_map/ppermute | solution.py:17
  672.8 378.9 %collective-permute-start.137 = (bf16[1536,2048]{1,0:T(8,128)(2,1)}, bf16[1536,2048]{1,0:T(8,128)(2,1)}, u32[]{:S(2)}, u32[]{:S(2)}) collective-permute-start(bf16[1536,2048]{1,0:T(8,128)(2,1)} %bitcast.42), channel_id=1, source_target_pairs={{0,4},{4,0},{8,12},{12,8},{16,20},{20,16},{24,28},{28,24},{1,5},{5... | collective-permute-start | bytes 18874376 | tf_op jit(solution)/shard_map/ppermute | solution.py:17
  1046.8 262.9 %collective-permute-start.116 = (bf16[1024,4096]{1,0:T(8,128)(2,1)}, bf16[1024,4096]{1,0:T(8,128)(2,1)}, u32[]{:S(2)}, u32[]{:S(2)}) collective-permute-start(bf16[1024,4096]{1,0:T(8,128)(2,1)} %convolution_convert_fusion.4), channel_id=1, source_target_pairs={{0,4},{4,0},{8,12},{12,8},{16,20},{20,16},{24,28},{28,24},{1,5},{5... | collective-permute-start | bytes 25165832 | tf_op jit(solution)/shard_map/ppermute | solution.py:17
  1046.8 266.4 %collective-permute-start.123 = (bf16[1024,4096]{1,0:T(8,128)(2,1)}, bf16[1024,4096]{1,0:T(8,128)(2,1)}, u32[]{:S(2)}, u32[]{:S(2)}) collective-permute-start(bf16[1024,4096]{1,0:T(8,128)(2,1)} %convolution_convert_fusion.2), channel_id=1, source_target_pairs={{0,4},{4,0},{8,12},{12,8},{16,20},{20,16},{24,28},{28,24},{1,5},{5... | collective-permute-start | bytes 25165832 | tf_op jit(solution)/shard_map/ppermute | solution.py:17
  1050.4 268.6 %collective-permute-start.130 = (bf16[1024,4096]{1,0:T(8,128)(2,1)}, bf16[1024,4096]{1,0:T(8,128)(2,1)}, u32[]{:S(2)}, u32[]{:S(2)}) collective-permute-start(bf16[1024,4096]{1,0:T(8,128)(2,1)} %convolution_convert_fusion), channel_id=1, source_target_pairs={{0,4},{4,0},{8,12},{12,8},{16,20},{20,16},{24,28},{28,24},{1,5},{5... | collective-permute-start | bytes 25165832 | tf_op jit(solution)/shard_map/ppermute | solution.py:17
  1075.1 96.9 %collective-permute-start.141 = (bf16[192,2048]{1,0:T(8,128)(2,1)}, bf16[192,2048]{1,0:T(8,128)(2,1)}, u32[]{:S(2)}, u32[]{:S(2)}) collective-permute-start(bf16[192,2048]{1,0:T(8,128)(2,1)} %add_convert_fusion.27), channel_id=1, source_target_pairs={{0,8},{4,12},{8,0},{12,4},{16,24},{20,28},{24,16},{28,20},{1,9},{5... | collective-permute-start | bytes 2359304 | tf_op jit(solution)/shard_map/ppermute | solution.py:17
  1175.9 71.3 %collective-permute-start.143 = (bf16[192,2048]{1,0:T(8,128)(2,1)}, bf16[192,2048]{1,0:T(8,128)(2,1)}, u32[]{:S(2)}, u32[]{:S(2)}) collective-permute-start(bf16[192,2048]{1,0:T(8,128)(2,1)} %get-tuple-element.167), channel_id=1, source_target_pairs={{0,8},{4,12},{8,0},{12,4},{16,24},{20,28},{24,16},{28,20},{1,9},{5... | collective-permute-start | bytes 2359304 | tf_op jit(solution)/shard_map/ppermute | solution.py:17
  1298.5 111.6 %collective-permute-start.106 = (bf16[1024,3072]{1,0:T(8,128)(2,1)}, bf16[1024,3072]{1,0:T(8,128)(2,1)}, u32[]{:S(2)}, u32[]{:S(2)}) collective-permute-start(bf16[1024,3072]{1,0:T(8,128)(2,1)} %pad_maximum_fusion.2), channel_id=1, source_target_pairs={{0,4},{4,0},{8,12},{12,8},{16,20},{20,16},{24,28},{28,24},{1,5},{5... | collective-permute-start | bytes 18874376 | tf_op jit(solution)/shard_map/ppermute | solution.py:17
  1304.6 331.4 %collective-permute-start.96 = (bf16[1536,2560]{1,0:T(8,128)(2,1)}, bf16[1536,2560]{1,0:T(8,128)(2,1)}, u32[]{:S(2)}, u32[]{:S(2)}) collective-permute-start(bf16[1536,2560]{1,0:T(8,128)(2,1)} %bitcast.203), channel_id=1, source_target_pairs={{0,4},{4,0},{8,12},{12,8},{16,20},{20,16},{24,28},{28,24},{1,5},{5... | collective-permute-start | bytes 23592968 | tf_op jit(solution)/shard_map/ppermute | solution.py:17
  1313.3 100.4 %collective-permute-start.117 = (bf16[128,4096]{1,0:T(8,128)(2,1)S(1)}, bf16[128,4096]{1,0:T(8,128)(2,1)S(1)}, u32[]{:S(2)}, u32[]{:S(2)}) collective-permute-start(bf16[128,4096]{1,0:T(8,128)(2,1)S(1)} %get-tuple-element.156), channel_id=1, source_target_pairs={{0,16},{4,20},{8,24},{12,28},{16,0},{20,4},{24,8},{28,12},{1,17},{... | collective-permute-start | bytes 3145736 | tf_op jit(solution)/shard_map/ppermute | solution.py:17
  1319.0 64.8 %collective-permute-start.125 = (bf16[128,4096]{1,0:T(8,128)(2,1)S(1)}, bf16[128,4096]{1,0:T(8,128)(2,1)S(1)}, u32[]{:S(2)}, u32[]{:S(2)}) collective-permute-start(bf16[128,4096]{1,0:T(8,128)(2,1)S(1)} %get-tuple-element.152), channel_id=1, source_target_pairs={{0,16},{4,20},{8,24},{12,28},{16,0},{20,4},{24,8},{28,12},{1,17},{... | collective-permute-start | bytes 3145736 | tf_op jit(solution)/shard_map/ppermute | solution.py:17
  1338.8 67.4 %collective-permute-start.132 = (bf16[128,4096]{1,0:T(8,128)(2,1)S(1)}, bf16[128,4096]{1,0:T(8,128)(2,1)S(1)}, u32[]{:S(2)}, u32[]{:S(2)}) collective-permute-start(bf16[128,4096]{1,0:T(8,128)(2,1)S(1)} %get-tuple-element.147), channel_id=1, source_target_pairs={{0,16},{4,20},{8,24},{12,28},{16,0},{20,4},{24,8},{28,12},{1,17},{... | collective-permute-start | bytes 3145736 | tf_op jit(solution)/shard_map/ppermute | solution.py:17
  1410.1 88.5 %collective-permute-start.131 = (bf16[128,4096]{1,0:T(8,128)(2,1)}, bf16[128,4096]{1,0:T(8,128)(2,1)S(1)}, u32[]{:S(2)}, u32[]{:S(2)}) collective-permute-start(bf16[128,4096]{1,0:T(8,128)(2,1)} %get-tuple-element.146), channel_id=1, source_target_pairs={{0,16},{4,20},{8,24},{12,28},{16,0},{20,4},{24,8},{28,12},{1,17},{... | collective-permute-start | bytes 3145736 | tf_op jit(solution)/shard_map/ppermute | solution.py:17
  1432.4 67.1 %collective-permute-start.133 = (bf16[128,4096]{1,0:T(8,128)(2,1)}, bf16[128,4096]{1,0:T(8,128)(2,1)S(1)}, u32[]{:S(2)}, u32[]{:S(2)}) collective-permute-start(bf16[128,4096]{1,0:T(8,128)(2,1)} %add_convert_fusion.4), channel_id=1, source_target_pairs={{0,8},{4,12},{8,0},{12,4},{16,24},{20,28},{24,16},{28,20},{1,9},{5... | collective-permute-start | bytes 3145736 | tf_op jit(solution)/shard_map/ppermute | solution.py:17
  1517.8 175.7 %collective-permute-start.122 = (bf16[128,4096]{1,0:T(8,128)(2,1)S(1)}, bf16[128,4096]{1,0:T(8,128)(2,1)}, u32[]{:S(2)}, u32[]{:S(2)}) collective-permute-start(bf16[128,4096]{1,0:T(8,128)(2,1)S(1)} %get-tuple-element.154), channel_id=1, source_target_pairs={{0,8},{4,12},{8,0},{12,4},{16,24},{20,28},{24,16},{28,20},{1,9},{5... | collective-permute-start | bytes 3145736 | tf_op jit(solution)/shard_map/ppermute | solution.py:17
  1534.6 253.1 %collective-permute-start.129 = (bf16[128,4096]{1,0:T(8,128)(2,1)S(1)}, bf16[128,4096]{1,0:T(8,128)(2,1)}, u32[]{:S(2)}, u32[]{:S(2)}) collective-permute-start(bf16[128,4096]{1,0:T(8,128)(2,1)S(1)} %get-tuple-element.149), channel_id=1, source_target_pairs={{0,8},{4,12},{8,0},{12,4},{16,24},{20,28},{24,16},{28,20},{1,9},{5... | collective-permute-start | bytes 3145736 | tf_op jit(solution)/shard_map/ppermute | solution.py:17
  1535.8 88.7 %collective-permute-start.127 = (bf16[128,4096]{1,0:T(8,128)(2,1)S(1)}, bf16[128,4096]{1,0:T(8,128)(2,1)}, u32[]{:S(2)}, u32[]{:S(2)}) collective-permute-start(bf16[128,4096]{1,0:T(8,128)(2,1)S(1)} %get-tuple-element.150), channel_id=1, source_target_pairs={{0,8},{4,12},{8,0},{12,4},{16,24},{20,28},{24,16},{28,20},{1,9},{5... | collective-permute-start | bytes 3145736 | tf_op jit(solution)/shard_map/ppermute | solution.py:17
  1588.2 171.9 %collective-permute-start.136 = (bf16[128,4096]{1,0:T(8,128)(2,1)S(1)}, bf16[128,4096]{1,0:T(8,128)(2,1)S(1)}, u32[]{:S(2)}, u32[]{:S(2)}) collective-permute-start(bf16[128,4096]{1,0:T(8,128)(2,1)S(1)} %get-tuple-element.144), channel_id=1, source_target_pairs={{0,8},{4,12},{8,0},{12,4},{16,24},{20,28},{24,16},{28,20},{1,9},{5... | collective-permute-start | bytes 3145736 | tf_op jit(solution)/shard_map/ppermute | solution.py:17
  1691.4 68.7 %collective-permute-start.135 = (bf16[128,4096]{1,0:T(8,128)(2,1)S(1)}, bf16[128,4096]{1,0:T(8,128)(2,1)S(1)}, u32[]{:S(2)}, u32[]{:S(2)}) collective-permute-start(bf16[128,4096]{1,0:T(8,128)(2,1)S(1)} %add_convert_fusion.2), channel_id=1, source_target_pairs={{0,16},{4,20},{8,24},{12,28},{16,0},{20,4},{24,8},{28,12},{1,17},{... | collective-permute-start | bytes 3145736 | tf_op jit(solution)/shard_map/ppermute | solution.py:17
  (259 other events, 5899.9 us)

commit v2 on v1

v2 whole, which is shorter than its diff:
```python
import functools

import jax
import jax.numpy as jnp
from jax import lax
from jax.experimental import pallas as pl
from jax.experimental.pallas import tpu as pltpu
from jax.sharding import PartitionSpec as P

NORM_EPS = 1e-06
ROPE_BASE = 10000.0
MASKED = -1e30
F32 = jnp.float32
BF16 = jnp.bfloat16


class Links:
    def __init__(self, window=2):
        self.window = window
        self.done = {}

    def send(self, value, axis, pairs, link):
        sent = self.done.setdefault(link, [])
        if len(sent) >= self.window:
            value, _ = lax.optimization_barrier((value, sent[-self.window]))
        result = lax.ppermute(value, axis, pairs)
        sent.append(result)
        return result


LINKS = Links()


def hop(value, bit):
    size = lax.axis_size("dp")
    pairs = [(d, d ^ bit) for d in range(size)]
    if bit == 1:
        return lax.ppermute(value, "dp", pairs)
    return LINKS.send(value, "dp", pairs, bit)


LOOSE = None


def ring(value, step, link="mp"):
    size = lax.axis_size("mp")
    pairs = [(d, (d + step) % size) for d in range(size)]
    if link is LOOSE:
        return lax.ppermute(value, "mp", pairs)
    return LINKS.send(value, "mp", pairs, link)


def ring_gather(value, link="mp"):
    out = [value]
    for _ in range(lax.axis_size("mp") - 1):
        out.append(ring(out[-1], 1, link))
    return out


def ring_scatter(parts, steps=None):
    total = parts[-1].astype(BF16)
    for part in parts[-2::-1]:
        moved = ring(total.astype(BF16), -1, LOOSE)
        if steps is not None:
            steps.append(moved)
        total = moved.astype(F32) + part.astype(F32)
    return total


def chip_order(size):
    return sorted(range(1, size), key=lambda c: (bin(c).count("1"), c))


def rel_blocks():
    size = lax.axis_size("dp")
    place = jnp.arange(size, dtype=jnp.int32)
    half = size // 2
    rel = (place % half) * 2 + place // half
    return jnp.bitwise_xor(rel, lax.axis_index("dp").astype(jnp.int32))


def dp_gather(shard):
    chips = lax.axis_size("dp") // 2
    half = shard.shape[0] // 2
    got = {0: [shard]}

    def top(c):
        return got[c][0] if len(got[c]) == 2 else got[c][0][:half]

    def bottom(c):
        return got[c][1] if len(got[c]) == 2 else got[c][0][half:]

    for c in chip_order(chips):
        high, low = 1 << (c.bit_length() - 1), c & -c
        if high == low:
            got[c] = [hop(shard, 2 * high)]
        else:
            got[c] = [hop(top(c ^ high), 2 * high), hop(bottom(c ^ low), 2 * low)]
    own = [piece for c in range(chips) for piece in got[c]]
    return own + [hop(piece, 1) for piece in own]


def scatter_rows(own, other, layout):
    size = lax.axis_size("dp")
    groups = lax.axis_size("mp")
    chips = size // 2
    rows = own.shape[0] // chips
    other = hop(other, 1)

    def block(c):
        cut = slice(c * rows, (c + 1) * rows)
        return own[cut].astype(F32) + other[cut].astype(F32)

    total = block(0)
    for c in range(1, chips):
        pairs = [(d, d ^ (2 * c)) for d in range(size)]
        total = total + lax.ppermute(block(c).astype(BF16), "dp", pairs).astype(F32)
    parts = []
    for r in range(groups):
        which = (lax.axis_index("mp") - r) % groups
        cuts, start = [], 0
        for part in layout:
            cuts.append(lax.dynamic_slice_in_dim(total, start + which * part, part, 0))
            start += groups * part
        parts.append(jnp.concatenate(cuts, axis=0))
    return ring_scatter(parts)


def _permute_blocks(inverse, order, *refs):
    half = len(refs) // 2
    for src, dst in zip(refs[:half], refs[half:]):
        block = src.shape[1] // order.shape[0]
        for g in range(order.shape[0]):
            here = slice(g * block, (g + 1) * block)
            there = pl.ds(pl.multiple_of(order[g] * block, block), block)
            if inverse:
                dst[:, there] = src[:, here]
            else:
                dst[:, here] = src[:, there]


def permute_columns(arrays, order, inverse=False):
    count = order.shape[0]
    if any(values.shape[1] // count % 128 for values in arrays):
        hit = order[:, None] == jnp.arange(count, dtype=order.dtype)[None, :]
        places = jnp.arange(count, dtype=order.dtype)
        back = jnp.sum(jnp.where(hit, places[:, None], 0), axis=0) if inverse else order
        outs = []
        for values in arrays:
            split = values.reshape(values.shape[0], count, -1)
            cuts = [lax.dynamic_slice_in_dim(split, back[g], 1, 1) for g in range(count)]
            outs.append(jnp.concatenate(cuts, axis=1).reshape(values.shape))
        return outs
    return pl.pallas_call(
        functools.partial(_permute_blocks, inverse),
        in_specs=[pl.BlockSpec(memory_space=pltpu.SMEM)]
        + [pl.BlockSpec(memory_space=pltpu.VMEM)] * len(arrays),
        out_specs=[pl.BlockSpec(memory_space=pltpu.VMEM)] * len(arrays),
        out_shape=[jax.ShapeDtypeStruct(values.shape, values.dtype) for values in arrays],
        compiler_params=pltpu.CompilerParams(vmem_limit_bytes=32 * 2**20),
    )(order, *arrays)


def _spread(count, order, pre, act, joint):
    rows = pre.shape[0]
    narrow = [value.shape[1] // count for value in (pre, act)]
    joint[...] = jnp.zeros_like(joint)
    for g in range(count):
        start = g * sum(narrow)
        there = pl.ds(pl.multiple_of(order[g] * narrow[0], narrow[0]), narrow[0])
        joint[:rows, start : start + narrow[0]] = pre[:, there]
        there = pl.ds(pl.multiple_of(order[g] * narrow[1], narrow[1]), narrow[1])
        joint[rows:, start + narrow[0] : start + sum(narrow)] = act[:, there]


def _unspread(count, order, joint, pre, act):
    rows = pre.shape[0]
    narrow = [value.shape[1] // count for value in (pre, act)]
    for g in range(count):
        start = g * sum(narrow)
        there = pl.ds(pl.multiple_of(order[g] * narrow[0], narrow[0]), narrow[0])
        pre[:, there] = joint[:rows, start : start + narrow[0]]
        there = pl.ds(pl.multiple_of(order[g] * narrow[1], narrow[1]), narrow[1])
        act[:, there] = joint[rows:, start + narrow[0] : start + sum(narrow)]


def block_call(body, order, arrays, shapes):
    return pl.pallas_call(
        functools.partial(body, order.shape[0]),
        in_specs=[pl.BlockSpec(memory_space=pltpu.SMEM)]
        + [pl.BlockSpec(memory_space=pltpu.VMEM)] * len(arrays),
        out_specs=[pl.BlockSpec(memory_space=pltpu.VMEM)] * len(shapes),
        out_shape=shapes,
        compiler_params=pltpu.CompilerParams(vmem_limit_bytes=32 * 2**20),
    )(order, *arrays)


def spread(pre, act, order):
    count = order.shape[0]
    rows, lines = pre.shape[0], act.shape[0]
    wide, thin = pre.shape[1] // count, act.shape[1] // count
    if wide % 128 or thin % 128:
        upper, lower = permute_columns([pre, act], order)
        upper = jnp.pad(upper.reshape(rows, count, wide), ((0, lines), (0, 0), (0, thin)))
        lower = jnp.pad(lower.reshape(lines, count, thin), ((rows, 0), (0, 0), (wide, 0)))
        return (upper + lower).reshape(rows + lines, -1)
    shape = jax.ShapeDtypeStruct((rows + lines, pre.shape[1] + act.shape[1]), pre.dtype)
    return block_call(_spread, order, [pre, act], [shape])[0]


def unspread(joint, rows, wide, thin, order):
    count = order.shape[0]
    lines = joint.shape[0] - rows
    if wide // count % 128 or thin // count % 128:
        blocks = joint.reshape(joint.shape[0], count, -1)
        upper = blocks[:rows, :, : wide // count].reshape(rows, wide)
        lower = blocks[rows:, :, wide // count :].reshape(lines, thin)
        return permute_columns([upper, lower], order, True)
    shapes = [
        jax.ShapeDtypeStruct((rows, wide), joint.dtype),
        jax.ShapeDtypeStruct((lines, thin), joint.dtype),
    ]
    return block_call(_unspread, order, [joint], shapes)


def inverse_rms(values):
    return lax.rsqrt(jnp.mean(values * values, axis=-1, keepdims=True) + NORM_EPS)


def rms_norm(values, gain_vec):
    return values * inverse_rms(values) * gain_vec


def rms_back(values, gain_vec, grads):
    inverse = inverse_rms(values)
    unit = values * inverse
    scaled = gain_vec * grads
    mean = jnp.mean(unit * scaled, axis=-1, keepdims=True)
    return inverse * (scaled - unit * mean), jnp.sum(grads * unit, axis=0)


def rope_tables(positions, head_dim):
    half_dim = head_dim // 2
    inverse = ROPE_BASE ** (-2.0 * jnp.arange(half_dim).astype(F32) / head_dim)
    angles = positions.astype(F32)[:, None] * inverse[None, :]
    return (jnp.cos(angles), jnp.sin(angles))


def rotate(values, cosine_tab, sine_tab):
    half_dim = values.shape[-1] // 2
    lower_half = values[..., :half_dim]
    upper_half = values[..., half_dim:]
    return jnp.concatenate(
        [
            lower_half * cosine_tab - upper_half * sine_tab,
            upper_half * cosine_tab + lower_half * sine_tab,
        ],
        axis=-1,
    )


def mm(left, right):
    return lax.dot_general(left, right, (((1,), (0,)), ((), ())), preferred_element_type=F32)


def mm_nt(left, right):
    return lax.dot_general(left, right, (((1,), (1,)), ((), ())), preferred_element_type=F32)


def mm_tn(left, right):
    return lax.dot_general(left, right, (((0,), (0,)), ((), ())), preferred_element_type=F32)


def geglu(gate_val, up_val, live_mask):
    return jax.nn.gelu(gate_val, approximate=True) * up_val * live_mask


def feed_forward(rows, cot_rows, gate, up, down_t, live_mask):
    gate_val = mm(rows, gate)
    up_val = mm(rows, up)
    hidden_back = mm(cot_rows, down_t)
    hidden, pull = jax.vjp(lambda g, u: geglu(g, u, live_mask), gate_val, up_val)
    gate_back, up_back = pull(hidden_back)
    return hidden.astype(BF16), gate_back.astype(BF16), up_back.astype(BF16)


def _feed_forward_tile(groups, *refs):
    pieces, (back_ref, gate_ref, up_ref) = refs[:groups], refs[groups : groups + 3]
    hidden_ref, gate_back_ref, up_back_ref, rows_ref = refs[groups + 3 :]
    count = pieces[0].shape[0]
    root, cube = 0.7978845608028654, 0.044715

    @pl.when(pl.program_id(0) == 0)
    def _():
        for r in range(groups):
            rows_ref[r * count : (r + 1) * count, :] = pieces[r][...]

    for r in range(groups):
        cut = slice(r * count, (r + 1) * count)
        rows = pieces[r][...]
        gate_val = jnp.dot(rows, gate_ref[...], preferred_element_type=F32)
        up_val = jnp.dot(rows, up_ref[...], preferred_element_type=F32)
        back = back_ref[cut, :].astype(F32)
        square = gate_val * gate_val
        bend = jnp.tanh(root * gate_val * (1.0 + cube * square))
        half_open = 0.5 * (1.0 + bend)
        active = gate_val * half_open
        inner = (0.5 * root) * gate_val * (1.0 - bend * bend) * (1.0 + 3.0 * cube * square)
        hidden_ref[cut, :] = (active * up_val).astype(BF16)
        gate_back_ref[cut, :] = (back * up_val * (half_open + inner)).astype(BF16)
        up_back_ref[cut, :] = (back * active).astype(BF16)


def feed_forward_kernel(pieces, hidden_back, gate, up, tile=512):
    groups = len(pieces)
    count, width = pieces[0].shape
    total = groups * count
    units = gate.shape[1]
    block = pl.BlockSpec((total, tile), lambda n: (0, n))
    weight = pl.BlockSpec((width, tile), lambda n: (0, n))
    fixed = pl.BlockSpec((count, width), lambda n: (0, 0), pipeline_mode=pl.Buffered(1))
    return pl.pallas_call(
        functools.partial(_feed_forward_tile, groups),
        grid=(units // tile,),
        in_specs=[fixed] * groups + [block, weight, weight],
        out_specs=[block] * 3 + [pl.BlockSpec((total, width), lambda n: (0, 0))],
        out_shape=[jax.ShapeDtypeStruct((total, units), BF16)] * 3
        + [jax.ShapeDtypeStruct((total, width), BF16)],
        compiler_params=pltpu.CompilerParams(vmem_limit_bytes=56 * 2**20),
        cost_estimate=pl.CostEstimate(
            flops=4 * total * width * units,
            bytes_accessed=4 * width * units + 8 * total * units + 4 * total * width,
            transcendentals=total * units,
        ),
    )(*pieces, hidden_back, gate, up)


def after(value, *first):
    return lax.optimization_barrier((value, *first))[0]


def shards(
    prefix_tokens,
    action_tokens,
    block_ids,
    live_dims,
    hidden_counts,
    pre_attn_gain,
    pre_mlp_gain,
    act_attn_gain,
    act_mlp_gain,
    pre_query,
    pre_keyval,
    pre_output,
    act_query,
    act_keyval,
    act_output,
    pre_gate,
    pre_up,
    pre_down,
    act_gate,
    act_up,
    act_down,
    action_head,
    prefix_cot,
    pred_cot,
):
    groups = lax.axis_size("mp")
    ways = lax.axis_size("dp")
    member = lax.axis_index("mp")
    items, pre_rows, width = prefix_tokens.shape
    act_rows, act_width = action_tokens.shape[1:]
    pre_len = pre_rows * groups
    head_dim = pre_keyval.shape[1] // 2
    query_width = pre_query.shape[1]
    heads = query_width // head_dim
    local_len = pre_rows + act_rows
    scale = head_dim ** (-0.5)
    order = rel_blocks()
    LINKS.done.clear()

    pre_part, act_part, out_part = pre_query.shape[0], act_query.shape[0], pre_output.shape[0]
    qkv_own = jnp.concatenate(
        [
            jnp.concatenate([pre_query, pre_keyval], axis=1),
            jnp.concatenate([act_query, act_keyval], axis=1),
        ],
        axis=0,
    )
    out_own = jnp.concatenate([pre_output, act_output], axis=1)

    def in_place(pieces):
        size = pieces[0].shape[0]
        twice = jnp.concatenate(pieces[::-1] * 2, axis=0)
        return lax.dynamic_slice_in_dim(twice, (groups - 1 - member) * size, groups * size, 0)

    qkv_ring = ring_gather(qkv_own)
    out_ring = ring_gather(out_own)
    qkv_block = jnp.concatenate(
        [
            in_place([piece[:pre_part] for piece in qkv_ring]),
            in_place([piece[pre_part:] for piece in qkv_ring]),
        ],
        axis=0,
    )
    pre_block = groups * pre_part
    out_block = in_place(out_ring)
    qkv_full = jnp.concatenate(dp_gather(qkv_block), axis=0)
    out_full = jnp.concatenate(dp_gather(out_block), axis=0)
    gate_full = lax.all_gather(pre_gate, "dp", axis=0, tiled=True)
    down_full = lax.all_gather(pre_down, "dp", axis=1, tiled=True)
    act_stack = jnp.concatenate([act_gate, act_up, act_down.T], axis=0)
    act_flat_w = lax.all_gather(act_stack, "dp", axis=0, tiled=True)
    up_full = lax.all_gather(after(pre_up, act_flat_w), "dp", axis=0, tiled=True)
    act_all = act_flat_w.reshape(ways, 3, -1, act_gate.shape[1])
    act_gate_full, act_up_full, act_down_full = (
        act_all[:, n].reshape(act_width, -1) for n in range(3)
    )

    pre_flat = prefix_tokens.reshape(items * pre_rows, width)
    act_flat = action_tokens.reshape(items * act_rows, act_width)
    cot_flat = prefix_cot.reshape(items * pre_rows, width)
    pre_x = pre_flat.astype(F32)
    act_x = act_flat.astype(F32)
    live_mask = live_dims[:, None, :].astype(F32)
    pred_back = (pred_cot * live_mask).astype(BF16).reshape(items * act_rows, -1)
    act_final_back = mm_nt(pred_back, action_head)
    count = items * pre_rows
    padded = -(-count // 16) * 16
    act_count = items * act_rows

    def pad(values):
        return jnp.pad(values, ((0, padded - count), (0, 0)))

    def ring_stack(value):
        return jnp.concatenate(ring_gather(value), axis=0)

    cot_all = ring_stack(pad(cot_flat))
    act_cot_all = ring_stack(act_final_back.astype(BF16))
    hidden_back = mm_nt(cot_all, down_full).astype(BF16)

    local_pos = jnp.concatenate(
        [
            member * pre_rows + jnp.arange(pre_rows),
            pre_len + member * act_rows + jnp.arange(act_rows),
        ]
    )
    cosine_tab, sine_tab = rope_tables(local_pos, head_dim)

    def blocks_of(which):
        return jnp.concatenate(
            [
                lax.dynamic_slice_in_dim(block_ids, which * pre_rows, pre_rows, 1),
                lax.dynamic_slice_in_dim(block_ids, pre_len + which * act_rows, act_rows, 1),
            ],
            axis=1,
        )

    local_blocks = blocks_of(member)
    key_blocks = jnp.concatenate(
        [blocks_of((member - r) % groups) for r in range(groups)], axis=1
    )
    allowed = key_blocks[:, None, None, :] <= local_blocks[:, None, :, None]

    act_padded = -(-act_count // 16) * 16

    def stack(pre_part_rows, act_part_rows):
        return (
            jnp.pad(pre_part_rows, ((0, padded - count), (0, 0))),
            jnp.pad(act_part_rows, ((0, act_padded - act_count), (0, 0))),
        )

    def to_items(joint):
        return jnp.concatenate(
            [
                joint[:count].reshape(items, pre_rows, -1),
                joint[padded : padded + act_count].reshape(items, act_rows, -1),
            ],
            axis=1,
        )

    def from_items(values):
        return jnp.concatenate(
            stack(
                values[:, :pre_rows].reshape(count, -1),
                values[:, pre_rows:].reshape(act_count, -1),
            ),
            axis=0,
        )

    normed = spread(
        *stack(
            rms_norm(pre_x, pre_attn_gain).astype(BF16),
            rms_norm(act_x, act_attn_gain).astype(BF16),
        ),
        order,
    )
    keyval_raw = to_items(mm(normed, qkv_full[:, query_width:]))
    keyval_rows = jnp.concatenate(
        [rotate(keyval_raw[..., :head_dim], cosine_tab, sine_tab), keyval_raw[..., head_dim:]],
        axis=-1,
    ).astype(BF16)
    all_keyval = jnp.concatenate(ring_gather(keyval_rows), axis=1)
    key_rows = all_keyval[..., :head_dim]
    value_rows = all_keyval[..., head_dim:]
    query_raw = to_items(mm(normed, qkv_full[:, :query_width]))
    query_rows = rotate(
        query_raw.reshape(items, local_len, heads, head_dim),
        cosine_tab[:, None, :],
        sine_tab[:, None, :],
    ).astype(BF16)
    scores = (
        jnp.einsum("iqhd,ikd->ihqk", query_rows, key_rows, preferred_element_type=F32) * scale
    )
    probs = jax.nn.softmax(jnp.where(allowed, scores, MASKED), axis=-1)
    probs_low = probs.astype(BF16)
    attended = jnp.einsum("ihqk,ikd->iqhd", probs_low, value_rows, preferred_element_type=F32)
    attended = attended.astype(BF16).reshape(items, local_len, query_width)
    (att_joint,) = permute_columns([from_items(attended)], order)
    mid = mm(att_joint, out_full)
    pre_mid = pre_x + mid[:count, :width]
    act_mid = act_x + mid[padded : padded + act_count, width:]

    act_second = rms_norm(act_mid, act_mlp_gain).astype(BF16)
    act_all_rows = jnp.concatenate(ring_gather(act_second, LOOSE), axis=0)
    slot_count = lax.dynamic_index_in_dim(hidden_counts, member, keepdims=False)
    slot_live = (jnp.arange(act_gate.shape[1]) < slot_count).astype(F32)

    def scatter_sum(value, dimension):
        return lax.psum_scatter(value, "dp", scatter_dimension=dimension, tiled=True)

    def split(partial):
        size = partial.shape[0] // groups
        return [partial[r * size : (r + 1) * size] for r in range(groups)]

    act_hidden, act_gate_back, act_up_back = feed_forward(
        act_all_rows, act_cot_all, act_gate_full, act_up_full, act_down_full, slot_live
    )
    act_terms = [
        mm_tn(act_all_rows, act_gate_back).astype(BF16),
        mm_tn(act_all_rows, act_up_back).astype(BF16),
        mm_tn(act_cot_all, act_hidden).astype(BF16),
    ]
    act_second_part = split(mm_nt(act_gate_back, act_gate_full) + mm_nt(act_up_back, act_up_full))
    act_sum_part = split(mm_nt(act_hidden, act_down_full))

    pre_second = pad(rms_norm(pre_mid, pre_mlp_gain).astype(BF16))
    second_pieces = [pre_second]
    for r in range(1, groups):
        piece = ring(second_pieces[-1], 1)
        if r == 1:
            piece, hidden_back = lax.optimization_barrier((piece, hidden_back))
        if r == groups - 1:
            piece, act_terms = lax.optimization_barrier((piece, act_terms))
        second_pieces.append(piece)
    act_stacked = jnp.concatenate(
        [term.reshape(ways, -1, act_gate.shape[1]) for term in act_terms], axis=1
    ).reshape(-1, act_gate.shape[1])
    grad_act = scatter_sum(act_stacked, 0)
    grad_act = grad_act.astype(F32).reshape(3, -1, act_gate.shape[1])
    grad_act_gate, grad_act_up, grad_act_down = grad_act[0], grad_act[1], grad_act[2].T

    pre_hidden, pre_gate_back, pre_up_back, pre_all = feed_forward_kernel(
        second_pieces, hidden_back, gate_full, up_full
    )
    gate_term = mm_tn(pre_all, pre_gate_back).astype(BF16)
    gate_term, pre_up_back = lax.optimization_barrier((gate_term, pre_up_back))
    grad_pre_gate = scatter_sum(gate_term, 0)
    half = groups // 2 * padded

    def second_rows(cut, gate_rows, up_rows):
        return mm_nt(gate_rows[cut], gate_full) + mm_nt(up_rows[cut], up_full)

    later = second_rows(slice(half, None), pre_gate_back, pre_up_back)
    later, gate_rows, up_rows = lax.optimization_barrier((later, pre_gate_back, pre_up_back))
    sooner = second_rows(slice(0, half), gate_rows, up_rows)

    act_lines = act_count * act_width // width

    def pack(pre_part_rows, act_part_rows):
        return jnp.concatenate([pre_part_rows, act_part_rows.reshape(act_lines, width)], axis=0)

    def unpack(packed):
        return packed[:count], packed[count:].reshape(act_count, act_width)

    def second_part(r):
        rows = sooner if r < groups // 2 else later
        return pack(rows[r % (groups // 2) * padded :][:count], act_second_part[r])

    up_term = down_term = None
    total = second_part(groups - 1)
    for r in range(groups - 2, -1, -1):
        moved = ring(total.astype(BF16), -1, LOOSE)
        if r == groups - 2:
            moved, up_rows = lax.optimization_barrier((moved, after(up_rows, sooner)))
            up_term = mm_tn(pre_all, up_rows).astype(BF16)
        elif r == groups - 3:
            moved, up_term, pre_hidden = lax.optimization_barrier((moved, up_term, pre_hidden))
            down_term = mm_tn(pre_hidden, cot_all).astype(BF16)
        elif r == groups - 4:
            moved, down_term = lax.optimization_barrier((moved, down_term))
        total = moved.astype(F32) + second_part(r)
    grad_pre_up = scatter_sum(up_term, 0)
    grad_pre_down = scatter_sum(down_term, 1)
    pre_second_back, act_second_back = unpack(total)

    pre_mid_part, grad_pre_mlp_gain = rms_back(pre_mid, pre_mlp_gain, pre_second_back)
    act_mid_part, grad_act_mlp_gain = rms_back(act_mid, act_mlp_gain, act_second_back)
    pre_mid_grad = cot_flat.astype(F32) + pre_mid_part
    act_mid_grad = act_final_back + act_mid_part
    back_joint = jnp.concatenate(
        [
            jnp.pad(pre_mid_grad.astype(BF16), ((0, padded - count), (0, act_width))),
            jnp.pad(act_mid_grad.astype(BF16), ((0, act_padded - act_count), (width, 0))),
        ],
        axis=0,
    )
    attended_back = to_items(
        permute_columns([mm_nt(back_joint, out_full).astype(BF16)], order, True)[0]
    ).reshape(items, local_len, heads, head_dim)
    out_half = query_width // 2
    grad_out = scatter_rows(
        mm_tn(att_joint[:, :out_half], back_joint).astype(BF16),
        mm_tn(att_joint[:, out_half:], back_joint).astype(BF16),
        (out_part,),
    )
    probs_back = jnp.einsum(
        "iqhd,ikd->ihqk", attended_back, value_rows, preferred_element_type=F32
    )
    value_back = jnp.einsum(
        "ihqk,iqhd->ikd", probs_low, attended_back, preferred_element_type=F32
    )
    scores_back = (
        probs * (probs_back - jnp.sum(probs * probs_back, axis=-1, keepdims=True))
    ).astype(BF16)
    key_back = (
        jnp.einsum("ihqk,iqhd->ikd", scores_back, query_rows, preferred_element_type=F32) * scale
    )
    query_back = (
        jnp.einsum("ihqk,ikd->iqhd", scores_back, key_rows, preferred_element_type=F32) * scale
    )
    keyval_back = jnp.concatenate([key_back, value_back], axis=-1).astype(BF16)
    keyval_back, pre_hidden = lax.optimization_barrier((keyval_back, pre_hidden))
    pre_sum_part = split(mm(pre_hidden, down_full))
    pre_sums, act_sums = unpack(
        ring_scatter([pack(each[:count], rest) for each, rest in zip(pre_sum_part, act_sum_part)])
    )
    own_kv_back = ring_scatter(
        [keyval_back[:, r * local_len : (r + 1) * local_len] for r in range(groups)]
    )
    keyval_low = jnp.concatenate(
        [rotate(own_kv_back[..., :head_dim], cosine_tab, -sine_tab), own_kv_back[..., head_dim:]],
        axis=-1,
    ).astype(BF16)
    query_low = rotate(query_back, cosine_tab[:, None, :], -sine_tab[:, None, :])
    query_low = query_low.reshape(items, local_len, query_width).astype(BF16)
    back_rows = from_items(jnp.concatenate([query_low, keyval_low], axis=-1))
    back_rows, grad_pre_gate = lax.optimization_barrier((back_rows, grad_pre_gate))
    qkv_half = normed.shape[1] // 2
    grad_qkv = scatter_rows(
        mm_tn(normed[:, :qkv_half], back_rows).astype(BF16),
        mm_tn(normed[:, qkv_half:], back_rows).astype(BF16),
        (pre_part, act_part),
    )

    prefix_out = (pre_mid + pre_sums).astype(BF16).reshape(prefix_tokens.shape)
    act_final_low = (act_mid + act_sums).astype(BF16)
    action_pred = mm(act_final_low, action_head).reshape(pred_cot.shape) * live_mask
    grad_head = mm_tn(act_final_low, pred_back)

    pre_normed_back, act_normed_back = unspread(
        mm_nt(back_rows, qkv_full), padded, width, act_width, order
    )
    pre_normed_back, act_normed_back = pre_normed_back[:count], act_normed_back[:act_count]
    pre_x_part, grad_pre_attn_gain = rms_back(pre_x, pre_attn_gain, pre_normed_back)
    act_x_part, grad_act_attn_gain = rms_back(act_x, act_attn_gain, act_normed_back)
    prefix_grad = (pre_mid_grad + pre_x_part).reshape(prefix_tokens.shape)
    action_grad = (act_mid_grad + act_x_part).reshape(action_tokens.shape)

    devices = ways * groups
    small = jnp.concatenate(
        [
            value.reshape(devices, -1)
            for value in (
                grad_pre_attn_gain,
                grad_pre_mlp_gain,
                grad_act_attn_gain,
                grad_act_mlp_gain,
                grad_head,
            )
        ],
        axis=1,
    )
    bit = 1
    while bit < ways:
        small = small + hop(small, bit)
        bit *= 2
    mine = lax.axis_index("dp") * groups
    terms = [
        lax.dynamic_slice_in_dim(small, mine + (member - r) % groups, 1, 0) for r in range(groups)
    ]
    total = terms[-1]
    for term in terms[-2::-1]:
        total = ring(total, -1, LOOSE) + term
    sizes = [width // devices] * 2 + [act_width // devices] * 2
    gains, start = [], 0
    for size in sizes:
        gains.append(total[0, start : start + size])
        start += size
    grad_head = total[0, start:].reshape(act_width // devices, -1)

    return (
        prefix_out,
        action_pred,
        prefix_grad,
        action_grad,
        *gains,
        grad_qkv[:pre_part, :query_width],
        grad_qkv[:pre_part, query_width:],
        grad_out[:, :width],
        grad_qkv[pre_part:, :query_width],
        grad_qkv[pre_part:, query_width:],
        grad_out[:, width:],
        grad_pre_gate.astype(F32),
        grad_pre_up.astype(F32),
        grad_pre_down.astype(F32),
        grad_act_gate,
        grad_act_up,
        grad_act_down,
        grad_head,
    )


def solution(mesh):
    rows = P("dp", "mp", None)
    both = P(("dp", "mp"), None)
    wide = P("dp", "mp")
    tall = P("mp", "dp")
    in_specs = (
        (rows, rows, P("dp", None), P("dp", None))
        + (P(),) * 5
        + (both,) * 6
        + (wide, wide, tall, wide, wide, tall, P(), rows, rows)
    )
    out_specs = (
        (rows,) * 4
        + (P(("dp", "mp")),) * 4
        + (both,) * 6
        + (wide, wide, tall, wide, wide, tall, both)
    )
    return jax.shard_map(shards, mesh=mesh, in_specs=in_specs, out_specs=out_specs, check_vma=False)
```

time: 1860 us -> 1210 us (0.65)
  waiting for transfers between devices: 843 us -> 527 us
  other arithmetic: 202 us -> 94.4 us
  matrix products: 380 us -> 291 us
  starting transfers between devices: 123 us -> 65.5 us
  local copies, waits for them, and re-layouts: 204 us -> 156 us
  Pallas kernels: 87.7 us -> 54.3 us
    ppermute x144 -> x68, waiting for transfers between devices: 843 us -> 525 us  [the longest x28 273 us: send(): result = lax.ppermute(value, axis, pairs)]
    dot_general x13 -> x8, matrix products: 124 us -> 45.8 us  [mm(): lax.dot_general(left, right, (((1,), (0,)), ((), ())), preferred_element_...]
    ppermute x144 -> x68, starting transfers between devices: 123 us -> 64.5 us  [the longest x21 35.4 us: ring(): return lax.ppermute(value, 'mp', pairs)]
    unnamed x392 -> x315, local copies, waits for them, and re-layouts: 135 us -> 92 us
    concatenate x14 -> x7, other arithmetic: 54.4 us -> 15.7 us  [the longest x1 12.3 us: shards(): jnp.concatenate([term.reshape(ways, -1, act_gate.shape[1]) for term in ac...]
    add x23 -> x10, other arithmetic: 53.4 us -> 15.8 us  [the longest x2 8.38 us: scatter_rows(): total = total + lax.ppermute(block(c).astype(BF16), 'dp', pairs).astype(F32)]
    pallas_call x16 -> x5, Pallas kernels: 87.7 us -> 54.3 us  [the longest x1 51.3 us: feed_forward_kernel(): pl.pallas_call(functools.partial(_feed_forward_tile, groups), grid=(units...]
    dot_general x21 -> x11, matrix products: 134 us -> 112 us  [mm_tn(): lax.dot_general(left, right, (((0,), (0,)), ((), ())), preferred_element_...]
  transfers between devices with their start and end apart: 144 -> 76, of which waited for: 61 -> 33; matrix products, arithmetic and copies ran while one was open for 41% -> 43% of each run, Pallas kernels for 4% -> 5%
where the time goes in v2:
time: 1210 us; the launch traced here: 1200 us
  waiting for transfers between devices  527 us (44%)
  matrix products  291 us (24%)
  local copies, waits for them, and re-layouts  156 us (13%)
  other arithmetic  94.4 us (8%)
  starting transfers between devices  65.5 us (5%)
  Pallas kernels  54.3 us (4%)
  between operations  16.7 us (1%)
    ppermute x28, waiting for transfers between devices, send(): result = lax.ppermute(value, axis, pairs)  273 us
    ppermute x6, waiting for transfers between devices, scatter_rows(): total = total + lax.ppermute(block(c).astype(BF16), 'dp', pairs).astype(F32)  170 us
    dot_general x11, matrix products, mm_nt(): lax.dot_general(left, right, (((1,), (1,)), ((), ())), preferred_element_...  124 us
    dot_general x11, matrix products, mm_tn(): lax.dot_general(left, right, (((0,), (0,)), ((), ())), preferred_element_...  112 us
    unnamed x315, local copies, waits for them, and re-layouts  92 us
    ppermute x21, waiting for transfers between devices, ring(): return lax.ppermute(value, 'mp', pairs)  82 us
    pallas_call x1, Pallas kernels, feed_forward_kernel(): pl.pallas_call(functools.partial(_feed_forward_tile, groups), grid=(units...  51.3 us
    dot_general x8, matrix products, mm(): lax.dot_general(left, right, (((1,), (0,)), ((), ())), preferred_element_...  45.8 us
  transfers between devices with their start and end apart: 76, of which 33 were waited for; matrix products, arithmetic and copies ran while one was open for 43% of the time, Pallas kernels for 5%

profile of v2, /device:TPU:0, one launch (start us, length us, event | category | flops | bytes accessed | tf_op | source)
XLA Modules:
  0.0 1204.5 jit_solution(1367558715581324905)
XLA Ops:
  31.3 13.0 %collective-permute-done.1 = bf16[96,2560]{1,0:T(8,128)(2,1)} collective-permute-done((bf16[96,2560]{1,0:T(8,128)(2,1)S(1)}, bf16[96,2560]{1,0:T(8,128)(2,1)}, u32[]{:S(2)}, u32[]{:S(2)}) %collective-permute-start.1) | collective-permute-done | bytes 491552 | tf_op jit(solution)/shard_map/ppermute | solution.py:26
  55.0 11.4 collective-permute-done.12
  100.4 8.5 collective-permute-done.15
  110.0 23.4 %collective-permute-done.14 = bf16[288,2048]{1,0:T(8,128)(2,1)S(1)} collective-permute-done((bf16[288,2048]{1,0:T(8,128)(2,1)S(1)}, bf16[288,2048]{1,0:T(8,128)(2,1)S(1)}, u32[]{:S(2)}, u32[]{:S(2)}) %collective-permute-start.14) | collective-permute-done | bytes 1179680 | tf_op jit(solution)/shard_map/ppermute | solution.py:26
  134.8 41.7 %collective-permute-done.4 = bf16[384,2560]{1,0:T(8,128)(2,1)S(1)} collective-permute-done((bf16[384,2560]{1,0:T(8,128)(2,1)S(1)}, bf16[384,2560]{1,0:T(8,128)(2,1)S(1)}, u32[]{:S(2)}, u32[]{:S(2)}) %collective-permute-start.4) | collective-permute-done | bytes 1966112 | tf_op jit(solution)/shard_map/ppermute | solution.py:26
  183.7 38.6 %collective-permute-done.6 = bf16[192,2560]{1,0:T(8,128)(2,1)S(1)} collective-permute-done((bf16[192,2560]{1,0:T(8,128)(2,1)S(1)}, bf16[192,2560]{1,0:T(8,128)(2,1)S(1)}, u32[]{:S(2)}, u32[]{:S(2)}) %collective-permute-start.6) | collective-permute-done | bytes 983072 | tf_op jit(solution)/shard_map/ppermute | solution.py:26
  228.0 42.1 %collective-permute-done.25 = bf16[256,3072]{1,0:T(8,128)(2,1)} collective-permute-done((bf16[256,3072]{1,0:T(8,128)(2,1)}, bf16[256,3072]{1,0:T(8,128)(2,1)}, u32[]{:S(2)}, u32[]{:S(2)}) %collective-permute-start.25) | collective-permute-done | bytes 1572896 | tf_op jit(solution)/shard_map/ppermute | solution.py:26
  292.2 18.5 %collective-permute-done.18 = bf16[288,2048]{1,0:T(8,128)(2,1)S(1)} collective-permute-done((bf16[288,2048]{1,0:T(8,128)(2,1)S(1)}, bf16[288,2048]{1,0:T(8,128)(2,1)S(1)}, u32[]{:S(2)}, u32[]{:S(2)}) %collective-permute-start.18) | collective-permute-done | bytes 1179680 | tf_op jit(solution)/shard_map/ppermute | solution.py:26
  348.1 8.9 collective-permute-done.23
  396.8 25.2 %convolution_convert_fusion.3.refs_4_ = bf16[1152,4096]{1,0:T(8,128)(2,1)} fusion(bf16[4096,2048]{1,0:T(8,128)(2,1)} %all-gather.5.cloned.1.call-done, bf16[288,2048]{1,0:T(8,128)(2,1)} %copy-done.120, bf16[288,2048]{1,0:T(8,128)(2,1)} %copy-done.118, bf16[288,2048]{1,0:T(8,128)(2,1)} %copy-done.116, bf16[288,2048]{1,0:T(8,128)(2,1)S(1)} %copy-done.63), kind=kOutput, calls=%fused_computation.4 | convolution fusion | flops 19350945792 | bytes 30932992 | tf_op jit(solution)/shard_map/dot_general | solution.py:267
  432.9 17.9 %collective-permute-done.34.refs_2_ = bf16[288,2048]{1,0:T(8,128)(2,1)S(1)} collective-permute-done((bf16[288,2048]{1,0:T(8,128)(2,1)}, bf16[288,2048]{1,0:T(8,128)(2,1)S(1)}, u32[]{:S(2)}, u32[]{:S(2)}) %collective-permute-start.34) | collective-permute-done | bytes 1179680 | tf_op jit(solution)/shard_map/ppermute | solution.py:26
  457.0 21.5 %collective-permute-done.35.refs_3_ = bf16[288,2048]{1,0:T(8,128)(2,1)S(1)} collective-permute-done((bf16[288,2048]{1,0:T(8,128)(2,1)S(1)}, bf16[288,2048]{1,0:T(8,128)(2,1)S(1)}, u32[]{:S(2)}, u32[]{:S(2)}) %collective-permute-start.35) | collective-permute-done | bytes 1179680 | tf_op jit(solution)/shard_map/ppermute | solution.py:26
  478.5 12.3 %pad_maximum_fusion = bf16[8,384,2048]{2,1,0:T(8,128)(2,1)} fusion(bf16[8,128,2048]{2,1,0:T(8,128)(2,1)S(1)} %bitcast.136, bf16[8,128,2048]{2,1,0:T(8,128)(2,1)S(1)} %bitcast.134, bf16[8,128,2048]{2,1,0:T(8,128)(2,1)S(1)} %bitcast.135), kind=kLoop, calls=%fused_computation.7 | loop fusion | flops 37748736 | bytes 25165824 | tf_op jit(solution)/shard_map/concatenate | solution.py:556
  491.1 51.3 %shard_map.393 = (bf16[1152,4096]{1,0:T(8,128)(2,1)}, bf16[1152,4096]{1,0:T(8,128)(2,1)}, bf16[1152,4096]{1,0:T(8,128)(2,1)}, bf16[1152,2048]{1,0:T(8,128)(2,1)}) custom-call(bf16[288,2048]{1,0:T(8,128)(2,1)} %copy-done.65, bf16[288,2048]{1,0:T(8,128)(2,1)} %collective-permute-done.33.refs_1_, bf16[288,2048]{1,0:T(8,128)(2,1)} %copy-done.122, ...), custom_call_target="tpu_custom_call" | custom-call | flops 38654705664 | bytes 80740352 | tf_op jit(solution)/shard_map/pallas_call | solution.py:322
  542.3 27.8 %convolution_convert_fusion.2 = bf16[2048,4096]{1,0:T(8,128)(2,1)} fusion(bf16[1152,2048]{1,0:T(8,128)(2,1)} %get-tuple-element.98, bf16[1152,4096]{1,0:T(8,128)(2,1)} %get-tuple-element.103), kind=kOutput, calls=%fused_computation.3 | convolution fusion | flops 19335741440 | bytes 30932992 | tf_op jit(solution)/shard_map/dot_general | solution.py:271
  576.8 16.4 %fusion.11 = f32[576,2048]{1,0:T(8,128)} fusion(bf16[2048,4096]{1,0:T(8,128)(2,1)} %all-gather.11.cloned.1.call-done.refs_6_, bf16[1152,4096]{1,0:T(8,128)(2,1)} %get-tuple-element.106), kind=kOutput, calls=%fused_computation.25 | convolution fusion | flops 9663676416 | bytes 26214400 | tf_op jit(solution)/shard_map/dot_general | solution.py:267
  593.2 19.7 %fusion.17 = f32[576,2048]{1,0:T(8,128)} fusion(f32[576,2048]{1,0:T(8,128)} %fusion.11, bf16[2048,4096]{1,0:T(8,128)(2,1)} %all-gather.9.cloned.1.call-done.refs_5_, bf16[1152,4096]{1,0:T(8,128)(2,1)} %get-tuple-element.103), kind=kOutput, calls=%fused_computation.40 | convolution fusion | flops 9664856064 | bytes 30932992 | tf_op jit(solution)/shard_map/dot_general | solution.py:267
  615.0 16.3 %fusion.7 = f32[576,2048]{1,0:T(8,128)} fusion(bf16[2048,4096]{1,0:T(8,128)(2,1)} %all-gather.11.cloned.1.call-done.refs_6_, bf16[1152,4096]{1,0:T(8,128)(2,1)} %get-tuple-element.106), kind=kOutput, calls=%fused_computation.21 | convolution fusion | flops 9663676416 | bytes 26214400 | tf_op jit(solution)/shard_map/dot_general | solution.py:267
  631.4 17.5 %fusion.20 = f32[576,2048]{1,0:T(8,128)} fusion(f32[576,2048]{1,0:T(8,128)} %fusion.7, bf16[2048,4096]{1,0:T(8,128)(2,1)} %all-gather.9.cloned.1.call-done.refs_5_, bf16[1152,4096]{1,0:T(8,128)(2,1)} %get-tuple-element.103), kind=kOutput, calls=%fused_computation.41 | convolution fusion | flops 9664856064 | bytes 30932992 | tf_op jit(solution)/shard_map/dot_general | solution.py:267
  651.3 28.0 %convolution_convert_fusion.1 = bf16[2048,4096]{1,0:T(8,128)(2,1)} fusion(bf16[1152,2048]{1,0:T(8,128)(2,1)} %get-tuple-element.98, bf16[1152,4096]{1,0:T(8,128)(2,1)} %get-tuple-element.106), kind=kOutput, calls=%fused_computation.2 | convolution fusion | flops 19335741440 | bytes 30932992 | tf_op jit(solution)/shard_map/dot_general | solution.py:271
  698.6 27.1 %convolution_convert_fusion = bf16[4096,2048]{1,0:T(8,128)(2,1)} fusion(bf16[1152,4096]{1,0:T(8,128)(2,1)} %get-tuple-element.111, bf16[288,2048]{1,0:T(8,128)(2,1)S(1)} %copy-done.121, bf16[288,2048]{1,0:T(8,128)(2,1)S(1)} %copy-done.119, bf16[288,2048]{1,0:T(8,128)(2,1)S(1)} %copy-done.117, bf16[288,2048]{1,0:T(8,128)(2,1)S(1)} %copy-done.64), kind=kOutput, calls=%fused_computation.1 | convolution fusion | flops 19354615808 | bytes 30932992 | tf_op jit(solution)/shard_map/dot_general | solution.py:271
  736.8 10.0 convolution_convert_fusion.11.refs_0_
  767.5 23.9 %fusion.109 = f32[1152,2048]{1,0:T(8,128)S(1)} fusion(bf16[1152,4096]{1,0:T(8,128)(2,1)} %get-tuple-element.111, bf16[4096,2048]{1,0:T(8,128)(2,1)} %all-gather.5.cloned.1.call-done), kind=kOutput, calls=%fused_computation.326 | convolution fusion | flops 19327352832 | bytes 35651584 | tf_op jit(solution)/shard_map/dot_general | solution.py:263
  798.9 28.5 %collective-permute-done.46 = bf16[2,152,512]{2,1,0:T(8,128)(2,1)S(1)} collective-permute-done((bf16[2,152,512]{2,1,0:T(8,128)(2,1)S(1)}, bf16[2,152,512]{2,1,0:T(8,128)(2,1)S(1)}, u32[]{:S(2)}, u32[]{:S(2)}) %collective-permute-start.46) | collective-permute-done | bytes 311328 | tf_op jit(solution)/shard_map/ppermute | solution.py:49
  850.2 17.3 %collective-permute-done.43 = bf16[292,2048]{1,0:T(8,128)(2,1)} collective-permute-done((bf16[292,2048]{1,0:T(8,128)(2,1)}, bf16[292,2048]{1,0:T(8,128)(2,1)}, u32[]{:S(2)}, u32[]{:S(2)}) %collective-permute-start.43) | collective-permute-done | bytes 1196064 | tf_op jit(solution)/shard_map/ppermute | solution.py:49
  884.8 7.8 convolution_convert_fusion.4
  902.4 39.0 %collective-permute-done.62 = bf16[256,3072]{1,0:T(8,128)(2,1)} collective-permute-done((bf16[256,3072]{1,0:T(8,128)(2,1)}, bf16[256,3072]{1,0:T(8,128)(2,1)}, u32[]{:S(2)}, u32[]{:S(2)}) %collective-permute-start.62) | collective-permute-done | bytes 1572896 | tf_op jit(solution)/shard_map/ppermute | solution.py:117
  941.4 55.8 %collective-permute-done.64 = bf16[256,3072]{1,0:T(8,128)(2,1)} collective-permute-done((bf16[256,3072]{1,0:T(8,128)(2,1)}, bf16[256,3072]{1,0:T(8,128)(2,1)}, u32[]{:S(2)}, u32[]{:S(2)}) %collective-permute-start.64) | collective-permute-done | bytes 1572896 | tf_op jit(solution)/shard_map/ppermute | solution.py:117
  1033.3 9.3 fusion.112.joint
  1078.3 34.0 %collective-permute-done.55 = bf16[384,2560]{1,0:T(8,128)(2,1)S(1)} collective-permute-done((bf16[384,2560]{1,0:T(8,128)(2,1)}, bf16[384,2560]{1,0:T(8,128)(2,1)S(1)}, u32[]{:S(2)}, u32[]{:S(2)}) %collective-permute-start.55) | collective-permute-done | bytes 1966112 | tf_op jit(solution)/shard_map/ppermute | solution.py:117
  1112.3 39.9 %collective-permute-done.57 = bf16[384,2560]{1,0:T(8,128)(2,1)} collective-permute-done((bf16[384,2560]{1,0:T(8,128)(2,1)}, bf16[384,2560]{1,0:T(8,128)(2,1)}, u32[]{:S(2)}, u32[]{:S(2)}) %collective-permute-start.57) | collective-permute-done | bytes 1966112 | tf_op jit(solution)/shard_map/ppermute | solution.py:117
  1159.4 8.4 collective-permute-done.58
  (673 shorter events, 426.8 us)
Async XLA Ops:
  7.2 78.9 %all-gather.7.cloned.1.call-start = ((), (), s32[]{:S(2)}) async-start(), calls=%async_computation.5 | async-start | bytes 14155776 | tf_op jit(solution)/shard_map/all_gather | solution.py:413
  11.2 385.6 %all-gather.5.cloned.1.call-start = ((), (), s32[]{:S(2)}) async-start(), calls=%async_computation.4 | async-start | bytes 18874368 | tf_op jit(solution)/shard_map/all_gather | solution.py:411
  12.0 479.1 %all-gather.9.cloned.1.call-start = ((), (), s32[]{:S(2)}) async-start(), calls=%async_computation.6 | async-start | bytes 18874368 | tf_op jit(solution)/shard_map/all_gather | solution.py:410
  12.7 478.4 %all-gather.11.cloned.1.call-start = ((), (), s32[]{:S(2)}) async-start(), calls=%async_computation.7 | async-start | bytes 18874368 | tf_op jit(solution)/shard_map/all_gather | solution.py:414
  86.1 600.2 %reduce-scatter.13.cloned.1.call-start = ((), (), s32[]{:S(2)}) async-start(), calls=%async_computation.11 | async-start | bytes 14155776
  96.7 129.6 %collective-permute-start.7 = (bf16[384,2560]{1,0:T(8,128)(2,1)S(1)}, bf16[384,2560]{1,0:T(8,128)(2,1)S(1)}, u32[]{:S(2)}, u32[]{:S(2)}) collective-permute-start(bf16[384,2560]{1,0:T(8,128)(2,1)S(1)} %pad_maximum_fusion.2), channel_id=1, source_target_pairs={{0,4},{4,0},{8,12},{12,8},{16,20},{20,16},{24,28},{28,24},{1,5},{5... | collective-permute-start | bytes 5898248 | tf_op jit(solution)/shard_map/ppermute | solution.py:38
  96.8 79.7 %collective-permute-start.4 = (bf16[384,2560]{1,0:T(8,128)(2,1)S(1)}, bf16[384,2560]{1,0:T(8,128)(2,1)S(1)}, u32[]{:S(2)}, u32[]{:S(2)}) collective-permute-start(bf16[384,2560]{1,0:T(8,128)(2,1)S(1)} %pad_maximum_fusion.2), channel_id=1, source_target_pairs={{0,16},{4,20},{8,24},{12,28},{16,0},{20,4},{24,8},{28,12},{1,17},{... | collective-permute-start | bytes 5898248 | tf_op jit(solution)/shard_map/ppermute | solution.py:26
  97.8 80.4 %collective-permute-start.3 = (bf16[384,2560]{1,0:T(8,128)(2,1)S(1)}, bf16[384,2560]{1,0:T(8,128)(2,1)S(1)}, u32[]{:S(2)}, u32[]{:S(2)}) collective-permute-start(bf16[384,2560]{1,0:T(8,128)(2,1)S(1)} %pad_maximum_fusion.2), channel_id=1, source_target_pairs={{0,8},{4,12},{8,0},{12,4},{16,24},{20,28},{24,16},{28,20},{1,9},{5... | collective-permute-start | bytes 5898248 | tf_op jit(solution)/shard_map/ppermute | solution.py:26
  133.4 48.3 %collective-permute-start.16 = (bf16[288,2048]{1,0:T(8,128)(2,1)S(1)}, bf16[288,2048]{1,0:T(8,128)(2,1)S(1)}, u32[]{:S(2)}, u32[]{:S(2)}) collective-permute-start(bf16[288,2048]{1,0:T(8,128)(2,1)S(1)} %collective-permute-done.14), channel_id=1, source_target_pairs={{0,1},{1,2},{2,3},{3,0},{4,5},{5,6},{6,7},{7,4},{8,9},{9,10},{10,1... | collective-permute-start | bytes 3538952 | tf_op jit(solution)/shard_map/ppermute | solution.py:26
  176.6 45.7 %collective-permute-start.6 = (bf16[192,2560]{1,0:T(8,128)(2,1)S(1)}, bf16[192,2560]{1,0:T(8,128)(2,1)S(1)}, u32[]{:S(2)}, u32[]{:S(2)}) collective-permute-start(bf16[192,2560]{1,0:T(8,128)(2,1)S(1)} %slice.446), channel_id=1, source_target_pairs={{0,8},{4,12},{8,0},{12,4},{16,24},{20,28},{24,16},{28,20},{1,9},{5... | collective-permute-start | bytes 2949128 | tf_op jit(solution)/shard_map/ppermute | solution.py:26
  178.3 45.7 %collective-permute-start.5 = (bf16[192,2560]{1,0:T(8,128)(2,1)S(1)}, bf16[192,2560]{1,0:T(8,128)(2,1)S(1)}, u32[]{:S(2)}, u32[]{:S(2)}) collective-permute-start(bf16[192,2560]{1,0:T(8,128)(2,1)S(1)} %slice.445), channel_id=1, source_target_pairs={{0,16},{4,20},{8,24},{12,28},{16,0},{20,4},{24,8},{28,12},{1,17},{... | collective-permute-start | bytes 2949128 | tf_op jit(solution)/shard_map/ppermute | solution.py:26
  180.2 89.9 %collective-permute-start.25 = (bf16[256,3072]{1,0:T(8,128)(2,1)}, bf16[256,3072]{1,0:T(8,128)(2,1)}, u32[]{:S(2)}, u32[]{:S(2)}) collective-permute-start(bf16[256,3072]{1,0:T(8,128)(2,1)} %get-tuple-element.87), channel_id=1, source_target_pairs={{0,16},{4,20},{8,24},{12,28},{16,0},{20,4},{24,8},{28,12},{1,17},{... | collective-permute-start | bytes 4718600 | tf_op jit(solution)/shard_map/ppermute | solution.py:26
  181.7 92.0 %collective-permute-start.24 = (bf16[256,3072]{1,0:T(8,128)(2,1)}, bf16[256,3072]{1,0:T(8,128)(2,1)}, u32[]{:S(2)}, u32[]{:S(2)}) collective-permute-start(bf16[256,3072]{1,0:T(8,128)(2,1)} %get-tuple-element.87), channel_id=1, source_target_pairs={{0,8},{4,12},{8,0},{12,4},{16,24},{20,28},{24,16},{28,20},{1,9},{5... | collective-permute-start | bytes 4718600 | tf_op jit(solution)/shard_map/ppermute | solution.py:26
  222.3 56.5 %collective-permute-start.8 = (bf16[384,2560]{1,0:T(8,128)(2,1)S(1)}, bf16[384,2560]{1,0:T(8,128)(2,1)S(1)}, u32[]{:S(2)}, u32[]{:S(2)}) collective-permute-start(bf16[384,2560]{1,0:T(8,128)(2,1)S(1)} %collective-permute-done.3), channel_id=1, source_target_pairs={{0,4},{4,0},{8,12},{12,8},{16,20},{20,16},{24,28},{28,24},{1,5},{5... | collective-permute-start | bytes 5898248 | tf_op jit(solution)/shard_map/ppermute | solution.py:38
  224.0 57.3 %collective-permute-start.9 = (bf16[384,2560]{1,0:T(8,128)(2,1)S(1)}, bf16[384,2560]{1,0:T(8,128)(2,1)S(1)}, u32[]{:S(2)}, u32[]{:S(2)}) collective-permute-start(bf16[384,2560]{1,0:T(8,128)(2,1)S(1)} %collective-permute-done.4), channel_id=1, source_target_pairs={{0,4},{4,0},{8,12},{12,8},{16,20},{20,16},{24,28},{28,24},{1,5},{5... | collective-permute-start | bytes 5898248 | tf_op jit(solution)/shard_map/ppermute | solution.py:38
  226.3 119.1 %collective-permute-start.28 = (bf16[256,3072]{1,0:T(8,128)(2,1)}, bf16[256,3072]{1,0:T(8,128)(2,1)}, u32[]{:S(2)}, u32[]{:S(2)}) collective-permute-start(bf16[256,3072]{1,0:T(8,128)(2,1)} %get-tuple-element.87), channel_id=1, source_target_pairs={{0,4},{4,0},{8,12},{12,8},{16,20},{20,16},{24,28},{28,24},{1,5},{5... | collective-permute-start | bytes 4718600 | tf_op jit(solution)/shard_map/ppermute | solution.py:38
  284.5 49.8 %collective-permute-start.27 = (bf16[128,3072]{1,0:T(8,128)(2,1)}, bf16[128,3072]{1,0:T(8,128)(2,1)}, u32[]{:S(2)}, u32[]{:S(2)}) collective-permute-start(bf16[128,3072]{1,0:T(8,128)(2,1)} %slice.464), channel_id=1, source_target_pairs={{0,8},{4,12},{8,0},{12,4},{16,24},{20,28},{24,16},{28,20},{1,9},{5... | collective-permute-start | bytes 2359304 | tf_op jit(solution)/shard_map/ppermute | solution.py:26
  287.0 47.3 %collective-permute-start.26 = (bf16[128,3072]{1,0:T(8,128)(2,1)}, bf16[128,3072]{1,0:T(8,128)(2,1)}, u32[]{:S(2)}, u32[]{:S(2)}) collective-permute-start(bf16[128,3072]{1,0:T(8,128)(2,1)} %slice.463), channel_id=1, source_target_pairs={{0,16},{4,20},{8,24},{12,28},{16,0},{20,4},{24,8},{28,12},{1,17},{... | collective-permute-start | bytes 2359304 | tf_op jit(solution)/shard_map/ppermute | solution.py:26
  334.3 39.6 %collective-permute-start.32 = (bf16[128,3072]{1,0:T(8,128)(2,1)}, bf16[128,3072]{1,0:T(8,128)(2,1)}, u32[]{:S(2)}, u32[]{:S(2)}) collective-permute-start(bf16[128,3072]{1,0:T(8,128)(2,1)} %collective-permute-done.27), channel_id=1, source_target_pairs={{0,4},{4,0},{8,12},{12,8},{16,20},{20,16},{24,28},{28,24},{1,5},{5... | collective-permute-start | bytes 2359304 | tf_op jit(solution)/shard_map/ppermute | solution.py:38
  490.8 394.0 %reduce-scatter.7.cloned.1.call-start = ((), (), s32[]{:S(2)}) async-start(), calls=%async_computation.8 | async-start | bytes 18874368 | tf_op jit(solution)/shard_map/reduce_scatter | solution.py:530
  570.2 616.3 %reduce-scatter.9.cloned.1.call-start = ((), (), s32[]{:S(2)}) async-start(), calls=%async_computation.9 | async-start | bytes 18874368 | tf_op jit(solution)/shard_map/reduce_scatter | solution.py:530
  679.4 511.3 %reduce-scatter.11.cloned.1.call-start = ((), (), s32[]{:S(2)}) async-start(), calls=%async_computation.10 | async-start | bytes 18874368 | tf_op jit(solution)/shard_map/reduce_scatter | solution.py:530
  767.4 107.1 %collective-permute-start.61 = (bf16[1024,3072]{1,0:T(8,128)(2,1)}, bf16[1024,3072]{1,0:T(8,128)(2,1)}, u32[]{:S(2)}, u32[]{:S(2)}) collective-permute-start(bf16[1024,3072]{1,0:T(8,128)(2,1)} %convolution_convert_fusion.6), channel_id=1, source_target_pairs={{0,4},{4,0},{8,12},{12,8},{16,20},{20,16},{24,28},{28,24},{1,5},{5... | collective-permute-start | bytes 18874376 | tf_op jit(solution)/shard_map/ppermute | solution.py:38
  791.7 45.1 %collective-permute-start.42 = (bf16[292,2048]{1,0:T(8,128)(2,1)S(1)}, bf16[292,2048]{1,0:T(8,128)(2,1)S(1)}, u32[]{:S(2)}, u32[]{:S(2)}) collective-permute-start(bf16[292,2048]{1,0:T(8,128)(2,1)S(1)} %pad_maximum_fusion.11), channel_id=1, source_target_pairs={{0,3},{1,0},{2,1},{3,2},{4,7},{5,4},{6,5},{7,6},{8,11},{9,8},{10,9... | collective-permute-start | bytes 3588104 | tf_op jit(solution)/shard_map/ppermute | solution.py:49
  881.3 60.1 %collective-permute-start.62 = (bf16[256,3072]{1,0:T(8,128)(2,1)}, bf16[256,3072]{1,0:T(8,128)(2,1)}, u32[]{:S(2)}, u32[]{:S(2)}) collective-permute-start(bf16[256,3072]{1,0:T(8,128)(2,1)} %get-tuple-element.253), channel_id=1, source_target_pairs={{0,8},{4,12},{8,0},{12,4},{16,24},{20,28},{24,16},{28,20},{1,9},{5... | collective-permute-start | bytes 4718600 | tf_op jit(solution)/shard_map/ppermute | solution.py:117
  882.8 114.4 %collective-permute-start.64 = (bf16[256,3072]{1,0:T(8,128)(2,1)}, bf16[256,3072]{1,0:T(8,128)(2,1)}, u32[]{:S(2)}, u32[]{:S(2)}) collective-permute-start(bf16[256,3072]{1,0:T(8,128)(2,1)} %get-tuple-element.254), channel_id=1, source_target_pairs={{0,24},{4,28},{8,16},{12,20},{16,8},{20,12},{24,0},{28,4},{1,25},{... | collective-permute-start | bytes 4718600 | tf_op jit(solution)/shard_map/ppermute | solution.py:117
  883.5 113.6 %collective-permute-start.63 = (bf16[256,3072]{1,0:T(8,128)(2,1)}, bf16[256,3072]{1,0:T(8,128)(2,1)}, u32[]{:S(2)}, u32[]{:S(2)}) collective-permute-start(bf16[256,3072]{1,0:T(8,128)(2,1)} %get-tuple-element.255), channel_id=1, source_target_pairs={{0,16},{4,20},{8,24},{12,28},{16,0},{20,4},{24,8},{28,12},{1,17},{... | collective-permute-start | bytes 4718600 | tf_op jit(solution)/shard_map/ppermute | solution.py:117
  892.6 168.5 %collective-permute-start.54 = (bf16[1536,2560]{1,0:T(8,128)(2,1)}, bf16[1536,2560]{1,0:T(8,128)(2,1)}, u32[]{:S(2)}, u32[]{:S(2)}) collective-permute-start(bf16[1536,2560]{1,0:T(8,128)(2,1)} %convolution_convert_fusion.4), channel_id=1, source_target_pairs={{0,4},{4,0},{8,12},{12,8},{16,20},{20,16},{24,28},{28,24},{1,5},{5... | collective-permute-start | bytes 23592968 | tf_op jit(solution)/shard_map/ppermute | solution.py:38
  1066.3 46.0 %collective-permute-start.55 = (bf16[384,2560]{1,0:T(8,128)(2,1)}, bf16[384,2560]{1,0:T(8,128)(2,1)S(1)}, u32[]{:S(2)}, u32[]{:S(2)}) collective-permute-start(bf16[384,2560]{1,0:T(8,128)(2,1)} %get-tuple-element.250), channel_id=1, source_target_pairs={{0,8},{4,12},{8,0},{12,4},{16,24},{20,28},{24,16},{28,20},{1,9},{5... | collective-permute-start | bytes 5898248 | tf_op jit(solution)/shard_map/ppermute | solution.py:117
  1067.0 85.1 %collective-permute-start.57 = (bf16[384,2560]{1,0:T(8,128)(2,1)}, bf16[384,2560]{1,0:T(8,128)(2,1)}, u32[]{:S(2)}, u32[]{:S(2)}) collective-permute-start(bf16[384,2560]{1,0:T(8,128)(2,1)} %get-tuple-element.251), channel_id=1, source_target_pairs={{0,24},{4,28},{8,16},{12,20},{16,8},{20,12},{24,0},{28,4},{1,25},{... | collective-permute-start | bytes 5898248 | tf_op jit(solution)/shard_map/ppermute | solution.py:117
  1068.3 85.2 %collective-permute-start.56 = (bf16[384,2560]{1,0:T(8,128)(2,1)}, bf16[384,2560]{1,0:T(8,128)(2,1)}, u32[]{:S(2)}, u32[]{:S(2)}) collective-permute-start(bf16[384,2560]{1,0:T(8,128)(2,1)} %get-tuple-element.252), channel_id=1, source_target_pairs={{0,16},{4,20},{8,24},{12,28},{16,0},{20,4},{24,8},{28,12},{1,17},{... | collective-permute-start | bytes 5898248 | tf_op jit(solution)/shard_map/ppermute | solution.py:117
  1076.4 105.7 %collective-permute-start.53 = (f32[1,1216]{1,0:T(1,128)S(1)}, f32[1,1216]{1,0:T(1,128)S(1)}, u32[]{:S(2)}, u32[]{:S(2)}) collective-permute-start(f32[1,1216]{1,0:T(1,128)S(1)} %fusion.77), channel_id=1, source_target_pairs={{0,3},{1,0},{2,1},{3,2},{4,7},{5,4},{6,5},{7,6},{8,11},{9,8},{10,9... | collective-permute-start | bytes 14600 | tf_op jit(solution)/shard_map/ppermute | solution.py:49
  (172 other events, 2494.6 us)
Sparse Core Ops, SparseCore 0:
  11.3 74.8 all-gather.6
  88.0 156.2 all-gather.4
  246.2 107.3 all-gather.8
  355.3 88.6 all-gather.10
  490.9 89.6 reduce-scatter.12
  584.1 115.9 reduce-scatter.6
  703.6 115.9 reduce-scatter.8
  823.2 168.3 reduce-scatter.10

commit v3 on v2

--- a/solution.py
+++ b/solution.py
@@ -100,30 +100,39 @@
     return own + [hop(piece, 1) for piece in own]
 
 
-def scatter_rows(own, other, layout):
+def chip_sums(own, other):
+    chips = lax.axis_size("dp") // 2
+    total = own.astype(F32) + hop(other, 1).astype(F32)
+    return total.reshape(chips, -1, own.shape[1])
+
+
+def send_blocks(blocks):
     size = lax.axis_size("dp")
+    return [
+        lax.ppermute(blocks[c].astype(BF16), "dp", [(d, d ^ (2 * c)) for d in range(size)])
+        for c in range(1, size // 2)
+    ]
+
+
+def add_up(first, arrived):
+    total = first
+    for each in arrived:
+        total = total + each.astype(F32)
+    return total
+
+
+def member_parts(values, layout):
     groups = lax.axis_size("mp")
-    chips = size // 2
-    rows = own.shape[0] // chips
-    other = hop(other, 1)
-
-    def block(c):
-        cut = slice(c * rows, (c + 1) * rows)
-        return own[cut].astype(F32) + other[cut].astype(F32)
-
-    total = block(0)
-    for c in range(1, chips):
-        pairs = [(d, d ^ (2 * c)) for d in range(size)]
-        total = total + lax.ppermute(block(c).astype(BF16), "dp", pairs).astype(F32)
+    axis = values.ndim - 2
     parts = []
     for r in range(groups):
         which = (lax.axis_index("mp") - r) % groups
         cuts, start = [], 0
         for part in layout:
-            cuts.append(lax.dynamic_slice_in_dim(total, start + which * part, part, 0))
+            cuts.append(lax.dynamic_slice_in_dim(values, start + which * part, part, axis))
             start += groups * part
-        parts.append(jnp.concatenate(cuts, axis=0))
-    return ring_scatter(parts)
+        parts.append(jnp.concatenate(cuts, axis=axis))
+    return parts
 
 
 def _permute_blocks(inverse, order, *refs):
@@ -173,17 +182,6 @@
         joint[rows:, start + narrow[0] : start + sum(narrow)] = act[:, there]
 
 
-def _unspread(count, order, joint, pre, act):
-    rows = pre.shape[0]
-    narrow = [value.shape[1] // count for value in (pre, act)]
-    for g in range(count):
-        start = g * sum(narrow)
-        there = pl.ds(pl.multiple_of(order[g] * narrow[0], narrow[0]), narrow[0])
-        pre[:, there] = joint[:rows, start : start + narrow[0]]
-        there = pl.ds(pl.multiple_of(order[g] * narrow[1], narrow[1]), narrow[1])
-        act[:, there] = joint[rows:, start + narrow[0] : start + sum(narrow)]
-
-
 def block_call(body, order, arrays, shapes):
     return pl.pallas_call(
         functools.partial(body, order.shape[0]),
@@ -206,21 +204,6 @@
         return (upper + lower).reshape(rows + lines, -1)
     shape = jax.ShapeDtypeStruct((rows + lines, pre.shape[1] + act.shape[1]), pre.dtype)
     return block_call(_spread, order, [pre, act], [shape])[0]
-
-
-def unspread(joint, rows, wide, thin, order):
-    count = order.shape[0]
-    lines = joint.shape[0] - rows
-    if wide // count % 128 or thin // count % 128:
-        blocks = joint.reshape(joint.shape[0], count, -1)
-        upper = blocks[:rows, :, : wide // count].reshape(rows, wide)
-        lower = blocks[rows:, :, wide // count :].reshape(lines, thin)
-        return permute_columns([upper, lower], order, True)
-    shapes = [
-        jax.ShapeDtypeStruct((rows, wide), joint.dtype),
-        jax.ShapeDtypeStruct((lines, thin), joint.dtype),
-    ]
-    return block_call(_unspread, order, [joint], shapes)
 
 
 def inverse_rms(values):
@@ -387,31 +370,21 @@
         ],
         axis=0,
     )
-    out_own = jnp.concatenate([pre_output, act_output], axis=1)
-
+    qkv_full = lax.all_gather(qkv_own, ("dp", "mp"), axis=0, tiled=True)
+    act_stack = jnp.concatenate([act_gate, act_up, act_down.T], axis=0)
     def in_place(pieces):
         size = pieces[0].shape[0]
         twice = jnp.concatenate(pieces[::-1] * 2, axis=0)
         return lax.dynamic_slice_in_dim(twice, (groups - 1 - member) * size, groups * size, 0)
 
-    qkv_ring = ring_gather(qkv_own)
-    out_ring = ring_gather(out_own)
-    qkv_block = jnp.concatenate(
-        [
-            in_place([piece[:pre_part] for piece in qkv_ring]),
-            in_place([piece[pre_part:] for piece in qkv_ring]),
-        ],
-        axis=0,
-    )
-    pre_block = groups * pre_part
+    out_ring = ring_gather(jnp.concatenate([pre_output, act_output], axis=1))
     out_block = in_place(out_ring)
-    qkv_full = jnp.concatenate(dp_gather(qkv_block), axis=0)
+    qkv_full, act_stack, out_block = lax.optimization_barrier((qkv_full, act_stack, out_block))
     out_full = jnp.concatenate(dp_gather(out_block), axis=0)
-    gate_full = lax.all_gather(pre_gate, "dp", axis=0, tiled=True)
-    down_full = lax.all_gather(pre_down, "dp", axis=1, tiled=True)
-    act_stack = jnp.concatenate([act_gate, act_up, act_down.T], axis=0)
+    qkv_full = qkv_full.reshape(ways * groups, -1, qkv_own.shape[1])
+    pre_qkv = qkv_full[:, :pre_part].reshape(width, -1)
+    act_qkv = qkv_full[:, pre_part:].reshape(act_width, -1)
     act_flat_w = lax.all_gather(act_stack, "dp", axis=0, tiled=True)
-    up_full = lax.all_gather(after(pre_up, act_flat_w), "dp", axis=0, tiled=True)
     act_all = act_flat_w.reshape(ways, 3, -1, act_gate.shape[1])
     act_gate_full, act_up_full, act_down_full = (
         act_all[:, n].reshape(act_width, -1) for n in range(3)
@@ -435,10 +408,6 @@
     def ring_stack(value):
         return jnp.concatenate(ring_gather(value), axis=0)
 
-    cot_all = ring_stack(pad(cot_flat))
-    act_cot_all = ring_stack(act_final_back.astype(BF16))
-    hidden_back = mm_nt(cot_all, down_full).astype(BF16)
-
     local_pos = jnp.concatenate(
         [
             member * pre_rows + jnp.arange(pre_rows),
@@ -488,22 +457,36 @@
             axis=0,
         )
 
-    normed = spread(
-        *stack(
-            rms_norm(pre_x, pre_attn_gain).astype(BF16),
-            rms_norm(act_x, act_attn_gain).astype(BF16),
-        ),
-        order,
-    )
-    keyval_raw = to_items(mm(normed, qkv_full[:, query_width:]))
+    pre_normed, act_normed = stack(
+        rms_norm(pre_x, pre_attn_gain).astype(BF16), rms_norm(act_x, act_attn_gain).astype(BF16)
+    )
+    normed = spread(pre_normed, act_normed, order)
+
+    def project(columns):
+        return to_items(
+            jnp.concatenate(
+                [mm(pre_normed, pre_qkv[:, columns]), mm(act_normed, act_qkv[:, columns])], axis=0
+            )
+        )
+
+    keyval_raw = project(slice(query_width, None))
     keyval_rows = jnp.concatenate(
         [rotate(keyval_raw[..., :head_dim], cosine_tab, sine_tab), keyval_raw[..., head_dim:]],
         axis=-1,
     ).astype(BF16)
+    keyval_rows, gate_own, up_own, down_own = lax.optimization_barrier(
+        (keyval_rows, pre_gate, pre_up, pre_down)
+    )
+    down_full = lax.all_gather(down_own, "dp", axis=1, tiled=True)
+    gate_full = lax.all_gather(gate_own, "dp", axis=0, tiled=True)
+    up_full = lax.all_gather(up_own, "dp", axis=0, tiled=True)
     all_keyval = jnp.concatenate(ring_gather(keyval_rows), axis=1)
+    cot_all = ring_stack(pad(cot_flat))
+    act_cot_all = ring_stack(act_final_back.astype(BF16))
+    hidden_back = mm_nt(cot_all, down_full).astype(BF16)
     key_rows = all_keyval[..., :head_dim]
     value_rows = all_keyval[..., head_dim:]
-    query_raw = to_items(mm(normed, qkv_full[:, :query_width]))
+    query_raw = project(slice(0, query_width))
     query_rows = rotate(
         query_raw.reshape(items, local_len, heads, head_dim),
         cosine_tab[:, None, :],
@@ -544,6 +527,9 @@
     act_second_part = split(mm_nt(act_gate_back, act_gate_full) + mm_nt(act_up_back, act_up_full))
     act_sum_part = split(mm_nt(act_hidden, act_down_full))
 
+    act_stacked = jnp.concatenate(
+        [term.reshape(ways, -1, act_gate.shape[1]) for term in act_terms], axis=1
+    ).reshape(-1, act_gate.shape[1])
     pre_second = pad(rms_norm(pre_mid, pre_mlp_gain).astype(BF16))
     second_pieces = [pre_second]
     for r in range(1, groups):
@@ -551,11 +537,8 @@
         if r == 1:
             piece, hidden_back = lax.optimization_barrier((piece, hidden_back))
         if r == groups - 1:
-            piece, act_terms = lax.optimization_barrier((piece, act_terms))
+            piece, act_stacked = lax.optimization_barrier((piece, act_stacked))
         second_pieces.append(piece)
-    act_stacked = jnp.concatenate(
-        [term.reshape(ways, -1, act_gate.shape[1]) for term in act_terms], axis=1
-    ).reshape(-1, act_gate.shape[1])
     grad_act = scatter_sum(act_stacked, 0)
     grad_act = grad_act.astype(F32).reshape(3, -1, act_gate.shape[1])
     grad_act_gate, grad_act_up, grad_act_down = grad_act[0], grad_act[1], grad_act[2].T
@@ -577,15 +560,13 @@
 
     act_lines = act_count * act_width // width
 
-    def pack(pre_part_rows, act_part_rows):
-        return jnp.concatenate([pre_part_rows, act_part_rows.reshape(act_lines, width)], axis=0)
-
-    def unpack(packed):
-        return packed[:count], packed[count:].reshape(act_count, act_width)
+    def lines(value):
+        return value.reshape(act_lines, width)
 
     def second_part(r):
         rows = sooner if r < groups // 2 else later
-        return pack(rows[r % (groups // 2) * padded :][:count], act_second_part[r])
+        rows = rows[r % (groups // 2) * padded :][:count]
+        return jnp.concatenate([rows, lines(act_second_part[r]), lines(act_sum_part[r])], axis=0)
 
     up_term = down_term = None
     total = second_part(groups - 1)
@@ -602,7 +583,9 @@
         total = moved.astype(F32) + second_part(r)
     grad_pre_up = scatter_sum(up_term, 0)
     grad_pre_down = scatter_sum(down_term, 1)
-    pre_second_back, act_second_back = unpack(total)
+    pre_second_back = total[:count]
+    act_second_back = total[count : count + act_lines].reshape(act_count, act_width)
+    act_sums = total[count + act_lines :].reshape(act_count, act_width)
 
     pre_mid_part, grad_pre_mlp_gain = rms_back(pre_mid, pre_mlp_gain, pre_second_back)
     act_mid_part, grad_act_mlp_gain = rms_back(act_mid, act_mlp_gain, act_second_back)
@@ -619,11 +602,12 @@
         permute_columns([mm_nt(back_joint, out_full).astype(BF16)], order, True)[0]
     ).reshape(items, local_len, heads, head_dim)
     out_half = query_width // 2
-    grad_out = scatter_rows(
+    out_sums = chip_sums(
         mm_tn(att_joint[:, :out_half], back_joint).astype(BF16),
         mm_tn(att_joint[:, out_half:], back_joint).astype(BF16),
-        (out_part,),
-    )
+    )
+    out_sums = ring_scatter(member_parts(out_sums, (out_part,)))
+    grad_out = add_up(out_sums[0], send_blocks(out_sums))
     probs_back = jnp.einsum(
         "iqhd,ikd->ihqk", attended_back, value_rows, preferred_element_type=F32
     )
@@ -640,11 +624,6 @@
         jnp.einsum("ihqk,ikd->iqhd", scores_back, key_rows, preferred_element_type=F32) * scale
     )
     keyval_back = jnp.concatenate([key_back, value_back], axis=-1).astype(BF16)
-    keyval_back, pre_hidden = lax.optimization_barrier((keyval_back, pre_hidden))
-    pre_sum_part = split(mm(pre_hidden, down_full))
-    pre_sums, act_sums = unpack(
-        ring_scatter([pack(each[:count], rest) for each, rest in zip(pre_sum_part, act_sum_part)])
-    )
     own_kv_back = ring_scatter(
         [keyval_back[:, r * local_len : (r + 1) * local_len] for r in range(groups)]
     )
@@ -657,21 +636,16 @@
     back_rows = from_items(jnp.concatenate([query_low, keyval_low], axis=-1))
     back_rows, grad_pre_gate = lax.optimization_barrier((back_rows, grad_pre_gate))
     qkv_half = normed.shape[1] // 2
-    grad_qkv = scatter_rows(
-        mm_tn(normed[:, :qkv_half], back_rows).astype(BF16),
-        mm_tn(normed[:, qkv_half:], back_rows).astype(BF16),
-        (pre_part, act_part),
-    )
-
-    prefix_out = (pre_mid + pre_sums).astype(BF16).reshape(prefix_tokens.shape)
+    qkv_own_part = mm_tn(normed[:, :qkv_half], back_rows).astype(BF16)
+    qkv_other_part = mm_tn(normed[:, qkv_half:], back_rows).astype(BF16)
+    qkv_sums = chip_sums(qkv_own_part, qkv_other_part).astype(BF16)
+    qkv_sums, pre_hidden = lax.optimization_barrier((qkv_sums, pre_hidden))
+    arrived = send_blocks(qkv_sums)
     act_final_low = (act_mid + act_sums).astype(BF16)
     action_pred = mm(act_final_low, action_head).reshape(pred_cot.shape) * live_mask
     grad_head = mm_tn(act_final_low, pred_back)
-
-    pre_normed_back, act_normed_back = unspread(
-        mm_nt(back_rows, qkv_full), padded, width, act_width, order
-    )
-    pre_normed_back, act_normed_back = pre_normed_back[:count], act_normed_back[:act_count]
+    pre_normed_back = mm_nt(back_rows[:padded], pre_qkv)[:count]
+    act_normed_back = mm_nt(back_rows[padded:], act_qkv)[:act_count]
     pre_x_part, grad_pre_attn_gain = rms_back(pre_x, pre_attn_gain, pre_normed_back)
     act_x_part, grad_act_attn_gain = rms_back(act_x, act_attn_gain, act_normed_back)
     prefix_grad = (pre_mid_grad + pre_x_part).reshape(prefix_tokens.shape)
@@ -691,6 +665,22 @@
         ],
         axis=1,
     )
+    arrived, small = lax.optimization_barrier((arrived, small))
+
+    pre_sum_part = split(mm(pre_hidden, down_full))
+    sum_parts = [each[:count] for each in pre_sum_part]
+    total = sum_parts[-1]
+    for r in range(groups - 2, -1, -1):
+        total = total.astype(BF16)
+        if r == 0:
+            total, arrived = lax.optimization_barrier((total, arrived))
+        total = ring(total, -1, LOOSE).astype(F32) + sum_parts[r]
+    pre_sums = total
+    prefix_out = (pre_mid + pre_sums).astype(BF16).reshape(prefix_tokens.shape)
+    grad_qkv = ring_scatter(
+        member_parts(add_up(qkv_sums[0].astype(F32), arrived), (pre_part, act_part))
+    )
+
     bit = 1
     while bit < ways:
         small = small + hop(small, bit)

time: 1210 us -> 1280 us (1.058)
  local copies, waits for them, and re-layouts: 156 us -> 176 us
  starting transfers between devices: 65.5 us -> 82.5 us
  waiting for transfers between devices: 527 us -> 544 us
  matrix products: 291 us -> 307 us
    all_gather x3 -> x4, waiting for transfers between devices: 0.06 us -> 164 us  [the longest x1 91.6 us: shards(): up_full = lax.all_gather(up_own, 'dp', axis=0, tiled=True)]
    ppermute x28 -> x21, waiting for transfers between devices: 273 us -> 142 us  [send(): result = lax.ppermute(value, axis, pairs)]
    ppermute x6, waiting for transfers between devices: 170 us -> 77.9 us  [send_blocks(): lax.ppermute(blocks[c].astype(BF16), 'dp', [(d, d ^ 2 * c) for d in range...]
    ppermute x21, waiting for transfers between devices: 82 us -> 159 us  [ring(): return lax.ppermute(value, 'mp', pairs)]
    unnamed x315 -> x283, local copies, waits for them, and re-layouts: 92 us -> 68.5 us
    ppermute x21, starting transfers between devices: 35.4 us -> 54.5 us  [ring(): return lax.ppermute(value, 'mp', pairs)]
    reshape x10 -> x11, local copies, waits for them, and re-layouts: 2.24 us -> 16.9 us  [the longest x1 16.7 us: shards(): act_stacked = jnp.concatenate([term.reshape(ways, -1, act_gate.shape[1])...]
    slice x9 -> x8, local copies, waits for them, and re-layouts: 10.8 us -> 24.5 us  [the longest x1 8.95 us: shards(): pre_qkv = qkv_full[:, :pre_part].reshape(width, -1)]
  transfers between devices with their start and end apart: 76 -> 65, of which waited for: 33 -> 32; matrix products, arithmetic and copies ran while one was open for 43% -> 41% of each run, Pallas kernels for 5% -> 0%
where the time goes in v3:
time: 1280 us; the launch traced here: 1270 us
  waiting for transfers between devices  544 us (42%)
  matrix products  307 us (24%)
  local copies, waits for them, and re-layouts  176 us (14%)
  other arithmetic  96.8 us (8%)
  starting transfers between devices  82.5 us (6%)
  Pallas kernels  52.3 us (4%)
  between operations  16.3 us (1%)
    ppermute x21, waiting for transfers between devices, ring(): return lax.ppermute(value, 'mp', pairs)  159 us
    ppermute x21, waiting for transfers between devices, send(): result = lax.ppermute(value, axis, pairs)  142 us
    dot_general x12, matrix products, mm_nt(): lax.dot_general(left, right, (((1,), (1,)), ((), ())), preferred_element_...  130 us
    dot_general x11, matrix products, mm_tn(): lax.dot_general(left, right, (((0,), (0,)), ((), ())), preferred_element_...  117 us
    all_gather x1, waiting for transfers between devices, shards(): up_full = lax.all_gather(up_own, 'dp', axis=0, tiled=True)  91.6 us
    ppermute x6, waiting for transfers between devices, send_blocks(): lax.ppermute(blocks[c].astype(BF16), 'dp', [(d, d ^ 2 * c) for d in range...  77.9 us
    all_gather x1, waiting for transfers between devices, shards(): qkv_full = lax.all_gather(qkv_own, ('dp', 'mp'), axis=0, tiled=True)  69.2 us
    unnamed x283, local copies, waits for them, and re-layouts  68.5 us
  transfers between devices with their start and end apart: 65, of which 32 were waited for; matrix products, arithmetic and copies ran while one was open for 41% of the time, Pallas kernels for 0%

profile of v3, /device:TPU:0, one launch (start us, length us, event | category | flops | bytes accessed | tf_op | source)
XLA Modules:
  0.0 1274.9 jit_solution(4735940284925972474)
XLA Ops:
  13.4 11.1 collective-permute-done
  24.6 21.5 %collective-permute-done.1 = bf16[64,3072]{1,0:T(8,128)(2,1)S(1)} collective-permute-done((bf16[64,3072]{1,0:T(8,128)(2,1)S(1)}, bf16[64,3072]{1,0:T(8,128)(2,1)S(1)}, u32[]{:S(2)}, u32[]{:S(2)}) %collective-permute-start.1) | collective-permute-done | bytes 393248 | tf_op jit(solution)/shard_map/ppermute | solution.py:26
  48.7 13.1 %collective-permute-done.2 = bf16[64,3072]{1,0:T(8,128)(2,1)S(1)} collective-permute-done((bf16[64,3072]{1,0:T(8,128)(2,1)S(1)}, bf16[64,3072]{1,0:T(8,128)(2,1)S(1)}, u32[]{:S(2)}, u32[]{:S(2)}) %collective-permute-start.2) | collective-permute-done | bytes 393248 | tf_op jit(solution)/shard_map/ppermute | solution.py:26
  63.4 69.2 %all-gather.6.cloned.1.call-done = bf16[3072,2560]{1,0:T(8,128)(2,1)} async-done(((bf16[96,2560]{1,0:T(8,128)(2,1)}), bf16[3072,2560]{1,0:T(8,128)(2,1)}) %all-gather.6.cloned.1.call-update) | async-done | bytes 15728656 | tf_op jit(solution)/shard_map/all_gather | solution.py:373
  200.5 11.9 collective-permute-done.5
  217.0 19.9 %collective-permute-done.7 = bf16[256,3072]{1,0:T(8,128)(2,1)S(1)} collective-permute-done((bf16[256,3072]{1,0:T(8,128)(2,1)}, bf16[256,3072]{1,0:T(8,128)(2,1)S(1)}, u32[]{:S(2)}, u32[]{:S(2)}) %collective-permute-start.7) | collective-permute-done | bytes 1572896 | tf_op jit(solution)/shard_map/ppermute | solution.py:26
  251.7 20.5 %collective-permute-done.9 = bf16[128,3072]{1,0:T(8,128)(2,1)} collective-permute-done((bf16[128,3072]{1,0:T(8,128)(2,1)}, bf16[128,3072]{1,0:T(8,128)(2,1)}, u32[]{:S(2)}, u32[]{:S(2)}) %collective-permute-start.9) | collective-permute-done | bytes 786464 | tf_op jit(solution)/shard_map/ppermute | solution.py:26
  315.3 12.1 collective-permute-done.24
  335.1 10.7 fusion.117
  345.8 25.7 %convolution_convert_fusion.3.refs_4_ = bf16[1152,4096]{1,0:T(8,128)(2,1)} fusion(bf16[4096,2048]{1,0:T(8,128)(2,1)} %all-gather.8.cloned.1.call-done, bf16[288,2048]{1,0:T(8,128)(2,1)} %copy-done.114, bf16[288,2048]{1,0:T(8,128)(2,1)} %copy-done.112, bf16[288,2048]{1,0:T(8,128)(2,1)} %collective-permute-done.15, bf16[288,2048]{1,0:T(8,128)(2,1)} %pad.42), kind=kOutput, calls=%fused_computation.5 | convolution fusion | flops 19350945792 | bytes 30932992 | tf_op jit(solution)/shard_map/dot_general | solution.py:250
  381.3 16.9 %collective-permute-done.22.refs_2_ = bf16[288,2048]{1,0:T(8,128)(2,1)} collective-permute-done((bf16[288,2048]{1,0:T(8,128)(2,1)}, bf16[288,2048]{1,0:T(8,128)(2,1)}, u32[]{:S(2)}, u32[]{:S(2)}) %collective-permute-start.22) | collective-permute-done | bytes 1179680 | tf_op jit(solution)/shard_map/ppermute | solution.py:26
  401.7 12.2 pad_maximum_fusion
  413.9 16.7 %copy.147 = bf16[3072,2048]{0,1:T(8,128)(2,1)} copy(bf16[3072,2048]{1,0:T(8,128)(2,1)} %bitcast.159) | data formatting | bytes 25165824 | tf_op jit(solution)/shard_map/reshape | solution.py:532
  433.9 91.6 %all-gather.14.cloned.1.call-done.refs_6_ = bf16[2048,4096]{1,0:T(8,128)(2,1)} async-done(((bf16[256,4096]{1,0:T(8,128)(2,1)}), bf16[2048,4096]{1,0:T(8,128)(2,1)}) %all-gather.14.cloned.1.call-update) | async-done | bytes 16777232 | tf_op jit(solution)/shard_map/all_gather | solution.py:482
  525.5 50.0 %shard_map.393 = (bf16[1152,4096]{1,0:T(8,128)(2,1)}, bf16[1152,4096]{1,0:T(8,128)(2,1)}, bf16[1152,4096]{1,0:T(8,128)(2,1)}, bf16[1152,2048]{1,0:T(8,128)(2,1)}) custom-call(bf16[288,2048]{1,0:T(8,128)(2,1)} %copy-done.58, bf16[288,2048]{1,0:T(8,128)(2,1)} %collective-permute-done.20.refs_1_, bf16[288,2048]{1,0:T(8,128)(2,1)} %collective-permute-done.22.refs_2_, ...), custom_call_target="tpu_custom_call" | custom-call | flops 38654705664 | bytes 80740352 | tf_op jit(solution)/shard_map/pallas_call | solution.py:305
  575.5 28.0 %convolution_convert_fusion.2 = bf16[2048,4096]{1,0:T(8,128)(2,1)} fusion(bf16[1152,2048]{1,0:T(8,128)(2,1)} %get-tuple-element.100, bf16[1152,4096]{1,0:T(8,128)(2,1)} %get-tuple-element.105), kind=kOutput, calls=%fused_computation.4 | convolution fusion | flops 19335741440 | bytes 30932992 | tf_op jit(solution)/shard_map/dot_general | solution.py:254
  607.2 17.7 %copy.148 = bf16[3072,2048]{1,0:T(8,128)(2,1)} copy(bf16[3072,2048]{0,1:T(8,128)(2,1)} %copy.147) | data formatting | bytes 25165824
  634.8 16.6 %fusion.11 = f32[576,2048]{1,0:T(8,128)} fusion(bf16[2048,4096]{1,0:T(8,128)(2,1)} %all-gather.14.cloned.1.call-done.refs_6_, bf16[1152,4096]{1,0:T(8,128)(2,1)} %get-tuple-element.108), kind=kOutput, calls=%fused_computation.26 | convolution fusion | flops 9663676416 | bytes 26214400 | tf_op jit(solution)/shard_map/dot_general | solution.py:250
  651.4 17.5 %fusion.21 = f32[576,2048]{1,0:T(8,128)} fusion(f32[576,2048]{1,0:T(8,128)} %fusion.11, bf16[2048,4096]{1,0:T(8,128)(2,1)} %all-gather.12.cloned.1.call-done.refs_5_, bf16[1152,4096]{1,0:T(8,128)(2,1)} %get-tuple-element.105), kind=kOutput, calls=%fused_computation.42 | convolution fusion | flops 9664856064 | bytes 30932992 | tf_op jit(solution)/shard_map/dot_general | solution.py:250
  674.1 16.9 %fusion.7 = f32[576,2048]{1,0:T(8,128)} fusion(bf16[2048,4096]{1,0:T(8,128)(2,1)} %all-gather.14.cloned.1.call-done.refs_6_, bf16[1152,4096]{1,0:T(8,128)(2,1)} %get-tuple-element.108), kind=kOutput, calls=%fused_computation.22 | convolution fusion | flops 9663676416 | bytes 26214400 | tf_op jit(solution)/shard_map/dot_general | solution.py:250
  691.0 17.7 %fusion.24 = f32[576,2048]{1,0:T(8,128)} fusion(f32[576,2048]{1,0:T(8,128)} %fusion.7, bf16[2048,4096]{1,0:T(8,128)(2,1)} %all-gather.12.cloned.1.call-done.refs_5_, bf16[1152,4096]{1,0:T(8,128)(2,1)} %get-tuple-element.105), kind=kOutput, calls=%fused_computation.43 | convolution fusion | flops 9664856064 | bytes 30932992 | tf_op jit(solution)/shard_map/dot_general | solution.py:250
  711.1 28.9 %convolution_convert_fusion.1 = bf16[2048,4096]{1,0:T(8,128)(2,1)} fusion(bf16[1152,2048]{1,0:T(8,128)(2,1)} %get-tuple-element.100, bf16[1152,4096]{1,0:T(8,128)(2,1)} %get-tuple-element.108), kind=kOutput, calls=%fused_computation.3 | convolution fusion | flops 19335741440 | bytes 30932992 | tf_op jit(solution)/shard_map/dot_general | solution.py:254
  748.7 27.4 %convolution_convert_fusion = bf16[4096,2048]{1,0:T(8,128)(2,1)} fusion(bf16[1152,4096]{1,0:T(8,128)(2,1)} %get-tuple-element.115, bf16[288,2048]{1,0:T(8,128)(2,1)S(1)} %copy-done.115, bf16[288,2048]{1,0:T(8,128)(2,1)S(1)} %copy-done.113, bf16[288,2048]{1,0:T(8,128)(2,1)} %collective-permute-done.15, bf16[288,2048]{1,0:T(8,128)(2,1)} %pad.42), kind=kOutput, calls=%fused_computation.2 | convolution fusion | flops 19354615808 | bytes 30932992 | tf_op jit(solution)/shard_map/dot_general | solution.py:254
  881.8 16.6 %collective-permute-done.50 = bf16[4,64,3072]{2,1,0:T(8,128)(2,1)} collective-permute-done((bf16[4,64,3072]{2,1,0:T(8,128)(2,1)}, bf16[4,64,3072]{2,1,0:T(8,128)(2,1)}, u32[]{:S(2)}, u32[]{:S(2)}) %collective-permute-start.50) | collective-permute-done | bytes 1572896 | tf_op jit(solution)/shard_map/ppermute | solution.py:49
  906.7 31.5 %collective-permute-done.51 = bf16[4,64,3072]{2,1,0:T(8,128)(2,1)} collective-permute-done((bf16[4,64,3072]{2,1,0:T(8,128)(2,1)}, bf16[4,64,3072]{2,1,0:T(8,128)(2,1)}, u32[]{:S(2)}, u32[]{:S(2)}) %collective-permute-start.51) | collective-permute-done | bytes 1572896 | tf_op jit(solution)/shard_map/ppermute | solution.py:49
  947.3 29.7 %collective-permute-done.52 = bf16[4,64,3072]{2,1,0:T(8,128)(2,1)} collective-permute-done((bf16[4,64,3072]{2,1,0:T(8,128)(2,1)}, bf16[4,64,3072]{2,1,0:T(8,128)(2,1)}, u32[]{:S(2)}, u32[]{:S(2)}) %collective-permute-start.52) | collective-permute-done | bytes 1572896 | tf_op jit(solution)/shard_map/ppermute | solution.py:49
  987.2 16.1 %collective-permute-done.53 = bf16[64,3072]{1,0:T(8,128)(2,1)} collective-permute-done((bf16[64,3072]{1,0:T(8,128)(2,1)}, bf16[64,3072]{1,0:T(8,128)(2,1)}, u32[]{:S(2)}, u32[]{:S(2)}) %collective-permute-start.53) | collective-permute-done | bytes 393248 | tf_op jit(solution)/shard_map/ppermute | solution.py:112
  1003.3 15.6 %collective-permute-done.55 = bf16[64,3072]{1,0:T(8,128)(2,1)} collective-permute-done((bf16[64,3072]{1,0:T(8,128)(2,1)S(1)}, bf16[64,3072]{1,0:T(8,128)(2,1)}, u32[]{:S(2)}, u32[]{:S(2)}) %collective-permute-start.55) | collective-permute-done | bytes 393248 | tf_op jit(solution)/shard_map/ppermute | solution.py:112
  1037.9 22.6 %fusion.128 = f32[1152,2048]{1,0:T(8,128)S(1)} fusion(bf16[1152,4096]{1,0:T(8,128)(2,1)S(1)} %bitcast.200, bf16[4096,2048]{1,0:T(8,128)(2,1)} %all-gather.8.cloned.1.call-done), kind=kOutput, calls=%fused_computation.319 | convolution fusion | flops 19327352832 | bytes 35651584 | tf_op jit(solution)/shard_map/dot_general | solution.py:246
  1115.8 10.6 collective-permute-done.38
  1126.4 35.7 %collective-permute-done.37 = bf16[384,2560]{1,0:T(8,128)(2,1)} collective-permute-done((bf16[384,2560]{1,0:T(8,128)(2,1)}, bf16[384,2560]{1,0:T(8,128)(2,1)}, u32[]{:S(2)}, u32[]{:S(2)}) %collective-permute-start.37) | collective-permute-done | bytes 1966112 | tf_op jit(solution)/shard_map/ppermute | solution.py:112
  1194.1 31.0 %collective-permute-done.44 = f32[1,1216]{1,0:T(1,128)S(1)} collective-permute-done((f32[1,1216]{1,0:T(1,128)S(1)}, f32[1,1216]{1,0:T(1,128)S(1)}, u32[]{:S(2)}, u32[]{:S(2)}) %collective-permute-start.44) | collective-permute-done | bytes 4896 | tf_op jit(solution)/shard_map/ppermute | solution.py:49
  (609 shorter events, 475.5 us)
Async XLA Ops:
  7.2 125.4 %all-gather.6.cloned.1.call-start = ((), (), s32[]{:S(2)}) async-start(), calls=%async_computation.4 | async-start | bytes 16220160 | tf_op jit(solution)/shard_map/all_gather | solution.py:373
  9.3 325.8 %all-gather.10.cloned.1.call-start = ((), (), s32[]{:S(2)}) async-start(), calls=%async_computation.6 | async-start | bytes 14155776 | tf_op jit(solution)/shard_map/all_gather | solution.py:387
  132.7 213.1 %all-gather.8.cloned.1.call-start = ((), (), s32[]{:S(2)}) async-start(), calls=%async_computation.5 | async-start | bytes 18874368 | tf_op jit(solution)/shard_map/all_gather | solution.py:480
  166.6 267.3 %all-gather.12.cloned.1.call-start = ((), (), s32[]{:S(2)}) async-start(), calls=%async_computation.7 | async-start | bytes 18874368 | tf_op jit(solution)/shard_map/all_gather | solution.py:481
  167.2 358.3 %all-gather.14.cloned.1.call-start = ((), (), s32[]{:S(2)}) async-start(), calls=%async_computation.8 | async-start | bytes 18874368 | tf_op jit(solution)/shard_map/all_gather | solution.py:482
  167.8 705.7 %reduce-scatter.7.cloned.1.call-start = ((), (), s32[]{:S(2)}) async-start(), calls=%async_computation.9 | async-start | bytes 18874368 | tf_op jit(solution)/shard_map/reduce_scatter | solution.py:513
  176.6 109.3 %collective-permute-start.10 = (bf16[256,3072]{1,0:T(8,128)(2,1)}, bf16[256,3072]{1,0:T(8,128)(2,1)}, u32[]{:S(2)}, u32[]{:S(2)}) collective-permute-start(bf16[256,3072]{1,0:T(8,128)(2,1)} %constant_dynamic-slice_fusion.20), channel_id=1, source_target_pairs={{0,4},{4,0},{8,12},{12,8},{16,20},{20,16},{24,28},{28,24},{1,5},{5... | collective-permute-start | bytes 4718600 | tf_op jit(solution)/shard_map/ppermute | solution.py:38
  176.9 60.0 %collective-permute-start.7 = (bf16[256,3072]{1,0:T(8,128)(2,1)}, bf16[256,3072]{1,0:T(8,128)(2,1)S(1)}, u32[]{:S(2)}, u32[]{:S(2)}) collective-permute-start(bf16[256,3072]{1,0:T(8,128)(2,1)} %constant_dynamic-slice_fusion.20), channel_id=1, source_target_pairs={{0,16},{4,20},{8,24},{12,28},{16,0},{20,4},{24,8},{28,12},{1,17},{... | collective-permute-start | bytes 4718600 | tf_op jit(solution)/shard_map/ppermute | solution.py:26
  178.3 66.5 %collective-permute-start.6 = (bf16[256,3072]{1,0:T(8,128)(2,1)}, bf16[256,3072]{1,0:T(8,128)(2,1)}, u32[]{:S(2)}, u32[]{:S(2)}) collective-permute-start(bf16[256,3072]{1,0:T(8,128)(2,1)} %constant_dynamic-slice_fusion.20), channel_id=1, source_target_pairs={{0,8},{4,12},{8,0},{12,4},{16,24},{20,28},{24,16},{28,20},{1,9},{5... | collective-permute-start | bytes 4718600 | tf_op jit(solution)/shard_map/ppermute | solution.py:26
  200.4 51.2 %collective-permute-start.15 = (bf16[288,2048]{1,0:T(8,128)(2,1)}, bf16[288,2048]{1,0:T(8,128)(2,1)}, u32[]{:S(2)}, u32[]{:S(2)}) collective-permute-start(bf16[288,2048]{1,0:T(8,128)(2,1)} %pad.42), channel_id=1, source_target_pairs={{0,1},{1,2},{2,3},{3,0},{4,5},{5,6},{6,7},{7,4},{8,9},{9,10},{10,1... | collective-permute-start | bytes 3538952 | tf_op jit(solution)/shard_map/ppermute | solution.py:26
  246.0 36.8 %collective-permute-start.8 = (bf16[128,3072]{1,0:T(8,128)(2,1)S(1)}, bf16[128,3072]{1,0:T(8,128)(2,1)S(1)}, u32[]{:S(2)}, u32[]{:S(2)}) collective-permute-start(bf16[128,3072]{1,0:T(8,128)(2,1)S(1)} %slice.422), channel_id=1, source_target_pairs={{0,16},{4,20},{8,24},{12,28},{16,0},{20,4},{24,8},{28,12},{1,17},{... | collective-permute-start | bytes 2359304 | tf_op jit(solution)/shard_map/ppermute | solution.py:26
  248.4 51.2 %collective-permute-start.11 = (bf16[256,3072]{1,0:T(8,128)(2,1)}, bf16[256,3072]{1,0:T(8,128)(2,1)S(1)}, u32[]{:S(2)}, u32[]{:S(2)}) collective-permute-start(bf16[256,3072]{1,0:T(8,128)(2,1)} %collective-permute-done.6), channel_id=1, source_target_pairs={{0,4},{4,0},{8,12},{12,8},{16,20},{20,16},{24,28},{28,24},{1,5},{5... | collective-permute-start | bytes 4718600 | tf_op jit(solution)/shard_map/ppermute | solution.py:38
  251.6 51.0 %collective-permute-start.12 = (bf16[256,3072]{1,0:T(8,128)(2,1)S(1)}, bf16[256,3072]{1,0:T(8,128)(2,1)S(1)}, u32[]{:S(2)}, u32[]{:S(2)}) collective-permute-start(bf16[256,3072]{1,0:T(8,128)(2,1)S(1)} %copy-done.35), channel_id=1, source_target_pairs={{0,4},{4,0},{8,12},{12,8},{16,20},{20,16},{24,28},{28,24},{1,5},{5... | collective-permute-start | bytes 4718600 | tf_op jit(solution)/shard_map/ppermute | solution.py:38
  333.8 40.4 %collective-permute-start.26 = (bf16[24,1024]{1,0:T(8,128)(2,1)S(1)}, bf16[24,1024]{1,0:T(8,128)(2,1)S(1)}, u32[]{:S(2)}, u32[]{:S(2)}) collective-permute-start(bf16[24,1024]{1,0:T(8,128)(2,1)S(1)} %collective-permute-done.25), channel_id=1, source_target_pairs={{0,1},{1,2},{2,3},{3,0},{4,5},{5,6},{6,7},{7,4},{8,9},{9,10},{10,1... | collective-permute-start | bytes 147464 | tf_op jit(solution)/shard_map/ppermute | solution.py:49
  334.8 36.7 %collective-permute-start.21 = (bf16[24,1024]{1,0:T(8,128)(2,1)S(1)}, bf16[24,1024]{1,0:T(8,128)(2,1)S(1)}, u32[]{:S(2)}, u32[]{:S(2)}) collective-permute-start(bf16[24,1024]{1,0:T(8,128)(2,1)S(1)} %collective-permute-done.19), channel_id=1, source_target_pairs={{0,1},{1,2},{2,3},{3,0},{4,5},{5,6},{6,7},{7,4},{8,9},{9,10},{10,1... | collective-permute-start | bytes 147464 | tf_op jit(solution)/shard_map/ppermute | solution.py:26
  334.8 36.6 %collective-permute-start.20 = (bf16[288,2048]{1,0:T(8,128)(2,1)S(1)}, bf16[288,2048]{1,0:T(8,128)(2,1)}, u32[]{:S(2)}, u32[]{:S(2)}) collective-permute-start(bf16[288,2048]{1,0:T(8,128)(2,1)S(1)} %pad.41.refs_0_), channel_id=1, source_target_pairs={{0,1},{1,2},{2,3},{3,0},{4,5},{5,6},{6,7},{7,4},{8,9},{9,10},{10,1... | collective-permute-start | bytes 3538952 | tf_op jit(solution)/shard_map/ppermute | solution.py:26
  603.5 418.5 %reduce-scatter.13.cloned.1.call-start = ((), (), s32[]{:S(2)}) async-start(), calls=%async_computation.12 | async-start | bytes 14155776
  624.9 545.3 %reduce-scatter.9.cloned.1.call-start = ((), (), s32[]{:S(2)}) async-start(), calls=%async_computation.10 | async-start | bytes 18874368 | tf_op jit(solution)/shard_map/reduce_scatter | solution.py:513
  670.8 38.0 %collective-permute-start.27 = (bf16[304,2048]{1,0:T(8,128)(2,1)S(1)}, bf16[304,2048]{1,0:T(8,128)(2,1)S(1)}, u32[]{:S(2)}, u32[]{:S(2)}) collective-permute-start(bf16[304,2048]{1,0:T(8,128)(2,1)S(1)} %pad_maximum_fusion.6), channel_id=1, source_target_pairs={{0,3},{1,0},{2,1},{3,2},{4,7},{5,4},{6,5},{7,6},{8,11},{9,8},{10,9... | collective-permute-start | bytes 3735560 | tf_op jit(solution)/shard_map/ppermute | solution.py:49
  740.0 434.3 %reduce-scatter.11.cloned.1.call-start = ((), (), s32[]{:S(2)}) async-start(), calls=%async_computation.11 | async-start | bytes 18874368 | tf_op jit(solution)/shard_map/reduce_scatter | solution.py:513
  792.2 57.8 %collective-permute-start.49 = (bf16[1024,3072]{1,0:T(8,128)(2,1)}, bf16[1024,3072]{1,0:T(8,128)(2,1)}, u32[]{:S(2)}, u32[]{:S(2)}) collective-permute-start(bf16[1024,3072]{1,0:T(8,128)(2,1)} %convolution_convert_fusion.6), channel_id=1, source_target_pairs={{0,4},{4,0},{8,12},{12,8},{16,20},{20,16},{24,28},{28,24},{1,5},{5... | collective-permute-start | bytes 18874376 | tf_op jit(solution)/shard_map/ppermute | solution.py:38
  861.7 36.7 %collective-permute-start.50 = (bf16[4,64,3072]{2,1,0:T(8,128)(2,1)}, bf16[4,64,3072]{2,1,0:T(8,128)(2,1)}, u32[]{:S(2)}, u32[]{:S(2)}) collective-permute-start(bf16[4,64,3072]{2,1,0:T(8,128)(2,1)} %dynamic-slice_convert_fusion), channel_id=1, source_target_pairs={{0,3},{1,0},{2,1},{3,2},{4,7},{5,4},{6,5},{7,6},{8,11},{9,8},{10,9... | collective-permute-start | bytes 4718600 | tf_op jit(solution)/shard_map/ppermute | solution.py:49
  881.8 145.9 %collective-permute-start.33 = (bf16[1536,2560]{1,0:T(8,128)(2,1)}, bf16[1536,2560]{1,0:T(8,128)(2,1)}, u32[]{:S(2)}, u32[]{:S(2)}) collective-permute-start(bf16[1536,2560]{1,0:T(8,128)(2,1)} %convolution_convert_fusion.4), channel_id=1, source_target_pairs={{0,4},{4,0},{8,12},{12,8},{16,20},{20,16},{24,28},{28,24},{1,5},{5... | collective-permute-start | bytes 23592968 | tf_op jit(solution)/shard_map/ppermute | solution.py:38
  902.3 35.9 %collective-permute-start.51 = (bf16[4,64,3072]{2,1,0:T(8,128)(2,1)}, bf16[4,64,3072]{2,1,0:T(8,128)(2,1)}, u32[]{:S(2)}, u32[]{:S(2)}) collective-permute-start(bf16[4,64,3072]{2,1,0:T(8,128)(2,1)} %add_convert_fusion.2), channel_id=1, source_target_pairs={{0,3},{1,0},{2,1},{3,2},{4,7},{5,4},{6,5},{7,6},{8,11},{9,8},{10,9... | collective-permute-start | bytes 4718600 | tf_op jit(solution)/shard_map/ppermute | solution.py:49
  942.1 34.9 %collective-permute-start.52 = (bf16[4,64,3072]{2,1,0:T(8,128)(2,1)}, bf16[4,64,3072]{2,1,0:T(8,128)(2,1)}, u32[]{:S(2)}, u32[]{:S(2)}) collective-permute-start(bf16[4,64,3072]{2,1,0:T(8,128)(2,1)} %add_convert_fusion.1), channel_id=1, source_target_pairs={{0,3},{1,0},{2,1},{3,2},{4,7},{5,4},{6,5},{7,6},{8,11},{9,8},{10,9... | collective-permute-start | bytes 4718600 | tf_op jit(solution)/shard_map/ppermute | solution.py:49
  984.0 34.8 %collective-permute-start.55 = (bf16[64,3072]{1,0:T(8,128)(2,1)S(1)}, bf16[64,3072]{1,0:T(8,128)(2,1)}, u32[]{:S(2)}, u32[]{:S(2)}) collective-permute-start(bf16[64,3072]{1,0:T(8,128)(2,1)S(1)} %get-tuple-element.277), channel_id=1, source_target_pairs={{0,24},{4,28},{8,16},{12,20},{16,8},{20,12},{24,0},{28,4},{1,25},{... | collective-permute-start | bytes 1179656 | tf_op jit(solution)/shard_map/ppermute | solution.py:112
  1079.3 47.0 %collective-permute-start.38 = (bf16[384,2560]{1,0:T(8,128)(2,1)}, bf16[384,2560]{1,0:T(8,128)(2,1)}, u32[]{:S(2)}, u32[]{:S(2)}) collective-permute-start(bf16[384,2560]{1,0:T(8,128)(2,1)} %get-tuple-element.255), channel_id=1, source_target_pairs={{0,24},{4,28},{8,16},{12,20},{16,8},{20,12},{24,0},{28,4},{1,25},{... | collective-permute-start | bytes 5898248 | tf_op jit(solution)/shard_map/ppermute | solution.py:112
  1081.0 81.0 %collective-permute-start.37 = (bf16[384,2560]{1,0:T(8,128)(2,1)}, bf16[384,2560]{1,0:T(8,128)(2,1)}, u32[]{:S(2)}, u32[]{:S(2)}) collective-permute-start(bf16[384,2560]{1,0:T(8,128)(2,1)} %get-tuple-element.256), channel_id=1, source_target_pairs={{0,16},{4,20},{8,24},{12,28},{16,0},{20,4},{24,8},{28,12},{1,17},{... | collective-permute-start | bytes 5898248 | tf_op jit(solution)/shard_map/ppermute | solution.py:112
  1081.1 81.0 %collective-permute-start.36 = (bf16[384,2560]{1,0:T(8,128)(2,1)}, bf16[384,2560]{1,0:T(8,128)(2,1)}, u32[]{:S(2)}, u32[]{:S(2)}) collective-permute-start(bf16[384,2560]{1,0:T(8,128)(2,1)} %get-tuple-element.257), channel_id=1, source_target_pairs={{0,8},{4,12},{8,0},{12,4},{16,24},{20,28},{24,16},{28,20},{1,9},{5... | collective-permute-start | bytes 5898248 | tf_op jit(solution)/shard_map/ppermute | solution.py:112
  1092.4 86.9 %collective-permute-start.35 = (bf16[280,2048]{1,0:T(8,128)(2,1)S(1)}, bf16[280,2048]{1,0:T(8,128)(2,1)}, u32[]{:S(2)}, u32[]{:S(2)}) collective-permute-start(bf16[280,2048]{1,0:T(8,128)(2,1)S(1)} %fusion.39), channel_id=1, source_target_pairs={{0,3},{1,0},{2,1},{3,2},{4,7},{5,4},{6,5},{7,6},{8,11},{9,8},{10,9... | collective-permute-start | bytes 3440648 | tf_op jit(solution)/shard_map/ppermute | solution.py:49
  1187.4 41.4 %collective-permute-start.46 = (bf16[96,2560]{1,0:T(8,128)(2,1)S(1)}, bf16[96,2560]{1,0:T(8,128)(2,1)S(1)}, u32[]{:S(2)}, u32[]{:S(2)}) collective-permute-start(bf16[96,2560]{1,0:T(8,128)(2,1)S(1)} %pad_maximum_fusion.14), channel_id=1, source_target_pairs={{0,3},{1,0},{2,1},{3,2},{4,7},{5,4},{6,5},{7,6},{8,11},{9,8},{10,9... | collective-permute-start | bytes 1474568 | tf_op jit(solution)/shard_map/ppermute | solution.py:49
  1187.5 61.8 %collective-permute-start.39 = (bf16[280,2048]{1,0:T(8,128)(2,1)}, bf16[280,2048]{1,0:T(8,128)(2,1)}, u32[]{:S(2)}, u32[]{:S(2)}) collective-permute-start(bf16[280,2048]{1,0:T(8,128)(2,1)} %fusion.38), channel_id=1, source_target_pairs={{0,3},{1,0},{2,1},{3,2},{4,7},{5,4},{6,5},{7,6},{8,11},{9,8},{10,9... | collective-permute-start | bytes 3440648 | tf_op jit(solution)/shard_map/ppermute | solution.py:49
  (157 other events, 3021.9 us)
Sparse Core Ops, SparseCore 0:
  11.4 121.1 all-gather.5
  135.1 93.5 all-gather.9
  230.6 111.6 all-gather.7
  344.0 89.8 all-gather.11
  435.6 89.8 all-gather.13
  603.6 115.9 reduce-scatter.6
  723.1 92.4 reduce-scatter.12
  819.1 115.9 reduce-scatter.8
  938.7 132.8 reduce-scatter.10

commit v4 on v3

--- a/solution.py
+++ b/solution.py
@@ -79,6 +79,14 @@
     return jnp.bitwise_xor(rel, lax.axis_index("dp").astype(jnp.int32))
 
 
+def direct_gather(shard):
+    size = lax.axis_size("dp")
+    own = [shard]
+    for c in range(1, size // 2):
+        own.append(lax.ppermute(shard, "dp", [(d, d ^ (2 * c)) for d in range(size)]))
+    return own + [hop(piece, 1) for piece in own]
+
+
 def dp_gather(shard):
     chips = lax.axis_size("dp") // 2
     half = shard.shape[0] // 2
@@ -111,6 +119,14 @@
     return [
         lax.ppermute(blocks[c].astype(BF16), "dp", [(d, d ^ (2 * c)) for d in range(size)])
         for c in range(1, size // 2)
+    ]
+
+
+def send_members(parts):
+    size = lax.axis_size("mp")
+    return [
+        lax.ppermute(parts[r], "mp", [(d, (d - r) % size) for d in range(size)])
+        for r in range(1, size)
     ]
 
 
@@ -267,10 +283,14 @@
     return hidden.astype(BF16), gate_back.astype(BF16), up_back.astype(BF16)
 
 
-def _feed_forward_tile(groups, *refs):
-    pieces, (back_ref, gate_ref, up_ref) = refs[:groups], refs[groups : groups + 3]
-    hidden_ref, gate_back_ref, up_back_ref, rows_ref = refs[groups + 3 :]
+def _feed_forward_tile(groups, order, *refs):
+    pieces, (back_ref, gate_ref) = refs[:groups], refs[groups : groups + 2]
+    up_pieces = refs[groups + 2 : -5]
+    hidden_ref, gate_back_ref, up_back_ref, rows_ref, up_ref = refs[-5:]
     count = pieces[0].shape[0]
+    for g, piece in enumerate(up_pieces):
+        size = piece.shape[0]
+        up_ref[pl.ds(pl.multiple_of(order[g] * size, size), size), :] = piece[...]
     root, cube = 0.7978845608028654, 0.044715
 
     @pl.when(pl.program_id(0) == 0)
@@ -294,28 +314,69 @@
         up_back_ref[cut, :] = (back * active).astype(BF16)
 
 
-def feed_forward_kernel(pieces, hidden_back, gate, up, tile=512):
+def feed_forward_kernel(order, pieces, hidden_back, gate, up_pieces, tile=512):
     groups = len(pieces)
     count, width = pieces[0].shape
     total = groups * count
     units = gate.shape[1]
-    block = pl.BlockSpec((total, tile), lambda n: (0, n))
-    weight = pl.BlockSpec((width, tile), lambda n: (0, n))
-    fixed = pl.BlockSpec((count, width), lambda n: (0, 0), pipeline_mode=pl.Buffered(1))
+    block = pl.BlockSpec((total, tile), lambda n, idx: (0, n))
+    weight = pl.BlockSpec((width, tile), lambda n, idx: (0, n))
+    part = pl.BlockSpec((width // len(up_pieces), tile), lambda n, idx: (0, n))
+    fixed = pl.BlockSpec((count, width), lambda n, idx: (0, 0), pipeline_mode=pl.Buffered(1))
     return pl.pallas_call(
         functools.partial(_feed_forward_tile, groups),
-        grid=(units // tile,),
-        in_specs=[fixed] * groups + [block, weight, weight],
-        out_specs=[block] * 3 + [pl.BlockSpec((total, width), lambda n: (0, 0))],
+        grid_spec=pltpu.PrefetchScalarGridSpec(
+            num_scalar_prefetch=1,
+            grid=(units // tile,),
+            in_specs=[fixed] * groups + [block, weight] + [part] * len(up_pieces),
+            out_specs=[block] * 3
+            + [pl.BlockSpec((total, width), lambda n, idx: (0, 0)), weight],
+        ),
         out_shape=[jax.ShapeDtypeStruct((total, units), BF16)] * 3
-        + [jax.ShapeDtypeStruct((total, width), BF16)],
+        + [
+            jax.ShapeDtypeStruct((total, width), BF16),
+            jax.ShapeDtypeStruct((width, units), BF16),
+        ],
         compiler_params=pltpu.CompilerParams(vmem_limit_bytes=56 * 2**20),
         cost_estimate=pl.CostEstimate(
             flops=4 * total * width * units,
-            bytes_accessed=4 * width * units + 8 * total * units + 4 * total * width,
+            bytes_accessed=6 * width * units + 8 * total * units + 4 * total * width,
             transcendentals=total * units,
         ),
-    )(*pieces, hidden_back, gate, up)
+    )(order, *pieces, hidden_back, gate, *up_pieces)
+
+
+def _stacked_grads(rows, cots, gate_back, up_back, hidden, out):
+    size = rows.shape[1]
+    for n, (left, right) in enumerate(((rows, gate_back), (rows, up_back), (cots, hidden))):
+        out[n * size : (n + 1) * size, :] = lax.dot_general(
+            left[...], right[...], (((0,), (0,)), ((), ())), preferred_element_type=F32
+        ).astype(BF16)
+
+
+def stacked_grads(ways, rows, cots, gate_back, up_back, hidden):
+    lines, width = rows.shape
+    units = hidden.shape[1]
+    size = width // ways
+    if size % 128:
+        terms = [mm_tn(rows, gate_back), mm_tn(rows, up_back), mm_tn(cots, hidden)]
+        cut = [term.astype(BF16).reshape(ways, size, units) for term in terms]
+        return jnp.concatenate(cut, axis=1).reshape(-1, units)
+    column = pl.BlockSpec((lines, size), lambda g: (0, g))
+    whole = pl.BlockSpec((lines, units), lambda g: (0, 0))
+    return pl.pallas_call(
+        _stacked_grads,
+        grid=(ways,),
+        in_specs=[column, column, whole, whole, whole],
+        out_specs=pl.BlockSpec((3 * size, units), lambda g: (g, 0)),
+        out_shape=jax.ShapeDtypeStruct((3 * width, units), BF16),
+        compiler_params=pltpu.CompilerParams(vmem_limit_bytes=32 * 2**20),
+        cost_estimate=pl.CostEstimate(
+            flops=6 * lines * width * units,
+            bytes_accessed=6 * width * units + 6 * lines * units,
+            transcendentals=0,
+        ),
+    )(rows, cots, gate_back, up_back, hidden)
 
 
 def after(value, *first):
@@ -379,7 +440,10 @@
 
     out_ring = ring_gather(jnp.concatenate([pre_output, act_output], axis=1))
     out_block = in_place(out_ring)
-    qkv_full, act_stack, out_block = lax.optimization_barrier((qkv_full, act_stack, out_block))
+    qkv_full, act_stack, out_block, up_own = lax.optimization_barrier(
+        (qkv_full, act_stack, out_block, pre_up)
+    )
+    up_pieces = direct_gather(up_own)
     out_full = jnp.concatenate(dp_gather(out_block), axis=0)
     qkv_full = qkv_full.reshape(ways * groups, -1, qkv_own.shape[1])
     pre_qkv = qkv_full[:, :pre_part].reshape(width, -1)
@@ -474,12 +538,11 @@
         [rotate(keyval_raw[..., :head_dim], cosine_tab, sine_tab), keyval_raw[..., head_dim:]],
         axis=-1,
     ).astype(BF16)
-    keyval_rows, gate_own, up_own, down_own = lax.optimization_barrier(
-        (keyval_rows, pre_gate, pre_up, pre_down)
+    keyval_rows, gate_own, down_own = lax.optimization_barrier(
+        (keyval_rows, pre_gate, pre_down)
     )
     down_full = lax.all_gather(down_own, "dp", axis=1, tiled=True)
     gate_full = lax.all_gather(gate_own, "dp", axis=0, tiled=True)
-    up_full = lax.all_gather(up_own, "dp", axis=0, tiled=True)
     all_keyval = jnp.concatenate(ring_gather(keyval_rows), axis=1)
     cot_all = ring_stack(pad(cot_flat))
     act_cot_all = ring_stack(act_final_back.astype(BF16))
@@ -519,17 +582,12 @@
     act_hidden, act_gate_back, act_up_back = feed_forward(
         act_all_rows, act_cot_all, act_gate_full, act_up_full, act_down_full, slot_live
     )
-    act_terms = [
-        mm_tn(act_all_rows, act_gate_back).astype(BF16),
-        mm_tn(act_all_rows, act_up_back).astype(BF16),
-        mm_tn(act_cot_all, act_hidden).astype(BF16),
-    ]
     act_second_part = split(mm_nt(act_gate_back, act_gate_full) + mm_nt(act_up_back, act_up_full))
     act_sum_part = split(mm_nt(act_hidden, act_down_full))
 
-    act_stacked = jnp.concatenate(
-        [term.reshape(ways, -1, act_gate.shape[1]) for term in act_terms], axis=1
-    ).reshape(-1, act_gate.shape[1])
+    act_stacked = stacked_grads(
+        ways, act_all_rows, act_cot_all, act_gate_back, act_up_back, act_hidden
+    )
     pre_second = pad(rms_norm(pre_mid, pre_mlp_gain).astype(BF16))
     second_pieces = [pre_second]
     for r in range(1, groups):
@@ -537,14 +595,14 @@
         if r == 1:
             piece, hidden_back = lax.optimization_barrier((piece, hidden_back))
         if r == groups - 1:
-            piece, act_stacked = lax.optimization_barrier((piece, act_stacked))
+            piece = after(piece, act_stacked)
         second_pieces.append(piece)
     grad_act = scatter_sum(act_stacked, 0)
     grad_act = grad_act.astype(F32).reshape(3, -1, act_gate.shape[1])
     grad_act_gate, grad_act_up, grad_act_down = grad_act[0], grad_act[1], grad_act[2].T
 
-    pre_hidden, pre_gate_back, pre_up_back, pre_all = feed_forward_kernel(
-        second_pieces, hidden_back, gate_full, up_full
+    pre_hidden, pre_gate_back, pre_up_back, pre_all, up_full = feed_forward_kernel(
+        order, second_pieces, hidden_back, gate_full, up_pieces
     )
     gate_term = mm_tn(pre_all, pre_gate_back).astype(BF16)
     gate_term, pre_up_back = lax.optimization_barrier((gate_term, pre_up_back))
@@ -605,9 +663,7 @@
     out_sums = chip_sums(
         mm_tn(att_joint[:, :out_half], back_joint).astype(BF16),
         mm_tn(att_joint[:, out_half:], back_joint).astype(BF16),
-    )
-    out_sums = ring_scatter(member_parts(out_sums, (out_part,)))
-    grad_out = add_up(out_sums[0], send_blocks(out_sums))
+    ).astype(BF16)
     probs_back = jnp.einsum(
         "iqhd,ikd->ihqk", attended_back, value_rows, preferred_element_type=F32
     )
@@ -634,16 +690,18 @@
     query_low = rotate(query_back, cosine_tab[:, None, :], -sine_tab[:, None, :])
     query_low = query_low.reshape(items, local_len, query_width).astype(BF16)
     back_rows = from_items(jnp.concatenate([query_low, keyval_low], axis=-1))
-    back_rows, grad_pre_gate = lax.optimization_barrier((back_rows, grad_pre_gate))
+    back_rows, grad_pre_gate, out_sums = lax.optimization_barrier(
+        (back_rows, grad_pre_gate, out_sums)
+    )
+    out_arrived = send_blocks(out_sums)
     qkv_half = normed.shape[1] // 2
     qkv_own_part = mm_tn(normed[:, :qkv_half], back_rows).astype(BF16)
     qkv_other_part = mm_tn(normed[:, qkv_half:], back_rows).astype(BF16)
     qkv_sums = chip_sums(qkv_own_part, qkv_other_part).astype(BF16)
-    qkv_sums, pre_hidden = lax.optimization_barrier((qkv_sums, pre_hidden))
-    arrived = send_blocks(qkv_sums)
     act_final_low = (act_mid + act_sums).astype(BF16)
     action_pred = mm(act_final_low, action_head).reshape(pred_cot.shape) * live_mask
     grad_head = mm_tn(act_final_low, pred_back)
+    back_rows, out_arrived = lax.optimization_barrier((back_rows, out_arrived))
     pre_normed_back = mm_nt(back_rows[:padded], pre_qkv)[:count]
     act_normed_back = mm_nt(back_rows[padded:], act_qkv)[:act_count]
     pre_x_part, grad_pre_attn_gain = rms_back(pre_x, pre_attn_gain, pre_normed_back)
@@ -665,33 +723,38 @@
         ],
         axis=1,
     )
-    arrived, small = lax.optimization_barrier((arrived, small))
-
-    pre_sum_part = split(mm(pre_hidden, down_full))
+    small = small + hop(small, 1)
+    spare = -(-groups // 8) * 8 - groups
+    sent_blocks = []
+    for c in range(ways // 2):
+        start = jnp.bitwise_xor(lax.axis_index("dp"), 2 * c) * groups
+        lines = lax.dynamic_slice_in_dim(small, start, groups, 0)
+        lines = jnp.pad(lines, ((0, spare), (0, qkv_sums.shape[2] - small.shape[1])))
+        sent_blocks.append(jnp.concatenate([qkv_sums[c], lines.astype(BF16)], axis=0))
+    sent_blocks, out_arrived, pre_hidden = lax.optimization_barrier(
+        (sent_blocks, out_arrived, pre_hidden)
+    )
+    arrived = send_blocks(sent_blocks)
+    pre_sum_part = split(mm(pre_hidden, down_full).astype(BF16))
     sum_parts = [each[:count] for each in pre_sum_part]
-    total = sum_parts[-1]
-    for r in range(groups - 2, -1, -1):
-        total = total.astype(BF16)
-        if r == 0:
-            total, arrived = lax.optimization_barrier((total, arrived))
-        total = ring(total, -1, LOOSE).astype(F32) + sum_parts[r]
-    pre_sums = total
+    sums_arrived = send_members(sum_parts)
+    arrived, out_arrived = lax.optimization_barrier((arrived, out_arrived))
+    qkv_parts = member_parts(
+        add_up(sent_blocks[0].astype(F32), arrived).astype(BF16), (pre_part, act_part, 1)
+    )
+    qkv_arrived = send_members(qkv_parts)
+    out_parts = member_parts(
+        add_up(out_sums[0].astype(F32), out_arrived).astype(BF16), (out_part,)
+    )
+    out_arrived = send_members(out_parts)
+    sums_arrived, grad_pre_up, grad_pre_down, qkv_first = lax.optimization_barrier(
+        (sums_arrived, grad_pre_up, grad_pre_down, qkv_parts[0])
+    )
+    pre_sums = add_up(sum_parts[0].astype(F32), sums_arrived)
     prefix_out = (pre_mid + pre_sums).astype(BF16).reshape(prefix_tokens.shape)
-    grad_qkv = ring_scatter(
-        member_parts(add_up(qkv_sums[0].astype(F32), arrived), (pre_part, act_part))
-    )
-
-    bit = 1
-    while bit < ways:
-        small = small + hop(small, bit)
-        bit *= 2
-    mine = lax.axis_index("dp") * groups
-    terms = [
-        lax.dynamic_slice_in_dim(small, mine + (member - r) % groups, 1, 0) for r in range(groups)
-    ]
-    total = terms[-1]
-    for term in terms[-2::-1]:
-        total = ring(total, -1, LOOSE) + term
+    grad_out = add_up(out_parts[0].astype(F32), out_arrived)
+    grad_qkv = add_up(qkv_first.astype(F32), qkv_arrived)
+    total = grad_qkv[pre_part + act_part :, : small.shape[1]]
     sizes = [width // devices] * 2 + [act_width // devices] * 2
     gains, start = [], 0
     for size in sizes:
@@ -708,8 +771,8 @@
         grad_qkv[:pre_part, :query_width],
         grad_qkv[:pre_part, query_width:],
         grad_out[:, :width],
-        grad_qkv[pre_part:, :query_width],
-        grad_qkv[pre_part:, query_width:],
+        grad_qkv[pre_part : pre_part + act_part, :query_width],
+        grad_qkv[pre_part : pre_part + act_part, query_width:],
         grad_out[:, width:],
         grad_pre_gate.astype(F32),
         grad_pre_up.astype(F32),

time: 1280 us -> 1240 us (0.969)
  local copies, waits for them, and re-layouts: 176 us -> 129 us
  waiting for transfers between devices: 544 us -> 589 us
  other arithmetic: 96.8 us -> 65.1 us
  starting transfers between devices: 82.5 us -> 57.6 us
    ppermute x21 -> x9, waiting for transfers between devices: 159 us -> 34.2 us  [ring(): return lax.ppermute(value, 'mp', pairs)]
    ppermute x6, waiting for transfers between devices: 77.9 us -> 186 us  [send_blocks(): lax.ppermute(blocks[c].astype(BF16), 'dp', [(d, d ^ 2 * c) for d in range...]
    all_gather x1 -> x0, waiting for transfers between devices: 91.6 us -> none  [shards(): up_full = lax.all_gather(up_own, 'dp', axis=0, tiled=True)]
    all_gather x1, waiting for transfers between devices: 3.3 us -> 55.5 us  [shards(): gate_full = lax.all_gather(gate_own, 'dp', axis=0, tiled=True)]
    ppermute x0 -> x12, waiting for transfers between devices: none -> 48 us  [the longest x3 26.4 us: direct_gather(): own.append(lax.ppermute(shard, 'dp', [(d, d ^ 2 * c) for d in range(size)]))]
    ppermute x21 -> x9, starting transfers between devices: 54.5 us -> 14.8 us  [ring(): return lax.ppermute(value, 'mp', pairs)]
    all_gather x1, waiting for transfers between devices: 0.02 us -> 36.5 us  [shards(): act_flat_w = lax.all_gather(act_stack, 'dp', axis=0, tiled=True)]
    unnamed x283 -> x272, local copies, waits for them, and re-layouts: 68.5 us -> 48.6 us
  transfers between devices with their start and end apart: 65 -> 66, of which waited for: 32 -> 30; matrix products, arithmetic and copies ran while one was open for 41% -> 35% of each run, Pallas kernels for 0% -> 1%
where the time goes in v4:
time: 1240 us; the launch traced here: 1230 us
  waiting for transfers between devices  589 us (48%)
  matrix products  308 us (25%)
  local copies, waits for them, and re-layouts  129 us (10%)
  other arithmetic  65.1 us (5%)
  Pallas kernels  61.7 us (5%)
  starting transfers between devices  57.6 us (5%)
  between operations  16.5 us (1%)
    ppermute x6, waiting for transfers between devices, send_blocks(): lax.ppermute(blocks[c].astype(BF16), 'dp', [(d, d ^ 2 * c) for d in range...  186 us
    ppermute x19, waiting for transfers between devices, send(): result = lax.ppermute(value, axis, pairs)  145 us
    dot_general x12, matrix products, mm_nt(): lax.dot_general(left, right, (((1,), (1,)), ((), ())), preferred_element_...  130 us
    dot_general x8, matrix products, mm_tn(): lax.dot_general(left, right, (((0,), (0,)), ((), ())), preferred_element_...  114 us
    all_gather x1, waiting for transfers between devices, shards(): qkv_full = lax.all_gather(qkv_own, ('dp', 'mp'), axis=0, tiled=True)  62.1 us
    all_gather x1, waiting for transfers between devices, shards(): gate_full = lax.all_gather(gate_own, 'dp', axis=0, tiled=True)  55.5 us
    pallas_call x1, Pallas kernels, feed_forward_kernel(): pl.pallas_call(functools.partial(_feed_forward_tile, groups), grid_spec=p...  54.1 us
    dot_general x10, matrix products, mm(): lax.dot_general(left, right, (((1,), (0,)), ((), ())), preferred_element_...  50.3 us
  transfers between devices with their start and end apart: 66, of which 30 were waited for; matrix products, arithmetic and copies ran while one was open for 35% of the time, Pallas kernels for 1%

profile of v4, /device:TPU:0, one launch (start us, length us, event | category | flops | bytes accessed | tf_op | source)
XLA Modules:
  0.0 1226.7 jit_solution(7669004695878512988)
XLA Ops:
  25.0 21.5 %collective-permute-done.1 = bf16[64,3072]{1,0:T(8,128)(2,1)} collective-permute-done((bf16[64,3072]{1,0:T(8,128)(2,1)}, bf16[64,3072]{1,0:T(8,128)(2,1)}, u32[]{:S(2)}, u32[]{:S(2)}) %collective-permute-start.1) | collective-permute-done | bytes 393248 | tf_op jit(solution)/shard_map/ppermute | solution.py:26
  48.5 15.2 %collective-permute-done.2 = bf16[64,3072]{1,0:T(8,128)(2,1)} collective-permute-done((bf16[64,3072]{1,0:T(8,128)(2,1)}, bf16[64,3072]{1,0:T(8,128)(2,1)}, u32[]{:S(2)}, u32[]{:S(2)}) %collective-permute-start.2) | collective-permute-done | bytes 393248 | tf_op jit(solution)/shard_map/ppermute | solution.py:26
  71.2 62.1 %all-gather.5.cloned.1.call-done = bf16[3072,2560]{1,0:T(8,128)(2,1)} async-done(((bf16[96,2560]{1,0:T(8,128)(2,1)}), bf16[3072,2560]{1,0:T(8,128)(2,1)}) %all-gather.5.cloned.1.call-update) | async-done | bytes 15728656 | tf_op jit(solution)/shard_map/all_gather | solution.py:434
  138.7 9.0 slice.412
  191.1 11.9 collective-permute-done.5
  207.5 20.3 %collective-permute-done.6 = bf16[256,3072]{1,0:T(8,128)(2,1)S(1)} collective-permute-done((bf16[256,3072]{1,0:T(8,128)(2,1)}, bf16[256,3072]{1,0:T(8,128)(2,1)S(1)}, u32[]{:S(2)}, u32[]{:S(2)}) %collective-permute-start.6) | collective-permute-done | bytes 1572896 | tf_op jit(solution)/shard_map/ppermute | solution.py:26
  241.2 24.6 %collective-permute-done.8 = bf16[128,3072]{1,0:T(8,128)(2,1)} collective-permute-done((bf16[128,3072]{1,0:T(8,128)(2,1)}, bf16[128,3072]{1,0:T(8,128)(2,1)}, u32[]{:S(2)}, u32[]{:S(2)}) %collective-permute-start.8) | collective-permute-done | bytes 786464 | tf_op jit(solution)/shard_map/ppermute | solution.py:26
  279.5 14.6 %collective-permute-done.16 = bf16[288,2048]{1,0:T(8,128)(2,1)S(1)} collective-permute-done((bf16[288,2048]{1,0:T(8,128)(2,1)}, bf16[288,2048]{1,0:T(8,128)(2,1)S(1)}, u32[]{:S(2)}, u32[]{:S(2)}) %collective-permute-start.16) | collective-permute-done | bytes 1179680 | tf_op jit(solution)/shard_map/ppermute | solution.py:26
  311.9 17.5 %collective-permute-done.24 = bf16[24,1024]{1,0:T(8,128)(2,1)S(1)} collective-permute-done((bf16[24,1024]{1,0:T(8,128)(2,1)S(1)}, bf16[24,1024]{1,0:T(8,128)(2,1)S(1)}, u32[]{:S(2)}, u32[]{:S(2)}) %collective-permute-start.24) | collective-permute-done | bytes 49184 | tf_op jit(solution)/shard_map/ppermute | solution.py:49
  336.6 25.2 %convolution_convert_fusion.3.refs_4_ = bf16[1152,4096]{1,0:T(8,128)(2,1)} fusion(bf16[4096,2048]{1,0:T(8,128)(2,1)} %all-gather.7.cloned.1.call-done, bf16[288,2048]{1,0:T(8,128)(2,1)} %copy-done.116, bf16[288,2048]{1,0:T(8,128)(2,1)S(1)} %copy-done.114, bf16[288,2048]{1,0:T(8,128)(2,1)} %collective-permute-done.15, bf16[288,2048]{1,0:T(8,128)(2,1)} %pad.59), kind=kOutput, calls=%fused_computation.5 | convolution fusion | flops 19350945792 | bytes 30932992 | tf_op jit(solution)/shard_map/dot_general | solution.py:266
  367.0 26.4 %collective-permute-done.28.refs_8_ = bf16[256,4096]{1,0:T(8,128)(2,1)} collective-permute-done((bf16[256,4096]{1,0:T(8,128)(2,1)}, bf16[256,4096]{1,0:T(8,128)(2,1)}, u32[]{:S(2)}, u32[]{:S(2)}) %collective-permute-start.28) | collective-permute-done | bytes 2097184 | tf_op jit(solution)/shard_map/ppermute | solution.py:86
  394.0 36.5 %all-gather.9.cloned.1.call-done = bf16[3072,2048]{1,0:T(8,128)(2,1)} async-done(((bf16[384,2048]{1,0:T(8,128)(2,1)}), bf16[3072,2048]{1,0:T(8,128)(2,1)}) %all-gather.9.cloned.1.call-update) | async-done | bytes 12582928 | tf_op jit(solution)/shard_map/all_gather | solution.py:451
  451.7 15.0 %collective-permute-done.23.refs_3_ = bf16[288,2048]{1,0:T(8,128)(2,1)} collective-permute-done((bf16[288,2048]{1,0:T(8,128)(2,1)}, bf16[288,2048]{1,0:T(8,128)(2,1)}, u32[]{:S(2)}, u32[]{:S(2)}) %collective-permute-start.23) | collective-permute-done | bytes 1179680 | tf_op jit(solution)/shard_map/ppermute | solution.py:26
  466.8 55.5 %all-gather.11.cloned.1.call-done.refs_5_ = bf16[2048,4096]{1,0:T(8,128)(2,1)} async-done(((bf16[256,4096]{1,0:T(8,128)(2,1)}), bf16[2048,4096]{1,0:T(8,128)(2,1)}) %all-gather.11.cloned.1.call-update) | async-done | bytes 16777232 | tf_op jit(solution)/shard_map/all_gather | solution.py:545
  522.2 54.1 %shard_map.394 = (bf16[1152,4096]{1,0:T(8,128)(2,1)}, bf16[1152,4096]{1,0:T(8,128)(2,1)}, bf16[1152,4096]{1,0:T(8,128)(2,1)}, bf16[1152,2048]{1,0:T(8,128)(2,1)}, bf16[2048,4096]{1,0:T(8,128)(2,1)}) custom-call(s32[8]{0:T(128)} %copy-done.4, bf16[288,2048]{1,0:T(8,128)(2,1)} %copy-done.53, bf16[288,2048]{1,0:T(8,128)(2,1)} %collective-permute-done.20.refs_1_, ...), custom_call_target="tpu_custom_call" | custom-call | flops 38654705664 | bytes 97517568 | tf_op jit(solution)/shard_map/pallas_call | solution.py:326
  576.3 28.0 %convolution_convert_fusion.2 = bf16[2048,4096]{1,0:T(8,128)(2,1)} fusion(bf16[1152,2048]{1,0:T(8,128)(2,1)} %get-tuple-element.113, bf16[1152,4096]{1,0:T(8,128)(2,1)} %get-tuple-element.119), kind=kOutput, calls=%fused_computation.4 | convolution fusion | flops 19335741440 | bytes 30932992 | tf_op jit(solution)/shard_map/dot_general | solution.py:270
  618.4 18.6 %fusion.11 = f32[576,2048]{1,0:T(8,128)} fusion(bf16[2048,4096]{1,0:T(8,128)(2,1)} %get-tuple-element.116, bf16[1152,4096]{1,0:T(8,128)(2,1)} %get-tuple-element.122), kind=kOutput, calls=%fused_computation.26 | convolution fusion | flops 9663676416 | bytes 26214400 | tf_op jit(solution)/shard_map/dot_general | solution.py:266
  636.9 17.7 %fusion.23 = f32[576,2048]{1,0:T(8,128)} fusion(f32[576,2048]{1,0:T(8,128)} %fusion.11, bf16[2048,4096]{1,0:T(8,128)(2,1)} %all-gather.11.cloned.1.call-done.refs_5_, bf16[1152,4096]{1,0:T(8,128)(2,1)} %get-tuple-element.119), kind=kOutput, calls=%fused_computation.42 | convolution fusion | flops 9664856064 | bytes 30932992 | tf_op jit(solution)/shard_map/dot_general | solution.py:266
  660.2 16.8 %fusion.9 = f32[576,2048]{1,0:T(8,128)} fusion(bf16[2048,4096]{1,0:T(8,128)(2,1)} %all-gather.11.cloned.1.call-done.refs_5_, bf16[1152,4096]{1,0:T(8,128)(2,1)} %get-tuple-element.119), kind=kOutput, calls=%fused_computation.24 | convolution fusion | flops 9663676416 | bytes 26214400 | tf_op jit(solution)/shard_map/dot_general | solution.py:266
  677.0 17.3 %fusion.26 = f32[576,2048]{1,0:T(8,128)} fusion(f32[576,2048]{1,0:T(8,128)} %fusion.9, bf16[2048,4096]{1,0:T(8,128)(2,1)} %get-tuple-element.116, bf16[1152,4096]{1,0:T(8,128)(2,1)} %get-tuple-element.122), kind=kOutput, calls=%fused_computation.43 | convolution fusion | flops 9664856064 | bytes 30932992 | tf_op jit(solution)/shard_map/dot_general | solution.py:266
  697.2 27.9 %convolution_convert_fusion.1 = bf16[2048,4096]{1,0:T(8,128)(2,1)} fusion(bf16[1152,2048]{1,0:T(8,128)(2,1)} %get-tuple-element.113, bf16[1152,4096]{1,0:T(8,128)(2,1)} %get-tuple-element.122), kind=kOutput, calls=%fused_computation.3 | convolution fusion | flops 19335741440 | bytes 30932992 | tf_op jit(solution)/shard_map/dot_general | solution.py:270
  734.3 28.4 %convolution_convert_fusion = bf16[4096,2048]{1,0:T(8,128)(2,1)} fusion(bf16[1152,4096]{1,0:T(8,128)(2,1)} %get-tuple-element.134, bf16[288,2048]{1,0:T(8,128)(2,1)S(1)} %copy-done.117, bf16[288,2048]{1,0:T(8,128)(2,1)S(1)} %copy-done.115, bf16[288,2048]{1,0:T(8,128)(2,1)} %collective-permute-done.15, bf16[288,2048]{1,0:T(8,128)(2,1)} %pad.59), kind=kOutput, calls=%fused_computation.2 | convolution fusion | flops 19354615808 | bytes 30932992 | tf_op jit(solution)/shard_map/dot_general | solution.py:270
  773.5 7.9 convolution_convert_fusion.8.refs_0_
  843.7 8.3 add_convert_fusion.1
  878.4 45.2 %collective-permute-done.44 = bf16[256,3072]{1,0:T(8,128)(2,1)} collective-permute-done((bf16[256,3072]{1,0:T(8,128)(2,1)}, bf16[256,3072]{1,0:T(8,128)(2,1)}, u32[]{:S(2)}, u32[]{:S(2)}) %collective-permute-start.44) | collective-permute-done | bytes 1572896 | tf_op jit(solution)/shard_map/ppermute | solution.py:120
  923.7 46.8 %collective-permute-done.43 = bf16[256,3072]{1,0:T(8,128)(2,1)} collective-permute-done((bf16[256,3072]{1,0:T(8,128)(2,1)}, bf16[256,3072]{1,0:T(8,128)(2,1)}, u32[]{:S(2)}, u32[]{:S(2)}) %collective-permute-start.43) | collective-permute-done | bytes 1572896 | tf_op jit(solution)/shard_map/ppermute | solution.py:120
  970.4 8.8 multiply_reduce_fusion
  998.4 25.4 %convolution_convert_fusion.6 = bf16[1152,2048]{1,0:T(8,128)(2,1)S(1)} fusion(bf16[1152,4096]{1,0:T(8,128)(2,1)} %get-tuple-element.134, bf16[4096,2048]{1,0:T(8,128)(2,1)} %all-gather.7.cloned.1.call-done), kind=kOutput, calls=%fused_computation.11 | convolution fusion | flops 19329712128 | bytes 30932992 | tf_op jit(solution)/shard_map/dot_general | solution.py:262
  1030.1 13.9 %collective-permute-done.49 = bf16[392,2560]{1,0:T(8,128)(2,1)S(1)} collective-permute-done((bf16[392,2560]{1,0:T(8,128)(2,1)S(1)}, bf16[392,2560]{1,0:T(8,128)(2,1)S(1)}, u32[]{:S(2)}, u32[]{:S(2)}) %collective-permute-start.49) | collective-permute-done | bytes 2007072 | tf_op jit(solution)/shard_map/ppermute | solution.py:120
  1047.3 80.2 %collective-permute-done.51 = bf16[392,2560]{1,0:T(8,128)(2,1)S(1)} collective-permute-done((bf16[392,2560]{1,0:T(8,128)(2,1)S(1)}, bf16[392,2560]{1,0:T(8,128)(2,1)S(1)}, u32[]{:S(2)}, u32[]{:S(2)}) %collective-permute-start.51) | collective-permute-done | bytes 2007072 | tf_op jit(solution)/shard_map/ppermute | solution.py:120
  1145.7 18.9 %reduce-scatter.9.cloned.1.call-done = bf16[4096,256]{1,0:T(8,128)(2,1)} async-done(((bf16[4096,2048]{1,0:T(8,128)(2,1)}), bf16[4096,256]{1,0:T(8,128)(2,1)}) %reduce-scatter.9.cloned.1.call-update) | async-done | bytes 2097168 | tf_op jit(solution)/shard_map/reduce_scatter | solution.py:576
  1188.7 14.8 %collective-permute-done.56 = bf16[64,3072]{1,0:T(8,128)(2,1)} collective-permute-done((bf16[64,3072]{1,0:T(8,128)(2,1)}, bf16[64,3072]{1,0:T(8,128)(2,1)}, u32[]{:S(2)}, u32[]{:S(2)}) %collective-permute-start.56) | collective-permute-done | bytes 393248 | tf_op jit(solution)/shard_map/ppermute | solution.py:128
  (588 shorter events, 376.1 us)
Async XLA Ops:
  7.2 126.0 %all-gather.5.cloned.1.call-start = ((), (), s32[]{:S(2)}) async-start(), calls=%async_computation.4 | async-start | bytes 16220160 | tf_op jit(solution)/shard_map/all_gather | solution.py:434
  9.3 327.3 %all-gather.7.cloned.1.call-start = ((), (), s32[]{:S(2)}) async-start(), calls=%async_computation.5 | async-start | bytes 18874368 | tf_op jit(solution)/shard_map/all_gather | solution.py:544
  158.1 272.5 %all-gather.9.cloned.1.call-start = ((), (), s32[]{:S(2)}) async-start(), calls=%async_computation.6 | async-start | bytes 14155776 | tf_op jit(solution)/shard_map/all_gather | solution.py:451
  158.8 363.4 %all-gather.11.cloned.1.call-start = ((), (), s32[]{:S(2)}) async-start(), calls=%async_computation.7 | async-start | bytes 18874368 | tf_op jit(solution)/shard_map/all_gather | solution.py:545
  159.4 692.6 %reduce-scatter.5.cloned.1.call-start = ((), (), s32[]{:S(2)}) async-start(), calls=%async_computation.8 | async-start | bytes 18874368 | tf_op jit(solution)/shard_map/reduce_scatter | solution.py:576
  167.8 109.0 %collective-permute-start.10 = (bf16[256,3072]{1,0:T(8,128)(2,1)}, bf16[256,3072]{1,0:T(8,128)(2,1)}, u32[]{:S(2)}, u32[]{:S(2)}) collective-permute-start(bf16[256,3072]{1,0:T(8,128)(2,1)} %constant_dynamic-slice_fusion.25), channel_id=1, source_target_pairs={{0,4},{4,0},{8,12},{12,8},{16,20},{20,16},{24,28},{28,24},{1,5},{5... | collective-permute-start | bytes 4718600 | tf_op jit(solution)/shard_map/ppermute | solution.py:38
  168.0 69.1 %collective-permute-start.7 = (bf16[256,3072]{1,0:T(8,128)(2,1)}, bf16[256,3072]{1,0:T(8,128)(2,1)}, u32[]{:S(2)}, u32[]{:S(2)}) collective-permute-start(bf16[256,3072]{1,0:T(8,128)(2,1)} %constant_dynamic-slice_fusion.25), channel_id=1, source_target_pairs={{0,16},{4,20},{8,24},{12,28},{16,0},{20,4},{24,8},{28,12},{1,17},{... | collective-permute-start | bytes 4718600 | tf_op jit(solution)/shard_map/ppermute | solution.py:26
  169.4 58.4 %collective-permute-start.6 = (bf16[256,3072]{1,0:T(8,128)(2,1)}, bf16[256,3072]{1,0:T(8,128)(2,1)S(1)}, u32[]{:S(2)}, u32[]{:S(2)}) collective-permute-start(bf16[256,3072]{1,0:T(8,128)(2,1)} %constant_dynamic-slice_fusion.25), channel_id=1, source_target_pairs={{0,8},{4,12},{8,0},{12,4},{16,24},{20,28},{24,16},{28,20},{1,9},{5... | collective-permute-start | bytes 4718600 | tf_op jit(solution)/shard_map/ppermute | solution.py:26
  239.4 56.2 %collective-permute-start.11 = (bf16[256,3072]{1,0:T(8,128)(2,1)S(1)}, bf16[256,3072]{1,0:T(8,128)(2,1)S(1)}, u32[]{:S(2)}, u32[]{:S(2)}) collective-permute-start(bf16[256,3072]{1,0:T(8,128)(2,1)S(1)} %copy-done.28), channel_id=1, source_target_pairs={{0,4},{4,0},{8,12},{12,8},{16,20},{20,16},{24,28},{28,24},{1,5},{5... | collective-permute-start | bytes 4718600 | tf_op jit(solution)/shard_map/ppermute | solution.py:38
  240.7 56.1 %collective-permute-start.12 = (bf16[256,3072]{1,0:T(8,128)(2,1)}, bf16[256,3072]{1,0:T(8,128)(2,1)S(1)}, u32[]{:S(2)}, u32[]{:S(2)}) collective-permute-start(bf16[256,3072]{1,0:T(8,128)(2,1)} %collective-permute-done.7), channel_id=1, source_target_pairs={{0,4},{4,0},{8,12},{12,8},{16,20},{20,16},{24,28},{28,24},{1,5},{5... | collective-permute-start | bytes 4718600 | tf_op jit(solution)/shard_map/ppermute | solution.py:38
  275.4 91.5 %collective-permute-start.29 = (bf16[256,4096]{1,0:T(8,128)(2,1)}, bf16[256,4096]{1,0:T(8,128)(2,1)}, u32[]{:S(2)}, u32[]{:S(2)}) collective-permute-start(bf16[256,4096]{1,0:T(8,128)(2,1)} %refs_6_), channel_id=1, source_target_pairs={{0,24},{4,28},{8,16},{12,20},{16,8},{20,12},{24,0},{28,4},{1,25},{... | collective-permute-start | bytes 6291464 | tf_op jit(solution)/shard_map/ppermute | solution.py:86
  294.1 99.3 %collective-permute-start.28 = (bf16[256,4096]{1,0:T(8,128)(2,1)}, bf16[256,4096]{1,0:T(8,128)(2,1)}, u32[]{:S(2)}, u32[]{:S(2)}) collective-permute-start(bf16[256,4096]{1,0:T(8,128)(2,1)} %refs_6_), channel_id=1, source_target_pairs={{0,16},{4,20},{8,24},{12,28},{16,0},{20,4},{24,8},{28,12},{1,17},{... | collective-permute-start | bytes 6291464 | tf_op jit(solution)/shard_map/ppermute | solution.py:86
  311.1 82.3 %collective-permute-start.27 = (bf16[256,4096]{1,0:T(8,128)(2,1)}, bf16[256,4096]{1,0:T(8,128)(2,1)}, u32[]{:S(2)}, u32[]{:S(2)}) collective-permute-start(bf16[256,4096]{1,0:T(8,128)(2,1)} %refs_6_), channel_id=1, source_target_pairs={{0,8},{4,12},{8,0},{12,4},{16,24},{20,28},{24,16},{28,20},{1,9},{5... | collective-permute-start | bytes 6291464 | tf_op jit(solution)/shard_map/ppermute | solution.py:86
  365.3 71.2 %collective-permute-start.22 = (bf16[288,2048]{1,0:T(8,128)(2,1)}, bf16[288,2048]{1,0:T(8,128)(2,1)}, u32[]{:S(2)}, u32[]{:S(2)}) collective-permute-start(bf16[288,2048]{1,0:T(8,128)(2,1)} %collective-permute-done.20.refs_1_), channel_id=1, source_target_pairs={{0,1},{1,2},{2,3},{3,0},{4,5},{5,6},{6,7},{7,4},{8,9},{9,10},{10,1... | collective-permute-start | bytes 3538952 | tf_op jit(solution)/shard_map/ppermute | solution.py:26
  366.9 99.8 %collective-permute-start.30 = (bf16[256,4096]{1,0:T(8,128)(2,1)}, bf16[256,4096]{1,0:T(8,128)(2,1)}, u32[]{:S(2)}, u32[]{:S(2)}) collective-permute-start(bf16[256,4096]{1,0:T(8,128)(2,1)} %refs_6_), channel_id=1, source_target_pairs={{0,4},{4,0},{8,12},{12,8},{16,20},{20,16},{24,28},{28,24},{1,5},{5... | collective-permute-start | bytes 6291464 | tf_op jit(solution)/shard_map/ppermute | solution.py:38
  393.4 73.3 %collective-permute-start.33 = (bf16[256,4096]{1,0:T(8,128)(2,1)}, bf16[256,4096]{1,0:T(8,128)(2,1)}, u32[]{:S(2)}, u32[]{:S(2)}) collective-permute-start(bf16[256,4096]{1,0:T(8,128)(2,1)} %collective-permute-done.29.refs_9_), channel_id=1, source_target_pairs={{0,4},{4,0},{8,12},{12,8},{16,20},{20,16},{24,28},{28,24},{1,5},{5... | collective-permute-start | bytes 6291464 | tf_op jit(solution)/shard_map/ppermute | solution.py:38
  393.4 73.3 %collective-permute-start.32 = (bf16[256,4096]{1,0:T(8,128)(2,1)}, bf16[256,4096]{1,0:T(8,128)(2,1)}, u32[]{:S(2)}, u32[]{:S(2)}) collective-permute-start(bf16[256,4096]{1,0:T(8,128)(2,1)} %collective-permute-done.28.refs_8_), channel_id=1, source_target_pairs={{0,4},{4,0},{8,12},{12,8},{16,20},{20,16},{24,28},{28,24},{1,5},{5... | collective-permute-start | bytes 6291464 | tf_op jit(solution)/shard_map/ppermute | solution.py:38
  393.9 72.8 %collective-permute-start.31 = (bf16[256,4096]{1,0:T(8,128)(2,1)}, bf16[256,4096]{1,0:T(8,128)(2,1)}, u32[]{:S(2)}, u32[]{:S(2)}) collective-permute-start(bf16[256,4096]{1,0:T(8,128)(2,1)} %collective-permute-done.27.refs_7_), channel_id=1, source_target_pairs={{0,4},{4,0},{8,12},{12,8},{16,20},{20,16},{24,28},{28,24},{1,5},{5... | collective-permute-start | bytes 6291464 | tf_op jit(solution)/shard_map/ppermute | solution.py:38
  604.3 265.4 %reduce-scatter.11.cloned.1.call-start = ((), (), s32[]{:S(2)}) async-start(), calls=%async_computation.11 | async-start | bytes 14155776 | tf_op jit(solution)/shard_map/reduce_scatter | solution.py:576
  608.1 537.6 %reduce-scatter.7.cloned.1.call-start = ((), (), s32[]{:S(2)}) async-start(), calls=%async_computation.9 | async-start | bytes 18874368 | tf_op jit(solution)/shard_map/reduce_scatter | solution.py:576
  726.0 438.6 %reduce-scatter.9.cloned.1.call-start = ((), (), s32[]{:S(2)}) async-start(), calls=%async_computation.10 | async-start | bytes 18874368 | tf_op jit(solution)/shard_map/reduce_scatter | solution.py:576
  859.9 126.2 %collective-permute-start.41 = (bf16[1536,2560]{1,0:T(8,128)(2,1)}, bf16[1536,2560]{1,0:T(8,128)(2,1)}, u32[]{:S(2)}, u32[]{:S(2)}) collective-permute-start(bf16[1536,2560]{1,0:T(8,128)(2,1)} %convolution_convert_fusion.4), channel_id=1, source_target_pairs={{0,4},{4,0},{8,12},{12,8},{16,20},{20,16},{24,28},{28,24},{1,5},{5... | collective-permute-start | bytes 23592968 | tf_op jit(solution)/shard_map/ppermute | solution.py:38
  864.6 59.1 %collective-permute-start.44 = (bf16[256,3072]{1,0:T(8,128)(2,1)}, bf16[256,3072]{1,0:T(8,128)(2,1)}, u32[]{:S(2)}, u32[]{:S(2)}) collective-permute-start(bf16[256,3072]{1,0:T(8,128)(2,1)} %get-tuple-element.283), channel_id=1, source_target_pairs={{0,24},{4,28},{8,16},{12,20},{16,8},{20,12},{24,0},{28,4},{1,25},{... | collective-permute-start | bytes 4718600 | tf_op jit(solution)/shard_map/ppermute | solution.py:120
  867.6 102.8 %collective-permute-start.43 = (bf16[256,3072]{1,0:T(8,128)(2,1)}, bf16[256,3072]{1,0:T(8,128)(2,1)}, u32[]{:S(2)}, u32[]{:S(2)}) collective-permute-start(bf16[256,3072]{1,0:T(8,128)(2,1)} %get-tuple-element.284), channel_id=1, source_target_pairs={{0,16},{4,20},{8,24},{12,28},{16,0},{20,4},{24,8},{28,12},{1,17},{... | collective-permute-start | bytes 4718600 | tf_op jit(solution)/shard_map/ppermute | solution.py:120
  867.6 102.8 %collective-permute-start.42 = (bf16[256,3072]{1,0:T(8,128)(2,1)}, bf16[256,3072]{1,0:T(8,128)(2,1)}, u32[]{:S(2)}, u32[]{:S(2)}) collective-permute-start(bf16[256,3072]{1,0:T(8,128)(2,1)} %get-tuple-element.285), channel_id=1, source_target_pairs={{0,8},{4,12},{8,0},{12,4},{16,24},{20,28},{24,16},{28,20},{1,9},{5... | collective-permute-start | bytes 4718600 | tf_op jit(solution)/shard_map/ppermute | solution.py:120
  996.9 130.6 %collective-permute-start.51 = (bf16[392,2560]{1,0:T(8,128)(2,1)S(1)}, bf16[392,2560]{1,0:T(8,128)(2,1)S(1)}, u32[]{:S(2)}, u32[]{:S(2)}) collective-permute-start(bf16[392,2560]{1,0:T(8,128)(2,1)S(1)} %get-tuple-element.140), channel_id=1, source_target_pairs={{0,24},{4,28},{8,16},{12,20},{16,8},{20,12},{24,0},{28,4},{1,25},{... | collective-permute-start | bytes 6021128 | tf_op jit(solution)/shard_map/ppermute | solution.py:120
  1026.3 117.2 %collective-permute-start.48 = (bf16[280,2048]{1,0:T(8,128)(2,1)S(1)}, bf16[280,2048]{1,0:T(8,128)(2,1)}, u32[]{:S(2)}, u32[]{:S(2)}) collective-permute-start(bf16[280,2048]{1,0:T(8,128)(2,1)S(1)} %get-tuple-element.286), channel_id=1, source_target_pairs={{0,1},{1,2},{2,3},{3,0},{4,5},{5,6},{6,7},{7,4},{8,9},{9,10},{10,1... | collective-permute-start | bytes 3440648 | tf_op jit(solution)/shard_map/ppermute | solution.py:128
  1027.7 117.4 %collective-permute-start.47 = (bf16[280,2048]{1,0:T(8,128)(2,1)S(1)}, bf16[280,2048]{1,0:T(8,128)(2,1)}, u32[]{:S(2)}, u32[]{:S(2)}) collective-permute-start(bf16[280,2048]{1,0:T(8,128)(2,1)S(1)} %get-tuple-element.287), channel_id=1, source_target_pairs={{0,2},{1,3},{2,0},{3,1},{4,6},{5,7},{6,4},{7,5},{8,10},{9,11},{10,... | collective-permute-start | bytes 3440648 | tf_op jit(solution)/shard_map/ppermute | solution.py:128
  1044.0 101.5 %collective-permute-start.46 = (bf16[280,2048]{1,0:T(8,128)(2,1)S(1)}, bf16[280,2048]{1,0:T(8,128)(2,1)}, u32[]{:S(2)}, u32[]{:S(2)}) collective-permute-start(bf16[280,2048]{1,0:T(8,128)(2,1)S(1)} %get-tuple-element.288), channel_id=1, source_target_pairs={{0,3},{1,0},{2,1},{3,2},{4,7},{5,4},{6,5},{7,6},{8,11},{9,8},{10,9... | collective-permute-start | bytes 3440648 | tf_op jit(solution)/shard_map/ppermute | solution.py:128
  1131.0 75.5 %collective-permute-start.53 = (bf16[97,2560]{1,0:T(8,128)(2,1)}, bf16[97,2560]{1,0:T(8,128)(2,1)}, u32[]{:S(2)}, u32[]{:S(2)}) collective-permute-start(bf16[97,2560]{1,0:T(8,128)(2,1)} %pad_maximum_fusion.15), channel_id=1, source_target_pairs={{0,2},{1,3},{2,0},{3,1},{4,6},{5,7},{6,4},{7,5},{8,10},{9,11},{10,... | collective-permute-start | bytes 1489928 | tf_op jit(solution)/shard_map/ppermute | solution.py:128
  1134.3 72.2 %collective-permute-start.54 = (bf16[97,2560]{1,0:T(8,128)(2,1)}, bf16[97,2560]{1,0:T(8,128)(2,1)}, u32[]{:S(2)}, u32[]{:S(2)}) collective-permute-start(bf16[97,2560]{1,0:T(8,128)(2,1)} %pad_maximum_fusion.16), channel_id=1, source_target_pairs={{0,1},{1,2},{2,3},{3,0},{4,5},{5,6},{6,7},{7,4},{8,9},{9,10},{10,1... | collective-permute-start | bytes 1489928 | tf_op jit(solution)/shard_map/ppermute | solution.py:128
  1145.5 57.9 %collective-permute-start.56 = (bf16[64,3072]{1,0:T(8,128)(2,1)}, bf16[64,3072]{1,0:T(8,128)(2,1)}, u32[]{:S(2)}, u32[]{:S(2)}) collective-permute-start(bf16[64,3072]{1,0:T(8,128)(2,1)} %get-tuple-element.315), channel_id=1, source_target_pairs={{0,2},{1,3},{2,0},{3,1},{4,6},{5,7},{6,4},{7,5},{8,10},{9,11},{10,... | collective-permute-start | bytes 1179656 | tf_op jit(solution)/shard_map/ppermute | solution.py:128
  (154 other events, 3192.6 us)
Sparse Core Ops, SparseCore 0:
  11.4 121.7 all-gather.4
  158.2 144.0 all-gather.6
  304.7 125.8 all-gather.8
  432.3 89.8 all-gather.10
  604.4 115.9 reduce-scatter.4
  723.8 92.4 reduce-scatter.10
  819.8 185.3 reduce-scatter.6
  1008.8 155.8 reduce-scatter.8

commit v5 on v4

--- a/solution.py
+++ b/solution.py
@@ -79,15 +79,7 @@
     return jnp.bitwise_xor(rel, lax.axis_index("dp").astype(jnp.int32))
 
 
-def direct_gather(shard):
-    size = lax.axis_size("dp")
-    own = [shard]
-    for c in range(1, size // 2):
-        own.append(lax.ppermute(shard, "dp", [(d, d ^ (2 * c)) for d in range(size)]))
-    return own + [hop(piece, 1) for piece in own]
-
-
-def dp_gather(shard):
+def dp_gather(shard, hold=None):
     chips = lax.axis_size("dp") // 2
     half = shard.shape[0] // 2
     got = {0: [shard]}
@@ -105,6 +97,9 @@
         else:
             got[c] = [hop(top(c ^ high), 2 * high), hop(bottom(c ^ low), 2 * low)]
     own = [piece for c in range(chips) for piece in got[c]]
+    if hold is not None:
+        own, hold = lax.optimization_barrier((own, hold))
+        return own + [hop(piece, 1) for piece in own], hold
     return own + [hop(piece, 1) for piece in own]
 
 
@@ -198,6 +193,17 @@
         joint[rows:, start + narrow[0] : start + sum(narrow)] = act[:, there]
 
 
+def _unspread(count, order, joint, pre, act):
+    rows = pre.shape[0]
+    narrow = [value.shape[1] // count for value in (pre, act)]
+    for g in range(count):
+        start = g * sum(narrow)
+        there = pl.ds(pl.multiple_of(order[g] * narrow[0], narrow[0]), narrow[0])
+        pre[:, there] = joint[:rows, start : start + narrow[0]]
+        there = pl.ds(pl.multiple_of(order[g] * narrow[1], narrow[1]), narrow[1])
+        act[:, there] = joint[rows:, start + narrow[0] : start + sum(narrow)]
+
+
 def block_call(body, order, arrays, shapes):
     return pl.pallas_call(
         functools.partial(body, order.shape[0]),
@@ -222,6 +228,21 @@
     return block_call(_spread, order, [pre, act], [shape])[0]
 
 
+def unspread(joint, rows, wide, thin, order):
+    count = order.shape[0]
+    lines = joint.shape[0] - rows
+    if wide // count % 128 or thin // count % 128:
+        blocks = joint.reshape(joint.shape[0], count, -1)
+        upper = blocks[:rows, :, : wide // count].reshape(rows, wide)
+        lower = blocks[rows:, :, wide // count :].reshape(lines, thin)
+        return permute_columns([upper, lower], order, True)
+    shapes = [
+        jax.ShapeDtypeStruct((rows, wide), joint.dtype),
+        jax.ShapeDtypeStruct((lines, thin), joint.dtype),
+    ]
+    return block_call(_unspread, order, [joint], shapes)
+
+
 def inverse_rms(values):
     return lax.rsqrt(jnp.mean(values * values, axis=-1, keepdims=True) + NORM_EPS)
 
@@ -283,14 +304,10 @@
     return hidden.astype(BF16), gate_back.astype(BF16), up_back.astype(BF16)
 
 
-def _feed_forward_tile(groups, order, *refs):
-    pieces, (back_ref, gate_ref) = refs[:groups], refs[groups : groups + 2]
-    up_pieces = refs[groups + 2 : -5]
-    hidden_ref, gate_back_ref, up_back_ref, rows_ref, up_ref = refs[-5:]
+def _feed_forward_tile(groups, *refs):
+    pieces, (back_ref, gate_ref, up_ref) = refs[:groups], refs[groups : groups + 3]
+    hidden_ref, gate_back_ref, up_back_ref, rows_ref = refs[groups + 3 :]
     count = pieces[0].shape[0]
-    for g, piece in enumerate(up_pieces):
-        size = piece.shape[0]
-        up_ref[pl.ds(pl.multiple_of(order[g] * size, size), size), :] = piece[...]
     root, cube = 0.7978845608028654, 0.044715
 
     @pl.when(pl.program_id(0) == 0)
@@ -314,36 +331,28 @@
         up_back_ref[cut, :] = (back * active).astype(BF16)
 
 
-def feed_forward_kernel(order, pieces, hidden_back, gate, up_pieces, tile=512):
+def feed_forward_kernel(pieces, hidden_back, gate, up, tile=512):
     groups = len(pieces)
     count, width = pieces[0].shape
     total = groups * count
     units = gate.shape[1]
-    block = pl.BlockSpec((total, tile), lambda n, idx: (0, n))
-    weight = pl.BlockSpec((width, tile), lambda n, idx: (0, n))
-    part = pl.BlockSpec((width // len(up_pieces), tile), lambda n, idx: (0, n))
-    fixed = pl.BlockSpec((count, width), lambda n, idx: (0, 0), pipeline_mode=pl.Buffered(1))
+    block = pl.BlockSpec((total, tile), lambda n: (0, n))
+    weight = pl.BlockSpec((width, tile), lambda n: (0, n))
+    fixed = pl.BlockSpec((count, width), lambda n: (0, 0), pipeline_mode=pl.Buffered(1))
     return pl.pallas_call(
         functools.partial(_feed_forward_tile, groups),
-        grid_spec=pltpu.PrefetchScalarGridSpec(
-            num_scalar_prefetch=1,
-            grid=(units // tile,),
-            in_specs=[fixed] * groups + [block, weight] + [part] * len(up_pieces),
-            out_specs=[block] * 3
-            + [pl.BlockSpec((total, width), lambda n, idx: (0, 0)), weight],
-        ),
+        grid=(units // tile,),
+        in_specs=[fixed] * groups + [block, weight, weight],
+        out_specs=[block] * 3 + [pl.BlockSpec((total, width), lambda n: (0, 0))],
         out_shape=[jax.ShapeDtypeStruct((total, units), BF16)] * 3
-        + [
-            jax.ShapeDtypeStruct((total, width), BF16),
-            jax.ShapeDtypeStruct((width, units), BF16),
-        ],
+        + [jax.ShapeDtypeStruct((total, width), BF16)],
         compiler_params=pltpu.CompilerParams(vmem_limit_bytes=56 * 2**20),
         cost_estimate=pl.CostEstimate(
             flops=4 * total * width * units,
-            bytes_accessed=6 * width * units + 8 * total * units + 4 * total * width,
+            bytes_accessed=4 * width * units + 8 * total * units + 4 * total * width,
             transcendentals=total * units,
         ),
-    )(order, *pieces, hidden_back, gate, *up_pieces)
+    )(*pieces, hidden_back, gate, up)
 
 
 def _stacked_grads(rows, cots, gate_back, up_back, hidden, out):
@@ -431,24 +440,29 @@
         ],
         axis=0,
     )
-    qkv_full = lax.all_gather(qkv_own, ("dp", "mp"), axis=0, tiled=True)
-    act_stack = jnp.concatenate([act_gate, act_up, act_down.T], axis=0)
+    out_own = jnp.concatenate([pre_output, act_output], axis=1)
+
     def in_place(pieces):
         size = pieces[0].shape[0]
         twice = jnp.concatenate(pieces[::-1] * 2, axis=0)
         return lax.dynamic_slice_in_dim(twice, (groups - 1 - member) * size, groups * size, 0)
 
-    out_ring = ring_gather(jnp.concatenate([pre_output, act_output], axis=1))
+    qkv_ring = ring_gather(qkv_own)
+    out_ring = ring_gather(out_own)
+    qkv_block = jnp.concatenate(
+        [
+            in_place([piece[:pre_part] for piece in qkv_ring]),
+            in_place([piece[pre_part:] for piece in qkv_ring]),
+        ],
+        axis=0,
+    )
+    pre_block = groups * pre_part
     out_block = in_place(out_ring)
-    qkv_full, act_stack, out_block, up_own = lax.optimization_barrier(
-        (qkv_full, act_stack, out_block, pre_up)
-    )
-    up_pieces = direct_gather(up_own)
-    out_full = jnp.concatenate(dp_gather(out_block), axis=0)
-    qkv_full = qkv_full.reshape(ways * groups, -1, qkv_own.shape[1])
-    pre_qkv = qkv_full[:, :pre_part].reshape(width, -1)
-    act_qkv = qkv_full[:, pre_part:].reshape(act_width, -1)
+    gate_full = lax.all_gather(pre_gate, "dp", axis=0, tiled=True)
+    down_full = lax.all_gather(pre_down, "dp", axis=1, tiled=True)
+    act_stack = jnp.concatenate([act_gate, act_up, act_down.T], axis=0)
     act_flat_w = lax.all_gather(act_stack, "dp", axis=0, tiled=True)
+    up_full = lax.all_gather(after(pre_up, act_flat_w), "dp", axis=0, tiled=True)
     act_all = act_flat_w.reshape(ways, 3, -1, act_gate.shape[1])
     act_gate_full, act_up_full, act_down_full = (
         act_all[:, n].reshape(act_width, -1) for n in range(3)
@@ -472,6 +486,14 @@
     def ring_stack(value):
         return jnp.concatenate(ring_gather(value), axis=0)
 
+    cot_pieces = ring_gather(pad(cot_flat))
+    qkv_pieces, cot_pieces = dp_gather(qkv_block, cot_pieces)
+    qkv_full = jnp.concatenate(qkv_pieces, axis=0)
+    out_full = jnp.concatenate(dp_gather(out_block), axis=0)
+    cot_all = jnp.concatenate(cot_pieces, axis=0)
+    act_cot_all = ring_stack(act_final_back.astype(BF16))
+    hidden_back = mm_nt(cot_all, down_full).astype(BF16)
+
     local_pos = jnp.concatenate(
         [
             member * pre_rows + jnp.arange(pre_rows),
@@ -521,35 +543,22 @@
             axis=0,
         )
 
-    pre_normed, act_normed = stack(
-        rms_norm(pre_x, pre_attn_gain).astype(BF16), rms_norm(act_x, act_attn_gain).astype(BF16)
-    )
-    normed = spread(pre_normed, act_normed, order)
-
-    def project(columns):
-        return to_items(
-            jnp.concatenate(
-                [mm(pre_normed, pre_qkv[:, columns]), mm(act_normed, act_qkv[:, columns])], axis=0
-            )
-        )
-
-    keyval_raw = project(slice(query_width, None))
+    normed = spread(
+        *stack(
+            rms_norm(pre_x, pre_attn_gain).astype(BF16),
+            rms_norm(act_x, act_attn_gain).astype(BF16),
+        ),
+        order,
+    )
+    keyval_raw = to_items(mm(normed, qkv_full[:, query_width:]))
     keyval_rows = jnp.concatenate(
         [rotate(keyval_raw[..., :head_dim], cosine_tab, sine_tab), keyval_raw[..., head_dim:]],
         axis=-1,
     ).astype(BF16)
-    keyval_rows, gate_own, down_own = lax.optimization_barrier(
-        (keyval_rows, pre_gate, pre_down)
-    )
-    down_full = lax.all_gather(down_own, "dp", axis=1, tiled=True)
-    gate_full = lax.all_gather(gate_own, "dp", axis=0, tiled=True)
     all_keyval = jnp.concatenate(ring_gather(keyval_rows), axis=1)
-    cot_all = ring_stack(pad(cot_flat))
-    act_cot_all = ring_stack(act_final_back.astype(BF16))
-    hidden_back = mm_nt(cot_all, down_full).astype(BF16)
     key_rows = all_keyval[..., :head_dim]
     value_rows = all_keyval[..., head_dim:]
-    query_raw = project(slice(0, query_width))
+    query_raw = to_items(mm(normed, qkv_full[:, :query_width]))
     query_rows = rotate(
         query_raw.reshape(items, local_len, heads, head_dim),
         cosine_tab[:, None, :],
@@ -569,6 +578,11 @@
 
     act_second = rms_norm(act_mid, act_mlp_gain).astype(BF16)
     act_all_rows = jnp.concatenate(ring_gather(act_second, LOOSE), axis=0)
+    pre_second = pad(rms_norm(pre_mid, pre_mlp_gain).astype(BF16))
+    first_piece, hidden_back, act_all_rows = lax.optimization_barrier(
+        (ring(pre_second, 1), hidden_back, act_all_rows)
+    )
+    second_pieces = [pre_second, first_piece]
     slot_count = lax.dynamic_index_in_dim(hidden_counts, member, keepdims=False)
     slot_live = (jnp.arange(act_gate.shape[1]) < slot_count).astype(F32)
 
@@ -585,27 +599,29 @@
     act_second_part = split(mm_nt(act_gate_back, act_gate_full) + mm_nt(act_up_back, act_up_full))
     act_sum_part = split(mm_nt(act_hidden, act_down_full))
 
-    act_stacked = stacked_grads(
-        ways, act_all_rows, act_cot_all, act_gate_back, act_up_back, act_hidden
-    )
-    pre_second = pad(rms_norm(pre_mid, pre_mlp_gain).astype(BF16))
-    second_pieces = [pre_second]
-    for r in range(1, groups):
+    for r in range(2, groups):
         piece = ring(second_pieces[-1], 1)
-        if r == 1:
-            piece, hidden_back = lax.optimization_barrier((piece, hidden_back))
+        if r == 2:
+            piece, act_gate_back, act_up_back, act_hidden = lax.optimization_barrier(
+                (piece, act_gate_back, act_up_back, act_hidden)
+            )
+            act_stacked = stacked_grads(
+                ways, act_all_rows, act_cot_all, act_gate_back, act_up_back, act_hidden
+            )
         if r == groups - 1:
             piece = after(piece, act_stacked)
         second_pieces.append(piece)
     grad_act = scatter_sum(act_stacked, 0)
+
+    pre_hidden, pre_gate_back, pre_up_back, pre_all = feed_forward_kernel(
+        second_pieces, hidden_back, gate_full, up_full
+    )
+    gate_term = mm_tn(pre_all, pre_gate_back).astype(BF16)
+    gate_term, pre_up_back, grad_act = lax.optimization_barrier(
+        (gate_term, pre_up_back, grad_act)
+    )
     grad_act = grad_act.astype(F32).reshape(3, -1, act_gate.shape[1])
     grad_act_gate, grad_act_up, grad_act_down = grad_act[0], grad_act[1], grad_act[2].T
-
-    pre_hidden, pre_gate_back, pre_up_back, pre_all, up_full = feed_forward_kernel(
-        order, second_pieces, hidden_back, gate_full, up_pieces
-    )
-    gate_term = mm_tn(pre_all, pre_gate_back).astype(BF16)
-    gate_term, pre_up_back = lax.optimization_barrier((gate_term, pre_up_back))
     grad_pre_gate = scatter_sum(gate_term, 0)
     half = groups // 2 * padded
 
@@ -693,7 +709,6 @@
     back_rows, grad_pre_gate, out_sums = lax.optimization_barrier(
         (back_rows, grad_pre_gate, out_sums)
     )
-    out_arrived = send_blocks(out_sums)
     qkv_half = normed.shape[1] // 2
     qkv_own_part = mm_tn(normed[:, :qkv_half], back_rows).astype(BF16)
     qkv_other_part = mm_tn(normed[:, qkv_half:], back_rows).astype(BF16)
@@ -701,9 +716,10 @@
     act_final_low = (act_mid + act_sums).astype(BF16)
     action_pred = mm(act_final_low, action_head).reshape(pred_cot.shape) * live_mask
     grad_head = mm_tn(act_final_low, pred_back)
-    back_rows, out_arrived = lax.optimization_barrier((back_rows, out_arrived))
-    pre_normed_back = mm_nt(back_rows[:padded], pre_qkv)[:count]
-    act_normed_back = mm_nt(back_rows[padded:], act_qkv)[:act_count]
+    pre_normed_back, act_normed_back = unspread(
+        mm_nt(back_rows, qkv_full), padded, width, act_width, order
+    )
+    pre_normed_back, act_normed_back = pre_normed_back[:count], act_normed_back[:act_count]
     pre_x_part, grad_pre_attn_gain = rms_back(pre_x, pre_attn_gain, pre_normed_back)
     act_x_part, grad_act_attn_gain = rms_back(act_x, act_attn_gain, act_normed_back)
     prefix_grad = (pre_mid_grad + pre_x_part).reshape(prefix_tokens.shape)
@@ -731,10 +747,11 @@
         lines = lax.dynamic_slice_in_dim(small, start, groups, 0)
         lines = jnp.pad(lines, ((0, spare), (0, qkv_sums.shape[2] - small.shape[1])))
         sent_blocks.append(jnp.concatenate([qkv_sums[c], lines.astype(BF16)], axis=0))
-    sent_blocks, out_arrived, pre_hidden = lax.optimization_barrier(
-        (sent_blocks, out_arrived, pre_hidden)
+    sent_blocks, out_sums, pre_hidden = lax.optimization_barrier(
+        (sent_blocks, out_sums, pre_hidden)
     )
     arrived = send_blocks(sent_blocks)
+    out_arrived = send_blocks(out_sums)
     pre_sum_part = split(mm(pre_hidden, down_full).astype(BF16))
     sum_parts = [each[:count] for each in pre_sum_part]
     sums_arrived = send_members(sum_parts)

time: 1240 us -> 1270 us (1.024)
  starting transfers between devices: 57.6 us -> 88.3 us
    all_gather x3, waiting for transfers between devices: 118 us -> 0.01 us  [the longest x1 0.01 us: shards(): gate_full = lax.all_gather(pre_gate, 'dp', axis=0, tiled=True)]
    ppermute x19 -> x26, waiting for transfers between devices: 145 us -> 256 us  [send(): result = lax.ppermute(value, axis, pairs)]
    ppermute x9, waiting for transfers between devices: 21.6 us -> 122 us  [send_members(): lax.ppermute(parts[r], 'mp', [(d, (d - r) % size) for d in range(size)])]
    all_gather x1, waiting for transfers between devices: 36.5 us -> 2.73 us  [shards(): act_flat_w = lax.all_gather(act_stack, 'dp', axis=0, tiled=True)]
    unnamed x272 -> x319, local copies, waits for them, and re-layouts: 48.6 us -> 80.4 us
    ppermute x3 -> x0, waiting for transfers between devices: 26.4 us -> none  [direct_gather(): own.append(lax.ppermute(shard, 'dp', [(d, d ^ 2 * c) for d in range(size)]))]
    ppermute x9, starting transfers between devices: 16.7 us -> 41.4 us  [send_members(): lax.ppermute(parts[r], 'mp', [(d, (d - r) % size) for d in range(size)])]
    reduce_scatter x4, waiting for transfers between devices: 18.9 us -> 0.04 us  [scatter_sum(): lax.psum_scatter(value, 'dp', scatter_dimension=dimension, tiled=True)]
  transfers between devices with their start and end apart: 66 -> 71, of which waited for: 30 -> 32; matrix products, arithmetic and copies ran while one was open for 35% -> 36% of each run, Pallas kernels for 1% -> 5%
where the time goes in v5:
time: 1270 us; the launch traced here: 1260 us
  waiting for transfers between devices  595 us (47%)
  matrix products  301 us (24%)
  local copies, waits for them, and re-layouts  140 us (11%)
  starting transfers between devices  88.3 us (7%)
  other arithmetic  64.7 us (5%)
  Pallas kernels  58.2 us (5%)
  between operations  17 us (1%)
    ppermute x26, waiting for transfers between devices, send(): result = lax.ppermute(value, axis, pairs)  256 us
    ppermute x6, waiting for transfers between devices, send_blocks(): lax.ppermute(blocks[c].astype(BF16), 'dp', [(d, d ^ 2 * c) for d in range...  180 us
    dot_general x11, matrix products, mm_nt(): lax.dot_general(left, right, (((1,), (1,)), ((), ())), preferred_element_...  124 us
    ppermute x9, waiting for transfers between devices, send_members(): lax.ppermute(parts[r], 'mp', [(d, (d - r) % size) for d in range(size)])  122 us
    dot_general x8, matrix products, mm_tn(): lax.dot_general(left, right, (((0,), (0,)), ((), ())), preferred_element_...  116 us
    unnamed x319, local copies, waits for them, and re-layouts  80.4 us
    pallas_call x1, Pallas kernels, feed_forward_kernel(): pl.pallas_call(functools.partial(_feed_forward_tile, groups), grid=(units...  50.2 us
    dot_general x8, matrix products, mm(): lax.dot_general(left, right, (((1,), (0,)), ((), ())), preferred_element_...  46.2 us
  transfers between devices with their start and end apart: 71, of which 32 were waited for; matrix products, arithmetic and copies ran while one was open for 36% of the time, Pallas kernels for 5%

profile of v5, /device:TPU:0, one launch (start us, length us, event | category | flops | bytes accessed | tf_op | source)
XLA Modules:
  0.0 1265.0 jit_solution(6132754926925858265)
XLA Ops:
  35.4 9.0 collective-permute-done.1
  47.9 10.6 collective-permute-done.7
  93.5 8.7 collective-permute-done.10
  106.6 20.4 %collective-permute-done.9 = bf16[288,2048]{1,0:T(8,128)(2,1)} collective-permute-done((bf16[288,2048]{1,0:T(8,128)(2,1)S(1)}, bf16[288,2048]{1,0:T(8,128)(2,1)}, u32[]{:S(2)}, u32[]{:S(2)}) %collective-permute-start.9) | collective-permute-done | bytes 1179680 | tf_op jit(solution)/shard_map/ppermute | solution.py:26
  129.0 33.4 %collective-permute-done.4 = bf16[384,2560]{1,0:T(8,128)(2,1)S(1)} collective-permute-done((bf16[384,2560]{1,0:T(8,128)(2,1)S(1)}, bf16[384,2560]{1,0:T(8,128)(2,1)S(1)}, u32[]{:S(2)}, u32[]{:S(2)}) %collective-permute-start.4) | collective-permute-done | bytes 1966112 | tf_op jit(solution)/shard_map/ppermute | solution.py:26
  176.5 58.8 %collective-permute-done.24 = bf16[256,3072]{1,0:T(8,128)(2,1)} collective-permute-done((bf16[256,3072]{1,0:T(8,128)(2,1)}, bf16[256,3072]{1,0:T(8,128)(2,1)}, u32[]{:S(2)}, u32[]{:S(2)}) %collective-permute-start.24) | collective-permute-done | bytes 1572896 | tf_op jit(solution)/shard_map/ppermute | solution.py:26
  236.5 20.4 %collective-permute-done.5 = bf16[192,2560]{1,0:T(8,128)(2,1)S(1)} collective-permute-done((bf16[192,2560]{1,0:T(8,128)(2,1)S(1)}, bf16[192,2560]{1,0:T(8,128)(2,1)S(1)}, u32[]{:S(2)}, u32[]{:S(2)}) %collective-permute-start.5) | collective-permute-done | bytes 983072 | tf_op jit(solution)/shard_map/ppermute | solution.py:26
  279.8 15.0 %collective-permute-done.26 = bf16[128,3072]{1,0:T(8,128)(2,1)} collective-permute-done((bf16[128,3072]{1,0:T(8,128)(2,1)S(1)}, bf16[128,3072]{1,0:T(8,128)(2,1)}, u32[]{:S(2)}, u32[]{:S(2)}) %collective-permute-start.26) | collective-permute-done | bytes 786464 | tf_op jit(solution)/shard_map/ppermute | solution.py:26
  328.2 8.5 collective-permute-done.22
  356.2 8.9 fusion.109
  389.2 25.6 %convolution_convert_fusion.3.refs_4_ = bf16[1152,4096]{1,0:T(8,128)(2,1)} fusion(bf16[1152,2048]{1,0:T(8,128)(2,1)} %copy-done.80, bf16[4096,2048]{1,0:T(8,128)(2,1)} %all-gather.5.cloned.1.call-done), kind=kOutput, calls=%fused_computation.5 | convolution fusion | flops 19332071424 | bytes 30932992 | tf_op jit(solution)/shard_map/dot_general | solution.py:287
  420.7 18.1 %collective-permute-done.37.refs_2_ = bf16[288,2048]{1,0:T(8,128)(2,1)S(1)} collective-permute-done((bf16[288,2048]{1,0:T(8,128)(2,1)}, bf16[288,2048]{1,0:T(8,128)(2,1)S(1)}, u32[]{:S(2)}, u32[]{:S(2)}) %collective-permute-start.37) | collective-permute-done | bytes 1179680 | tf_op jit(solution)/shard_map/ppermute | solution.py:26
  448.8 23.0 %collective-permute-done.38.refs_3_ = bf16[288,2048]{1,0:T(8,128)(2,1)} collective-permute-done((bf16[288,2048]{1,0:T(8,128)(2,1)S(1)}, bf16[288,2048]{1,0:T(8,128)(2,1)}, u32[]{:S(2)}, u32[]{:S(2)}) %collective-permute-start.38) | collective-permute-done | bytes 1179680 | tf_op jit(solution)/shard_map/ppermute | solution.py:26
  471.8 50.2 %shard_map.394 = (bf16[1152,4096]{1,0:T(8,128)(2,1)}, bf16[1152,4096]{1,0:T(8,128)(2,1)}, bf16[1152,4096]{1,0:T(8,128)(2,1)}, bf16[1152,2048]{1,0:T(8,128)(2,1)}) custom-call(bf16[288,2048]{1,0:T(8,128)(2,1)} %copy-done.62, bf16[288,2048]{1,0:T(8,128)(2,1)} %collective-permute-done.33.refs_1_, bf16[288,2048]{1,0:T(8,128)(2,1)} %copy-done.122, ...), custom_call_target="tpu_custom_call" | custom-call | flops 38654705664 | bytes 80740352 | tf_op jit(solution)/shard_map/pallas_call | solution.py:342
  522.0 27.8 %convolution_convert_fusion.2 = bf16[2048,4096]{1,0:T(8,128)(2,1)} fusion(bf16[1152,2048]{1,0:T(8,128)(2,1)} %get-tuple-element.139, bf16[1152,4096]{1,0:T(8,128)(2,1)} %get-tuple-element.144), kind=kOutput, calls=%fused_computation.4 | convolution fusion | flops 19335741440 | bytes 30932992 | tf_op jit(solution)/shard_map/dot_general | solution.py:291
  561.8 18.6 %fusion.11 = f32[576,2048]{1,0:T(8,128)} fusion(bf16[2048,4096]{1,0:T(8,128)(2,1)} %all-gather.11.cloned.1.call-done.refs_6_, bf16[1152,4096]{1,0:T(8,128)(2,1)} %get-tuple-element.147), kind=kOutput, calls=%fused_computation.25 | convolution fusion | flops 9663676416 | bytes 26214400 | tf_op jit(solution)/shard_map/dot_general | solution.py:287
  580.4 17.7 %fusion.21 = f32[576,2048]{1,0:T(8,128)} fusion(f32[576,2048]{1,0:T(8,128)} %fusion.11, bf16[2048,4096]{1,0:T(8,128)(2,1)} %all-gather.9.cloned.1.call-done.refs_5_, bf16[1152,4096]{1,0:T(8,128)(2,1)} %get-tuple-element.144), kind=kOutput, calls=%fused_computation.39 | convolution fusion | flops 9664856064 | bytes 30932992 | tf_op jit(solution)/shard_map/dot_general | solution.py:287
  600.3 16.8 %fusion.7 = f32[576,2048]{1,0:T(8,128)} fusion(bf16[2048,4096]{1,0:T(8,128)(2,1)} %all-gather.11.cloned.1.call-done.refs_6_, bf16[1152,4096]{1,0:T(8,128)(2,1)} %get-tuple-element.147), kind=kOutput, calls=%fused_computation.21 | convolution fusion | flops 9663676416 | bytes 26214400 | tf_op jit(solution)/shard_map/dot_general | solution.py:287
  617.1 17.5 %fusion.24 = f32[576,2048]{1,0:T(8,128)} fusion(f32[576,2048]{1,0:T(8,128)} %fusion.7, bf16[2048,4096]{1,0:T(8,128)(2,1)} %all-gather.9.cloned.1.call-done.refs_5_, bf16[1152,4096]{1,0:T(8,128)(2,1)} %get-tuple-element.144), kind=kOutput, calls=%fused_computation.40 | convolution fusion | flops 9664856064 | bytes 30932992 | tf_op jit(solution)/shard_map/dot_general | solution.py:287
  636.8 28.1 %convolution_convert_fusion.1 = bf16[2048,4096]{1,0:T(8,128)(2,1)} fusion(bf16[1152,2048]{1,0:T(8,128)(2,1)} %get-tuple-element.139, bf16[1152,4096]{1,0:T(8,128)(2,1)} %get-tuple-element.147), kind=kOutput, calls=%fused_computation.3 | convolution fusion | flops 19335741440 | bytes 30932992 | tf_op jit(solution)/shard_map/dot_general | solution.py:291
  671.7 28.3 %convolution_convert_fusion = bf16[4096,2048]{1,0:T(8,128)(2,1)} fusion(bf16[1152,4096]{1,0:T(8,128)(2,1)} %get-tuple-element.157, bf16[1152,2048]{1,0:T(8,128)(2,1)} %copy-done.80), kind=kOutput, calls=%fused_computation.2 | convolution fusion | flops 19335741440 | bytes 30932992 | tf_op jit(solution)/shard_map/dot_general | solution.py:291
  709.2 7.9 convolution_convert_fusion.8.refs_0_
  794.6 9.3 fusion.114.joint
  812.5 10.2 add_convert_fusion
  845.7 49.0 %collective-permute-done.56 = bf16[256,3072]{1,0:T(8,128)(2,1)} collective-permute-done((bf16[256,3072]{1,0:T(8,128)(2,1)}, bf16[256,3072]{1,0:T(8,128)(2,1)}, u32[]{:S(2)}, u32[]{:S(2)}) %collective-permute-start.56) | collective-permute-done | bytes 1572896 | tf_op jit(solution)/shard_map/ppermute | solution.py:115
  895.5 25.6 %convolution_convert_fusion.6 = bf16[1152,2048]{1,0:T(8,128)(2,1)S(1)} fusion(bf16[1152,4096]{1,0:T(8,128)(2,1)} %get-tuple-element.157, bf16[4096,2048]{1,0:T(8,128)(2,1)} %all-gather.5.cloned.1.call-done), kind=kOutput, calls=%fused_computation.11 | convolution fusion | flops 19329712128 | bytes 30932992 | tf_op jit(solution)/shard_map/dot_general | solution.py:283
  924.4 131.0 %collective-permute-done.55 = bf16[256,3072]{1,0:T(8,128)(2,1)S(1)} collective-permute-done((bf16[256,3072]{1,0:T(8,128)(2,1)}, bf16[256,3072]{1,0:T(8,128)(2,1)S(1)}, u32[]{:S(2)}, u32[]{:S(2)}) %collective-permute-start.55) | collective-permute-done | bytes 1572896 | tf_op jit(solution)/shard_map/ppermute | solution.py:115
  1063.6 22.2 %collective-permute-done.50 = bf16[280,2048]{1,0:T(8,128)(2,1)} collective-permute-done((bf16[280,2048]{1,0:T(8,128)(2,1)}, bf16[280,2048]{1,0:T(8,128)(2,1)}, u32[]{:S(2)}, u32[]{:S(2)}) %collective-permute-start.50) | collective-permute-done | bytes 1146912 | tf_op jit(solution)/shard_map/ppermute | solution.py:123
  1085.8 48.1 %collective-permute-done.49 = bf16[280,2048]{1,0:T(8,128)(2,1)} collective-permute-done((bf16[280,2048]{1,0:T(8,128)(2,1)}, bf16[280,2048]{1,0:T(8,128)(2,1)}, u32[]{:S(2)}, u32[]{:S(2)}) %collective-permute-start.49) | collective-permute-done | bytes 1146912 | tf_op jit(solution)/shard_map/ppermute | solution.py:123
  1147.0 24.0 %collective-permute-start.58 = (bf16[97,2560]{1,0:T(8,128)(2,1)}, bf16[97,2560]{1,0:T(8,128)(2,1)}, u32[]{:S(2)}, u32[]{:S(2)}) collective-permute-start(bf16[97,2560]{1,0:T(8,128)(2,1)} %pad_maximum_fusion.14), channel_id=1, source_target_pairs={{0,2},{1,3},{2,0},{3,1},{4,6},{5,7},{6,4},{7,5},{8,10},{9,11},{10,... | collective-permute-start | bytes 1489928 | tf_op jit(solution)/shard_map/ppermute | solution.py:123
  1196.7 8.0 collective-permute-done.62
  1204.6 36.2 %collective-permute-done.61 = bf16[64,3072]{1,0:T(8,128)(2,1)} collective-permute-done((bf16[64,3072]{1,0:T(8,128)(2,1)}, bf16[64,3072]{1,0:T(8,128)(2,1)}, u32[]{:S(2)}, u32[]{:S(2)}) %collective-permute-start.61) | collective-permute-done | bytes 393248 | tf_op jit(solution)/shard_map/ppermute | solution.py:123
  (657 shorter events, 411.0 us)
Async XLA Ops:
  7.2 78.9 %all-gather.7.cloned.1.call-start = ((), (), s32[]{:S(2)}) async-start(), calls=%async_computation.5 | async-start | bytes 14155776 | tf_op jit(solution)/shard_map/all_gather | solution.py:464
  11.2 378.0 %all-gather.5.cloned.1.call-start = ((), (), s32[]{:S(2)}) async-start(), calls=%async_computation.4 | async-start | bytes 18874368 | tf_op jit(solution)/shard_map/all_gather | solution.py:462
  11.9 459.8 %all-gather.9.cloned.1.call-start = ((), (), s32[]{:S(2)}) async-start(), calls=%async_computation.6 | async-start | bytes 18874368 | tf_op jit(solution)/shard_map/all_gather | solution.py:461
  12.7 459.1 %all-gather.11.cloned.1.call-start = ((), (), s32[]{:S(2)}) async-start(), calls=%async_computation.7 | async-start | bytes 18874368 | tf_op jit(solution)/shard_map/all_gather | solution.py:465
  86.1 463.7 %reduce-scatter.5.cloned.1.call-start = ((), (), s32[]{:S(2)}) async-start(), calls=%async_computation.8 | async-start | bytes 14155776 | tf_op jit(solution)/shard_map/reduce_scatter | solution.py:590
  90.0 72.4 %collective-permute-start.4 = (bf16[384,2560]{1,0:T(8,128)(2,1)S(1)}, bf16[384,2560]{1,0:T(8,128)(2,1)S(1)}, u32[]{:S(2)}, u32[]{:S(2)}) collective-permute-start(bf16[384,2560]{1,0:T(8,128)(2,1)S(1)} %pad_maximum_fusion), channel_id=1, source_target_pairs={{0,16},{4,20},{8,24},{12,28},{16,0},{20,4},{24,8},{28,12},{1,17},{... | collective-permute-start | bytes 5898248 | tf_op jit(solution)/shard_map/ppermute | solution.py:26
  91.0 73.1 %collective-permute-start.3 = (bf16[384,2560]{1,0:T(8,128)(2,1)S(1)}, bf16[384,2560]{1,0:T(8,128)(2,1)S(1)}, u32[]{:S(2)}, u32[]{:S(2)}) collective-permute-start(bf16[384,2560]{1,0:T(8,128)(2,1)S(1)} %pad_maximum_fusion), channel_id=1, source_target_pairs={{0,8},{4,12},{8,0},{12,4},{16,24},{20,28},{24,16},{28,20},{1,9},{5... | collective-permute-start | bytes 5898248 | tf_op jit(solution)/shard_map/ppermute | solution.py:26
  127.0 46.5 %collective-permute-start.11 = (bf16[288,2048]{1,0:T(8,128)(2,1)}, bf16[288,2048]{1,0:T(8,128)(2,1)}, u32[]{:S(2)}, u32[]{:S(2)}) collective-permute-start(bf16[288,2048]{1,0:T(8,128)(2,1)} %collective-permute-done.9), channel_id=1, source_target_pairs={{0,1},{1,2},{2,3},{3,0},{4,5},{5,6},{6,7},{7,4},{8,9},{9,10},{10,1... | collective-permute-start | bytes 3538952 | tf_op jit(solution)/shard_map/ppermute | solution.py:26
  164.1 71.2 %collective-permute-start.24 = (bf16[256,3072]{1,0:T(8,128)(2,1)}, bf16[256,3072]{1,0:T(8,128)(2,1)}, u32[]{:S(2)}, u32[]{:S(2)}) collective-permute-start(bf16[256,3072]{1,0:T(8,128)(2,1)} %get-tuple-element.119), channel_id=1, source_target_pairs={{0,8},{4,12},{8,0},{12,4},{16,24},{20,28},{24,16},{28,20},{1,9},{5... | collective-permute-start | bytes 4718600 | tf_op jit(solution)/shard_map/ppermute | solution.py:26
  166.1 92.3 %collective-permute-start.25 = (bf16[256,3072]{1,0:T(8,128)(2,1)}, bf16[256,3072]{1,0:T(8,128)(2,1)}, u32[]{:S(2)}, u32[]{:S(2)}) collective-permute-start(bf16[256,3072]{1,0:T(8,128)(2,1)} %get-tuple-element.119), channel_id=1, source_target_pairs={{0,16},{4,20},{8,24},{12,28},{16,0},{20,4},{24,8},{28,12},{1,17},{... | collective-permute-start | bytes 4718600 | tf_op jit(solution)/shard_map/ppermute | solution.py:26
  169.2 91.3 %collective-permute-start.6 = (bf16[192,2560]{1,0:T(8,128)(2,1)S(1)}, bf16[192,2560]{1,0:T(8,128)(2,1)S(1)}, u32[]{:S(2)}, u32[]{:S(2)}) collective-permute-start(bf16[192,2560]{1,0:T(8,128)(2,1)S(1)} %slice.419), channel_id=1, source_target_pairs={{0,8},{4,12},{8,0},{12,4},{16,24},{20,28},{24,16},{28,20},{1,9},{5... | collective-permute-start | bytes 2949128 | tf_op jit(solution)/shard_map/ppermute | solution.py:26
  170.6 86.3 %collective-permute-start.5 = (bf16[192,2560]{1,0:T(8,128)(2,1)S(1)}, bf16[192,2560]{1,0:T(8,128)(2,1)S(1)}, u32[]{:S(2)}, u32[]{:S(2)}) collective-permute-start(bf16[192,2560]{1,0:T(8,128)(2,1)S(1)} %slice.418), channel_id=1, source_target_pairs={{0,16},{4,20},{8,24},{12,28},{16,0},{20,4},{24,8},{28,12},{1,17},{... | collective-permute-start | bytes 2949128 | tf_op jit(solution)/shard_map/ppermute | solution.py:26
  173.5 93.7 %collective-permute-start.12 = (bf16[288,2048]{1,0:T(8,128)(2,1)}, bf16[288,2048]{1,0:T(8,128)(2,1)S(1)}, u32[]{:S(2)}, u32[]{:S(2)}) collective-permute-start(bf16[288,2048]{1,0:T(8,128)(2,1)} %collective-permute-done.11), channel_id=1, source_target_pairs={{0,1},{1,2},{2,3},{3,0},{4,5},{5,6},{6,7},{7,4},{8,9},{9,10},{10,1... | collective-permute-start | bytes 3538952 | tf_op jit(solution)/shard_map/ppermute | solution.py:26
  235.3 38.4 %collective-permute-start.28 = (bf16[256,3072]{1,0:T(8,128)(2,1)}, bf16[256,3072]{1,0:T(8,128)(2,1)S(1)}, u32[]{:S(2)}, u32[]{:S(2)}) collective-permute-start(bf16[256,3072]{1,0:T(8,128)(2,1)} %get-tuple-element.119), channel_id=1, source_target_pairs={{0,4},{4,0},{8,12},{12,8},{16,20},{20,16},{24,28},{28,24},{1,5},{5... | collective-permute-start | bytes 4718600 | tf_op jit(solution)/shard_map/ppermute | solution.py:38
  258.4 36.4 %collective-permute-start.26 = (bf16[128,3072]{1,0:T(8,128)(2,1)S(1)}, bf16[128,3072]{1,0:T(8,128)(2,1)}, u32[]{:S(2)}, u32[]{:S(2)}) collective-permute-start(bf16[128,3072]{1,0:T(8,128)(2,1)S(1)} %slice.436), channel_id=1, source_target_pairs={{0,16},{4,20},{8,24},{12,28},{16,0},{20,4},{24,8},{28,12},{1,17},{... | collective-permute-start | bytes 2359304 | tf_op jit(solution)/shard_map/ppermute | solution.py:26
  378.3 36.6 %collective-permute-start.33 = (bf16[288,2048]{1,0:T(8,128)(2,1)S(1)}, bf16[288,2048]{1,0:T(8,128)(2,1)}, u32[]{:S(2)}, u32[]{:S(2)}) collective-permute-start(bf16[288,2048]{1,0:T(8,128)(2,1)S(1)} %pad.59.refs_0_), channel_id=1, source_target_pairs={{0,1},{1,2},{2,3},{3,0},{4,5},{5,6},{6,7},{7,4},{8,9},{9,10},{10,1... | collective-permute-start | bytes 3538952 | tf_op jit(solution)/shard_map/ppermute | solution.py:26
  448.5 333.9 %reduce-scatter.7.cloned.1.call-start = ((), (), s32[]{:S(2)}) async-start(), calls=%async_computation.9 | async-start | bytes 18874368 | tf_op jit(solution)/shard_map/reduce_scatter | solution.py:590
  549.8 513.7 %reduce-scatter.9.cloned.1.call-start = ((), (), s32[]{:S(2)}) async-start(), calls=%async_computation.10 | async-start | bytes 18874368 | tf_op jit(solution)/shard_map/reduce_scatter | solution.py:590
  665.0 398.6 %reduce-scatter.11.cloned.1.call-start = ((), (), s32[]{:S(2)}) async-start(), calls=%async_computation.11 | async-start | bytes 18874368 | tf_op jit(solution)/shard_map/reduce_scatter | solution.py:590
  725.6 49.2 %collective-permute-start.45 = (bf16[1024,3072]{1,0:T(8,128)(2,1)}, bf16[1024,3072]{1,0:T(8,128)(2,1)}, u32[]{:S(2)}, u32[]{:S(2)}) collective-permute-start(bf16[1024,3072]{1,0:T(8,128)(2,1)} %convolution_convert_fusion.7), channel_id=1, source_target_pairs={{0,4},{4,0},{8,12},{12,8},{16,20},{20,16},{24,28},{28,24},{1,5},{5... | collective-permute-start | bytes 18874376 | tf_op jit(solution)/shard_map/ppermute | solution.py:38
  831.9 62.8 %collective-permute-start.56 = (bf16[256,3072]{1,0:T(8,128)(2,1)}, bf16[256,3072]{1,0:T(8,128)(2,1)}, u32[]{:S(2)}, u32[]{:S(2)}) collective-permute-start(bf16[256,3072]{1,0:T(8,128)(2,1)} %get-tuple-element.307), channel_id=1, source_target_pairs={{0,24},{4,28},{8,16},{12,20},{16,8},{20,12},{24,0},{28,4},{1,25},{... | collective-permute-start | bytes 4718600 | tf_op jit(solution)/shard_map/ppermute | solution.py:115
  842.2 217.1 %collective-permute-start.51 = (bf16[392,2560]{1,0:T(8,128)(2,1)S(1)}, bf16[392,2560]{1,0:T(8,128)(2,1)S(1)}, u32[]{:S(2)}, u32[]{:S(2)}) collective-permute-start(bf16[392,2560]{1,0:T(8,128)(2,1)S(1)} %copy-done.47), channel_id=1, source_target_pairs={{0,8},{4,12},{8,0},{12,4},{16,24},{20,28},{24,16},{28,20},{1,9},{5... | collective-permute-start | bytes 6021128 | tf_op jit(solution)/shard_map/ppermute | solution.py:115
  842.2 218.5 %collective-permute-start.52 = (bf16[392,2560]{1,0:T(8,128)(2,1)S(1)}, bf16[392,2560]{1,0:T(8,128)(2,1)S(1)}, u32[]{:S(2)}, u32[]{:S(2)}) collective-permute-start(bf16[392,2560]{1,0:T(8,128)(2,1)S(1)} %copy-done.46), channel_id=1, source_target_pairs={{0,16},{4,20},{8,24},{12,28},{16,0},{20,4},{24,8},{28,12},{1,17},{... | collective-permute-start | bytes 6021128 | tf_op jit(solution)/shard_map/ppermute | solution.py:115
  842.8 217.8 %collective-permute-start.53 = (bf16[392,2560]{1,0:T(8,128)(2,1)S(1)}, bf16[392,2560]{1,0:T(8,128)(2,1)S(1)}, u32[]{:S(2)}, u32[]{:S(2)}) collective-permute-start(bf16[392,2560]{1,0:T(8,128)(2,1)S(1)} %copy-done.45), channel_id=1, source_target_pairs={{0,24},{4,28},{8,16},{12,20},{16,8},{20,12},{24,0},{28,4},{1,25},{... | collective-permute-start | bytes 6021128 | tf_op jit(solution)/shard_map/ppermute | solution.py:115
  845.6 209.7 %collective-permute-start.55 = (bf16[256,3072]{1,0:T(8,128)(2,1)}, bf16[256,3072]{1,0:T(8,128)(2,1)S(1)}, u32[]{:S(2)}, u32[]{:S(2)}) collective-permute-start(bf16[256,3072]{1,0:T(8,128)(2,1)} %get-tuple-element.308), channel_id=1, source_target_pairs={{0,16},{4,20},{8,24},{12,28},{16,0},{20,4},{24,8},{28,12},{1,17},{... | collective-permute-start | bytes 4718600 | tf_op jit(solution)/shard_map/ppermute | solution.py:115
  894.7 160.7 %collective-permute-start.54 = (bf16[256,3072]{1,0:T(8,128)(2,1)}, bf16[256,3072]{1,0:T(8,128)(2,1)S(1)}, u32[]{:S(2)}, u32[]{:S(2)}) collective-permute-start(bf16[256,3072]{1,0:T(8,128)(2,1)} %get-tuple-element.309), channel_id=1, source_target_pairs={{0,8},{4,12},{8,0},{12,4},{16,24},{20,28},{24,16},{28,20},{1,9},{5... | collective-permute-start | bytes 4718600 | tf_op jit(solution)/shard_map/ppermute | solution.py:115
  1055.4 78.5 %collective-permute-start.49 = (bf16[280,2048]{1,0:T(8,128)(2,1)}, bf16[280,2048]{1,0:T(8,128)(2,1)}, u32[]{:S(2)}, u32[]{:S(2)}) collective-permute-start(bf16[280,2048]{1,0:T(8,128)(2,1)} %get-tuple-element.311), channel_id=1, source_target_pairs={{0,2},{1,3},{2,0},{3,1},{4,6},{5,7},{6,4},{7,5},{8,10},{9,11},{10,... | collective-permute-start | bytes 3440648 | tf_op jit(solution)/shard_map/ppermute | solution.py:123
  1059.3 74.6 %collective-permute-start.48 = (bf16[280,2048]{1,0:T(8,128)(2,1)}, bf16[280,2048]{1,0:T(8,128)(2,1)}, u32[]{:S(2)}, u32[]{:S(2)}) collective-permute-start(bf16[280,2048]{1,0:T(8,128)(2,1)} %get-tuple-element.312), channel_id=1, source_target_pairs={{0,3},{1,0},{2,1},{3,2},{4,7},{5,4},{6,5},{7,6},{8,11},{9,8},{10,9... | collective-permute-start | bytes 3440648 | tf_op jit(solution)/shard_map/ppermute | solution.py:123
  1147.0 96.8 %collective-permute-start.58 = (bf16[97,2560]{1,0:T(8,128)(2,1)}, bf16[97,2560]{1,0:T(8,128)(2,1)}, u32[]{:S(2)}, u32[]{:S(2)}) collective-permute-start(bf16[97,2560]{1,0:T(8,128)(2,1)} %pad_maximum_fusion.14), channel_id=1, source_target_pairs={{0,2},{1,3},{2,0},{3,1},{4,6},{5,7},{6,4},{7,5},{8,10},{9,11},{10,... | collective-permute-start | bytes 1489928 | tf_op jit(solution)/shard_map/ppermute | solution.py:123
  1178.5 62.3 %collective-permute-start.61 = (bf16[64,3072]{1,0:T(8,128)(2,1)}, bf16[64,3072]{1,0:T(8,128)(2,1)}, u32[]{:S(2)}, u32[]{:S(2)}) collective-permute-start(bf16[64,3072]{1,0:T(8,128)(2,1)} %get-tuple-element.339), channel_id=1, source_target_pairs={{0,2},{1,3},{2,0},{3,1},{4,6},{5,7},{6,4},{7,5},{8,10},{9,11},{10,... | collective-permute-start | bytes 1179656 | tf_op jit(solution)/shard_map/ppermute | solution.py:123
  1179.9 64.0 %collective-permute-start.59 = (bf16[97,2560]{1,0:T(8,128)(2,1)}, bf16[97,2560]{1,0:T(8,128)(2,1)}, u32[]{:S(2)}, u32[]{:S(2)}) collective-permute-start(bf16[97,2560]{1,0:T(8,128)(2,1)} %pad_maximum_fusion.15), channel_id=1, source_target_pairs={{0,1},{1,2},{2,3},{3,0},{4,5},{5,6},{6,7},{7,4},{8,9},{9,10},{10,1... | collective-permute-start | bytes 1489928 | tf_op jit(solution)/shard_map/ppermute | solution.py:123
  1192.5 58.9 %collective-permute-start.57 = (bf16[97,2560]{1,0:T(8,128)(2,1)S(1)}, bf16[97,2560]{1,0:T(8,128)(2,1)S(1)}, u32[]{:S(2)}, u32[]{:S(2)}) collective-permute-start(bf16[97,2560]{1,0:T(8,128)(2,1)S(1)} %pad_maximum_fusion.13), channel_id=1, source_target_pairs={{0,3},{1,0},{2,1},{3,2},{4,7},{5,4},{6,5},{7,6},{8,11},{9,8},{10,9... | collective-permute-start | bytes 1489928 | tf_op jit(solution)/shard_map/ppermute | solution.py:123
  (169 other events, 3046.2 us)
Sparse Core Ops, SparseCore 0:
  11.3 74.8 all-gather.6
  88.0 155.5 all-gather.4
  245.5 106.8 all-gather.8
  354.2 89.8 all-gather.10
  448.6 91.1 reduce-scatter.4
  550.0 113.2 reduce-scatter.6
  666.8 115.9 reduce-scatter.8
  786.3 260.3 reduce-scatter.10

commit v6 on v5

--- a/solution.py
+++ b/solution.py
@@ -109,12 +109,22 @@
     return total.reshape(chips, -1, own.shape[1])
 
 
-def send_blocks(blocks):
+def chips_sum(blocks):
     size = lax.axis_size("dp")
-    return [
-        lax.ppermute(blocks[c].astype(BF16), "dp", [(d, d ^ (2 * c)) for d in range(size)])
-        for c in range(1, size // 2)
-    ]
+    cut = blocks[0].shape[0] // 16 * 8
+    bits = [1 << n for n in range((size // 2).bit_length() - 1)]
+    halves = []
+    for rows, turns in ((slice(0, cut), bits), (slice(cut, None), bits[::-1])):
+        kept = {c: block[rows].astype(F32) for c, block in enumerate(blocks)}
+        for bit in turns:
+            sent = sorted(c for c in kept if c & bit)
+            moved = jnp.concatenate([kept.pop(c).astype(BF16) for c in sent], axis=0)
+            moved = lax.ppermute(moved, "dp", [(d, d ^ (2 * bit)) for d in range(size)])
+            lines = moved.shape[0] // len(sent)
+            for n, c in enumerate(sent):
+                kept[c ^ bit] = kept[c ^ bit] + moved[n * lines : (n + 1) * lines].astype(F32)
+        halves.append(kept[0])
+    return jnp.concatenate(halves, axis=0)
 
 
 def send_members(parts):
@@ -653,10 +663,14 @@
             moved, up_term, pre_hidden = lax.optimization_barrier((moved, up_term, pre_hidden))
             down_term = mm_tn(pre_hidden, cot_all).astype(BF16)
         elif r == groups - 4:
-            moved, down_term = lax.optimization_barrier((moved, down_term))
+            down_term, pre_hidden = lax.optimization_barrier((down_term, pre_hidden))
+            pre_sum_part = mm(pre_hidden, down_full).astype(BF16)
+            moved, pre_sum_part = lax.optimization_barrier((moved, pre_sum_part))
         total = moved.astype(F32) + second_part(r)
     grad_pre_up = scatter_sum(up_term, 0)
     grad_pre_down = scatter_sum(down_term, 1)
+    sum_parts = [each[:count] for each in split(pre_sum_part)]
+    sums_arrived = send_members(sum_parts)
     pre_second_back = total[:count]
     act_second_back = total[count : count + act_lines].reshape(act_count, act_width)
     act_sums = total[count + act_lines :].reshape(act_count, act_width)
@@ -747,30 +761,20 @@
         lines = lax.dynamic_slice_in_dim(small, start, groups, 0)
         lines = jnp.pad(lines, ((0, spare), (0, qkv_sums.shape[2] - small.shape[1])))
         sent_blocks.append(jnp.concatenate([qkv_sums[c], lines.astype(BF16)], axis=0))
-    sent_blocks, out_sums, pre_hidden = lax.optimization_barrier(
-        (sent_blocks, out_sums, pre_hidden)
-    )
-    arrived = send_blocks(sent_blocks)
-    out_arrived = send_blocks(out_sums)
-    pre_sum_part = split(mm(pre_hidden, down_full).astype(BF16))
-    sum_parts = [each[:count] for each in pre_sum_part]
-    sums_arrived = send_members(sum_parts)
-    arrived, out_arrived = lax.optimization_barrier((arrived, out_arrived))
-    qkv_parts = member_parts(
-        add_up(sent_blocks[0].astype(F32), arrived).astype(BF16), (pre_part, act_part, 1)
-    )
+    sent_blocks, out_sums = lax.optimization_barrier((sent_blocks, out_sums))
+    qkv_total = chips_sum(sent_blocks)
+    out_total = chips_sum([out_sums[c] for c in range(ways // 2)])
+    qkv_parts = member_parts(qkv_total.astype(BF16), (pre_part, act_part, 1))
     qkv_arrived = send_members(qkv_parts)
-    out_parts = member_parts(
-        add_up(out_sums[0].astype(F32), out_arrived).astype(BF16), (out_part,)
-    )
+    out_parts = member_parts(out_total.astype(BF16), (out_part,))
     out_arrived = send_members(out_parts)
-    sums_arrived, grad_pre_up, grad_pre_down, qkv_first = lax.optimization_barrier(
-        (sums_arrived, grad_pre_up, grad_pre_down, qkv_parts[0])
+    qkv_arrived, sums_arrived, grad_pre_up, grad_pre_down = lax.optimization_barrier(
+        (qkv_arrived, sums_arrived, grad_pre_up, grad_pre_down)
     )
     pre_sums = add_up(sum_parts[0].astype(F32), sums_arrived)
     prefix_out = (pre_mid + pre_sums).astype(BF16).reshape(prefix_tokens.shape)
     grad_out = add_up(out_parts[0].astype(F32), out_arrived)
-    grad_qkv = add_up(qkv_first.astype(F32), qkv_arrived)
+    grad_qkv = add_up(qkv_parts[0].astype(F32), qkv_arrived)
     total = grad_qkv[pre_part + act_part :, : small.shape[1]]
     sizes = [width // devices] * 2 + [act_width // devices] * 2
     gains, start = [], 0

time: 1270 us -> 1150 us (0.906)
  waiting for transfers between devices: 595 us -> 459 us
    ppermute x9, waiting for transfers between devices: 122 us -> 35.9 us  [send_members(): lax.ppermute(parts[r], 'mp', [(d, (d - r) % size) for d in range(size)])]
    ppermute x6 -> x8, waiting for transfers between devices: 180 us -> 126 us  [chips_sum(): moved = lax.ppermute(moved, 'dp', [(d, d ^ 2 * bit) for d in range(size)])]
    unnamed x319 -> x337, local copies, waits for them, and re-layouts: 80.4 us -> 82.4 us
  transfers between devices with their start and end apart: 71 -> 73, of which waited for: 32 -> 35; matrix products, arithmetic and copies ran while one was open for 36% -> 39% of each run, Pallas kernels for 5% -> 5%
where the time goes in v6:
time: 1150 us; the launch traced here: 1140 us
  waiting for transfers between devices  459 us (40%)
  matrix products  299 us (26%)
  local copies, waits for them, and re-layouts  138 us (12%)
  starting transfers between devices  94.2 us (8%)
  other arithmetic  70.8 us (6%)
  Pallas kernels  59 us (5%)
  between operations  16.9 us (1%)
    ppermute x26, waiting for transfers between devices, send(): result = lax.ppermute(value, axis, pairs)  257 us
    ppermute x8, waiting for transfers between devices, chips_sum(): moved = lax.ppermute(moved, 'dp', [(d, d ^ 2 * bit) for d in range(size)])  126 us
    dot_general x11, matrix products, mm_nt(): lax.dot_general(left, right, (((1,), (1,)), ((), ())), preferred_element_...  123 us
    dot_general x8, matrix products, mm_tn(): lax.dot_general(left, right, (((0,), (0,)), ((), ())), preferred_element_...  116 us
    unnamed x337, local copies, waits for them, and re-layouts  82.4 us
    pallas_call x1, Pallas kernels, feed_forward_kernel(): pl.pallas_call(functools.partial(_feed_forward_tile, groups), grid=(units...  51 us
    dot_general x8, matrix products, mm(): lax.dot_general(left, right, (((1,), (0,)), ((), ())), preferred_element_...  48.2 us
    ppermute x9, starting transfers between devices, send_members(): lax.ppermute(parts[r], 'mp', [(d, (d - r) % size) for d in range(size)])  47.8 us
  transfers between devices with their start and end apart: 73, of which 35 were waited for; matrix products, arithmetic and copies ran while one was open for 39% of the time, Pallas kernels for 5%

profile of v6, /device:TPU:0, one launch (start us, length us, event | category | flops | bytes accessed | tf_op | source)
XLA Modules:
  0.0 1136.8 jit_solution(17331847666715197893)
XLA Ops:
  35.0 9.3 collective-permute-done.1
  46.2 12.3 %collective-permute-done.7 = bf16[64,3072]{1,0:T(8,128)(2,1)} collective-permute-done((bf16[64,3072]{1,0:T(8,128)(2,1)}, bf16[64,3072]{1,0:T(8,128)(2,1)}, u32[]{:S(2)}, u32[]{:S(2)}) %collective-permute-start.7) | collective-permute-done | bytes 393248 | tf_op jit(solution)/shard_map/ppermute | solution.py:26
  93.4 8.7 collective-permute-done.10
  106.5 20.4 %collective-permute-done.9 = bf16[288,2048]{1,0:T(8,128)(2,1)} collective-permute-done((bf16[288,2048]{1,0:T(8,128)(2,1)S(1)}, bf16[288,2048]{1,0:T(8,128)(2,1)}, u32[]{:S(2)}, u32[]{:S(2)}) %collective-permute-start.9) | collective-permute-done | bytes 1179680 | tf_op jit(solution)/shard_map/ppermute | solution.py:26
  128.9 33.4 %collective-permute-done.4 = bf16[384,2560]{1,0:T(8,128)(2,1)S(1)} collective-permute-done((bf16[384,2560]{1,0:T(8,128)(2,1)S(1)}, bf16[384,2560]{1,0:T(8,128)(2,1)S(1)}, u32[]{:S(2)}, u32[]{:S(2)}) %collective-permute-start.4) | collective-permute-done | bytes 1966112 | tf_op jit(solution)/shard_map/ppermute | solution.py:26
  175.8 59.4 %collective-permute-done.24 = bf16[256,3072]{1,0:T(8,128)(2,1)} collective-permute-done((bf16[256,3072]{1,0:T(8,128)(2,1)}, bf16[256,3072]{1,0:T(8,128)(2,1)}, u32[]{:S(2)}, u32[]{:S(2)}) %collective-permute-start.24) | collective-permute-done | bytes 1572896 | tf_op jit(solution)/shard_map/ppermute | solution.py:26
  236.4 20.4 %collective-permute-done.5 = bf16[192,2560]{1,0:T(8,128)(2,1)S(1)} collective-permute-done((bf16[192,2560]{1,0:T(8,128)(2,1)S(1)}, bf16[192,2560]{1,0:T(8,128)(2,1)S(1)}, u32[]{:S(2)}, u32[]{:S(2)}) %collective-permute-start.5) | collective-permute-done | bytes 983072 | tf_op jit(solution)/shard_map/ppermute | solution.py:26
  279.7 15.0 %collective-permute-done.26 = bf16[128,3072]{1,0:T(8,128)(2,1)} collective-permute-done((bf16[128,3072]{1,0:T(8,128)(2,1)S(1)}, bf16[128,3072]{1,0:T(8,128)(2,1)}, u32[]{:S(2)}, u32[]{:S(2)}) %collective-permute-start.26) | collective-permute-done | bytes 786464 | tf_op jit(solution)/shard_map/ppermute | solution.py:26
  357.3 9.5 fusion.128
  390.6 25.7 %convolution_convert_fusion.3.refs_4_ = bf16[1152,4096]{1,0:T(8,128)(2,1)} fusion(bf16[1152,2048]{1,0:T(8,128)(2,1)} %copy-done.81, bf16[4096,2048]{1,0:T(8,128)(2,1)} %all-gather.5.cloned.1.call-done), kind=kOutput, calls=%fused_computation.5 | convolution fusion | flops 19332071424 | bytes 30932992 | tf_op jit(solution)/shard_map/dot_general | solution.py:297
  422.4 17.4 %collective-permute-done.37.refs_2_ = bf16[288,2048]{1,0:T(8,128)(2,1)S(1)} collective-permute-done((bf16[288,2048]{1,0:T(8,128)(2,1)}, bf16[288,2048]{1,0:T(8,128)(2,1)S(1)}, u32[]{:S(2)}, u32[]{:S(2)}) %collective-permute-start.37) | collective-permute-done | bytes 1179680 | tf_op jit(solution)/shard_map/ppermute | solution.py:26
  452.1 22.5 %collective-permute-done.38.refs_3_ = bf16[288,2048]{1,0:T(8,128)(2,1)} collective-permute-done((bf16[288,2048]{1,0:T(8,128)(2,1)S(1)}, bf16[288,2048]{1,0:T(8,128)(2,1)}, u32[]{:S(2)}, u32[]{:S(2)}) %collective-permute-start.38) | collective-permute-done | bytes 1179680 | tf_op jit(solution)/shard_map/ppermute | solution.py:26
  474.6 51.0 %shard_map.394 = (bf16[1152,4096]{1,0:T(8,128)(2,1)}, bf16[1152,4096]{1,0:T(8,128)(2,1)}, bf16[1152,4096]{1,0:T(8,128)(2,1)}, bf16[1152,2048]{1,0:T(8,128)(2,1)}) custom-call(bf16[288,2048]{1,0:T(8,128)(2,1)} %copy-done.65, bf16[288,2048]{1,0:T(8,128)(2,1)} %collective-permute-done.33.refs_1_, bf16[288,2048]{1,0:T(8,128)(2,1)} %copy-done.128, ...), custom_call_target="tpu_custom_call" | custom-call | flops 38654705664 | bytes 80740352 | tf_op jit(solution)/shard_map/pallas_call | solution.py:352
  525.6 28.0 %convolution_convert_fusion.2 = bf16[2048,4096]{1,0:T(8,128)(2,1)} fusion(bf16[1152,2048]{1,0:T(8,128)(2,1)} %get-tuple-element.136, bf16[1152,4096]{1,0:T(8,128)(2,1)} %get-tuple-element.141), kind=kOutput, calls=%fused_computation.4 | convolution fusion | flops 19335741440 | bytes 30932992 | tf_op jit(solution)/shard_map/dot_general | solution.py:301
  565.3 18.6 %fusion.11 = f32[576,2048]{1,0:T(8,128)} fusion(bf16[2048,4096]{1,0:T(8,128)(2,1)} %all-gather.11.cloned.1.call-done.refs_6_, bf16[1152,4096]{1,0:T(8,128)(2,1)} %get-tuple-element.144), kind=kOutput, calls=%fused_computation.49 | convolution fusion | flops 9663676416 | bytes 26214400 | tf_op jit(solution)/shard_map/dot_general | solution.py:297
  583.9 17.7 %fusion.21 = f32[576,2048]{1,0:T(8,128)} fusion(f32[576,2048]{1,0:T(8,128)} %fusion.11, bf16[2048,4096]{1,0:T(8,128)(2,1)} %all-gather.9.cloned.1.call-done.refs_5_, bf16[1152,4096]{1,0:T(8,128)(2,1)} %get-tuple-element.141), kind=kOutput, calls=%fused_computation.62 | convolution fusion | flops 9664856064 | bytes 30932992 | tf_op jit(solution)/shard_map/dot_general | solution.py:297
  604.1 16.8 %fusion.7 = f32[576,2048]{1,0:T(8,128)} fusion(bf16[2048,4096]{1,0:T(8,128)(2,1)} %all-gather.11.cloned.1.call-done.refs_6_, bf16[1152,4096]{1,0:T(8,128)(2,1)} %get-tuple-element.144), kind=kOutput, calls=%fused_computation.45 | convolution fusion | flops 9663676416 | bytes 26214400 | tf_op jit(solution)/shard_map/dot_general | solution.py:297
  620.9 17.5 %fusion.24 = f32[576,2048]{1,0:T(8,128)} fusion(f32[576,2048]{1,0:T(8,128)} %fusion.7, bf16[2048,4096]{1,0:T(8,128)(2,1)} %all-gather.9.cloned.1.call-done.refs_5_, bf16[1152,4096]{1,0:T(8,128)(2,1)} %get-tuple-element.141), kind=kOutput, calls=%fused_computation.63 | convolution fusion | flops 9664856064 | bytes 30932992 | tf_op jit(solution)/shard_map/dot_general | solution.py:297
  640.6 28.1 %convolution_convert_fusion.1 = bf16[2048,4096]{1,0:T(8,128)(2,1)} fusion(bf16[1152,2048]{1,0:T(8,128)(2,1)} %get-tuple-element.136, bf16[1152,4096]{1,0:T(8,128)(2,1)} %get-tuple-element.144), kind=kOutput, calls=%fused_computation.3 | convolution fusion | flops 19335741440 | bytes 30932992 | tf_op jit(solution)/shard_map/dot_general | solution.py:301
  674.7 28.5 %convolution_convert_fusion = bf16[4096,2048]{1,0:T(8,128)(2,1)} fusion(bf16[1152,4096]{1,0:T(8,128)(2,1)} %get-tuple-element.148, bf16[1152,2048]{1,0:T(8,128)(2,1)} %copy-done.81), kind=kOutput, calls=%fused_computation.2 | convolution fusion | flops 19335741440 | bytes 30932992 | tf_op jit(solution)/shard_map/dot_general | solution.py:301
  703.2 27.1 %convolution_convert_fusion.6 = bf16[1152,2048]{1,0:T(8,128)(2,1)} fusion(bf16[1152,4096]{1,0:T(8,128)(2,1)} %get-tuple-element.148, bf16[4096,2048]{1,0:T(8,128)(2,1)} %all-gather.5.cloned.1.call-done), kind=kOutput, calls=%fused_computation.11 | convolution fusion | flops 19329712128 | bytes 30932992 | tf_op jit(solution)/shard_map/dot_general | solution.py:293
  802.9 8.8 add_convert_fusion.1
  829.4 8.8 fusion.133.joint
  848.8 8.7 add_convert_fusion
  881.0 45.4 %collective-permute-done.60 = bf16[256,3072]{1,0:T(8,128)(2,1)} collective-permute-done((bf16[256,3072]{1,0:T(8,128)(2,1)}, bf16[256,3072]{1,0:T(8,128)(2,1)}, u32[]{:S(2)}, u32[]{:S(2)}) %collective-permute-start.60) | collective-permute-done | bytes 1572896 | tf_op jit(solution)/shard_map/ppermute | solution.py:122
  929.6 13.6 %collective-permute-done.48 = bf16[384,2560]{1,0:T(8,128)(2,1)} collective-permute-done((bf16[384,2560]{1,0:T(8,128)(2,1)}, bf16[384,2560]{1,0:T(8,128)(2,1)}, u32[]{:S(2)}, u32[]{:S(2)}) %collective-permute-start.48) | collective-permute-done | bytes 1966112 | tf_op jit(solution)/shard_map/ppermute | solution.py:122
  945.1 36.1 %collective-permute-done.50 = bf16[400,2560]{1,0:T(8,128)(2,1)S(1)} collective-permute-done((bf16[400,2560]{1,0:T(8,128)(2,1)S(1)}, bf16[400,2560]{1,0:T(8,128)(2,1)S(1)}, u32[]{:S(2)}, u32[]{:S(2)}) %collective-permute-start.50) | collective-permute-done | bytes 2048032 | tf_op jit(solution)/shard_map/ppermute | solution.py:122
  985.7 10.7 collective-permute-done.61
  1006.5 14.1 %collective-permute-done.51 = bf16[200,2560]{1,0:T(8,128)(2,1)S(1)} collective-permute-done((bf16[200,2560]{1,0:T(8,128)(2,1)S(1)}, bf16[200,2560]{1,0:T(8,128)(2,1)S(1)}, u32[]{:S(2)}, u32[]{:S(2)}) %collective-permute-start.51) | collective-permute-done | bytes 1024032 | tf_op jit(solution)/shard_map/ppermute | solution.py:122
  1038.9 34.1 %collective-permute-start.54 = (bf16[97,2560]{1,0:T(8,128)(2,1)}, bf16[97,2560]{1,0:T(8,128)(2,1)}, u32[]{:S(2)}, u32[]{:S(2)}) collective-permute-start(bf16[97,2560]{1,0:T(8,128)(2,1)} %pad_maximum_fusion.18), channel_id=1, source_target_pairs={{0,1},{1,2},{2,3},{3,0},{4,5},{5,6},{6,7},{7,4},{8,9},{9,10},{10,1... | collective-permute-start | bytes 1489928 | tf_op jit(solution)/shard_map/ppermute | solution.py:133
  1073.0 12.9 %collective-permute-done.63 = bf16[64,3072]{1,0:T(8,128)(2,1)S(1)} collective-permute-done((bf16[64,3072]{1,0:T(8,128)(2,1)S(1)}, bf16[64,3072]{1,0:T(8,128)(2,1)S(1)}, u32[]{:S(2)}, u32[]{:S(2)}) %collective-permute-start.63) | collective-permute-done | bytes 393248 | tf_op jit(solution)/shard_map/ppermute | solution.py:133
  1087.9 13.8 %collective-permute-done.53 = bf16[97,2560]{1,0:T(8,128)(2,1)} collective-permute-done((bf16[97,2560]{1,0:T(8,128)(2,1)}, bf16[97,2560]{1,0:T(8,128)(2,1)}, u32[]{:S(2)}, u32[]{:S(2)}) %collective-permute-start.53) | collective-permute-done | bytes 496672 | tf_op jit(solution)/shard_map/ppermute | solution.py:133
  (693 shorter events, 425.7 us)
Async XLA Ops:
  7.2 78.8 %all-gather.7.cloned.1.call-start = ((), (), s32[]{:S(2)}) async-start(), calls=%async_computation.5 | async-start | bytes 14155776 | tf_op jit(solution)/shard_map/all_gather | solution.py:474
  11.1 379.5 %all-gather.5.cloned.1.call-start = ((), (), s32[]{:S(2)}) async-start(), calls=%async_computation.4 | async-start | bytes 18874368 | tf_op jit(solution)/shard_map/all_gather | solution.py:472
  11.9 462.7 %all-gather.9.cloned.1.call-start = ((), (), s32[]{:S(2)}) async-start(), calls=%async_computation.6 | async-start | bytes 18874368 | tf_op jit(solution)/shard_map/all_gather | solution.py:471
  12.6 462.0 %all-gather.11.cloned.1.call-start = ((), (), s32[]{:S(2)}) async-start(), calls=%async_computation.7 | async-start | bytes 18874368 | tf_op jit(solution)/shard_map/all_gather | solution.py:475
  86.0 467.5 %reduce-scatter.5.cloned.1.call-start = ((), (), s32[]{:S(2)}) async-start(), calls=%async_computation.8 | async-start | bytes 14155776 | tf_op jit(solution)/shard_map/reduce_scatter | solution.py:600
  89.9 72.4 %collective-permute-start.4 = (bf16[384,2560]{1,0:T(8,128)(2,1)S(1)}, bf16[384,2560]{1,0:T(8,128)(2,1)S(1)}, u32[]{:S(2)}, u32[]{:S(2)}) collective-permute-start(bf16[384,2560]{1,0:T(8,128)(2,1)S(1)} %pad_maximum_fusion.1), channel_id=1, source_target_pairs={{0,16},{4,20},{8,24},{12,28},{16,0},{20,4},{24,8},{28,12},{1,17},{... | collective-permute-start | bytes 5898248 | tf_op jit(solution)/shard_map/ppermute | solution.py:26
  90.8 73.1 %collective-permute-start.3 = (bf16[384,2560]{1,0:T(8,128)(2,1)S(1)}, bf16[384,2560]{1,0:T(8,128)(2,1)S(1)}, u32[]{:S(2)}, u32[]{:S(2)}) collective-permute-start(bf16[384,2560]{1,0:T(8,128)(2,1)S(1)} %pad_maximum_fusion.1), channel_id=1, source_target_pairs={{0,8},{4,12},{8,0},{12,4},{16,24},{20,28},{24,16},{28,20},{1,9},{5... | collective-permute-start | bytes 5898248 | tf_op jit(solution)/shard_map/ppermute | solution.py:26
  126.9 45.9 %collective-permute-start.11 = (bf16[288,2048]{1,0:T(8,128)(2,1)}, bf16[288,2048]{1,0:T(8,128)(2,1)}, u32[]{:S(2)}, u32[]{:S(2)}) collective-permute-start(bf16[288,2048]{1,0:T(8,128)(2,1)} %collective-permute-done.9), channel_id=1, source_target_pairs={{0,1},{1,2},{2,3},{3,0},{4,5},{5,6},{6,7},{7,4},{8,9},{9,10},{10,1... | collective-permute-start | bytes 3538952 | tf_op jit(solution)/shard_map/ppermute | solution.py:26
  164.0 71.2 %collective-permute-start.24 = (bf16[256,3072]{1,0:T(8,128)(2,1)}, bf16[256,3072]{1,0:T(8,128)(2,1)}, u32[]{:S(2)}, u32[]{:S(2)}) collective-permute-start(bf16[256,3072]{1,0:T(8,128)(2,1)} %get-tuple-element.116), channel_id=1, source_target_pairs={{0,8},{4,12},{8,0},{12,4},{16,24},{20,28},{24,16},{28,20},{1,9},{5... | collective-permute-start | bytes 4718600 | tf_op jit(solution)/shard_map/ppermute | solution.py:26
  166.0 92.3 %collective-permute-start.25 = (bf16[256,3072]{1,0:T(8,128)(2,1)}, bf16[256,3072]{1,0:T(8,128)(2,1)}, u32[]{:S(2)}, u32[]{:S(2)}) collective-permute-start(bf16[256,3072]{1,0:T(8,128)(2,1)} %get-tuple-element.116), channel_id=1, source_target_pairs={{0,16},{4,20},{8,24},{12,28},{16,0},{20,4},{24,8},{28,12},{1,17},{... | collective-permute-start | bytes 4718600 | tf_op jit(solution)/shard_map/ppermute | solution.py:26
  169.1 91.3 %collective-permute-start.6 = (bf16[192,2560]{1,0:T(8,128)(2,1)S(1)}, bf16[192,2560]{1,0:T(8,128)(2,1)S(1)}, u32[]{:S(2)}, u32[]{:S(2)}) collective-permute-start(bf16[192,2560]{1,0:T(8,128)(2,1)S(1)} %slice.531), channel_id=1, source_target_pairs={{0,8},{4,12},{8,0},{12,4},{16,24},{20,28},{24,16},{28,20},{1,9},{5... | collective-permute-start | bytes 2949128 | tf_op jit(solution)/shard_map/ppermute | solution.py:26
  170.5 86.3 %collective-permute-start.5 = (bf16[192,2560]{1,0:T(8,128)(2,1)S(1)}, bf16[192,2560]{1,0:T(8,128)(2,1)S(1)}, u32[]{:S(2)}, u32[]{:S(2)}) collective-permute-start(bf16[192,2560]{1,0:T(8,128)(2,1)S(1)} %slice.530), channel_id=1, source_target_pairs={{0,16},{4,20},{8,24},{12,28},{16,0},{20,4},{24,8},{28,12},{1,17},{... | collective-permute-start | bytes 2949128 | tf_op jit(solution)/shard_map/ppermute | solution.py:26
  172.8 94.3 %collective-permute-start.12 = (bf16[288,2048]{1,0:T(8,128)(2,1)}, bf16[288,2048]{1,0:T(8,128)(2,1)S(1)}, u32[]{:S(2)}, u32[]{:S(2)}) collective-permute-start(bf16[288,2048]{1,0:T(8,128)(2,1)} %collective-permute-done.11), channel_id=1, source_target_pairs={{0,1},{1,2},{2,3},{3,0},{4,5},{5,6},{6,7},{7,4},{8,9},{9,10},{10,1... | collective-permute-start | bytes 3538952 | tf_op jit(solution)/shard_map/ppermute | solution.py:26
  235.2 38.4 %collective-permute-start.28 = (bf16[256,3072]{1,0:T(8,128)(2,1)}, bf16[256,3072]{1,0:T(8,128)(2,1)S(1)}, u32[]{:S(2)}, u32[]{:S(2)}) collective-permute-start(bf16[256,3072]{1,0:T(8,128)(2,1)} %get-tuple-element.116), channel_id=1, source_target_pairs={{0,4},{4,0},{8,12},{12,8},{16,20},{20,16},{24,28},{28,24},{1,5},{5... | collective-permute-start | bytes 4718600 | tf_op jit(solution)/shard_map/ppermute | solution.py:38
  258.3 36.4 %collective-permute-start.26 = (bf16[128,3072]{1,0:T(8,128)(2,1)S(1)}, bf16[128,3072]{1,0:T(8,128)(2,1)}, u32[]{:S(2)}, u32[]{:S(2)}) collective-permute-start(bf16[128,3072]{1,0:T(8,128)(2,1)S(1)} %slice.548), channel_id=1, source_target_pairs={{0,16},{4,20},{8,24},{12,28},{16,0},{20,4},{24,8},{28,12},{1,17},{... | collective-permute-start | bytes 2359304 | tf_op jit(solution)/shard_map/ppermute | solution.py:26
  379.7 36.6 %collective-permute-start.33 = (bf16[288,2048]{1,0:T(8,128)(2,1)S(1)}, bf16[288,2048]{1,0:T(8,128)(2,1)}, u32[]{:S(2)}, u32[]{:S(2)}) collective-permute-start(bf16[288,2048]{1,0:T(8,128)(2,1)S(1)} %pad.59.refs_0_), channel_id=1, source_target_pairs={{0,1},{1,2},{2,3},{3,0},{4,5},{5,6},{6,7},{7,4},{8,9},{9,10},{10,1... | collective-permute-start | bytes 3538952 | tf_op jit(solution)/shard_map/ppermute | solution.py:26
  450.5 361.2 %reduce-scatter.7.cloned.1.call-start = ((), (), s32[]{:S(2)}) async-start(), calls=%async_computation.9 | async-start | bytes 18874368 | tf_op jit(solution)/shard_map/reduce_scatter | solution.py:600
  553.6 534.3 %reduce-scatter.9.cloned.1.call-start = ((), (), s32[]{:S(2)}) async-start(), calls=%async_computation.10 | async-start | bytes 18874368 | tf_op jit(solution)/shard_map/reduce_scatter | solution.py:600
  668.8 419.1 %reduce-scatter.11.cloned.1.call-start = ((), (), s32[]{:S(2)}) async-start(), calls=%async_computation.11 | async-start | bytes 18874368 | tf_op jit(solution)/shard_map/reduce_scatter | solution.py:600
  674.5 55.9 %collective-permute-start.41 = (bf16[304,2048]{1,0:T(8,128)(2,1)S(1)}, bf16[304,2048]{1,0:T(8,128)(2,1)S(1)}, u32[]{:S(2)}, u32[]{:S(2)}) collective-permute-start(bf16[304,2048]{1,0:T(8,128)(2,1)S(1)} %fusion.37), channel_id=1, source_target_pairs={{0,3},{1,0},{2,1},{3,2},{4,7},{5,4},{6,5},{7,6},{8,11},{9,8},{10,9... | collective-permute-start | bytes 3735560 | tf_op jit(solution)/shard_map/ppermute | solution.py:49
  756.5 46.3 %collective-permute-start.45 = (bf16[1024,3072]{1,0:T(8,128)(2,1)}, bf16[1024,3072]{1,0:T(8,128)(2,1)}, u32[]{:S(2)}, u32[]{:S(2)}) collective-permute-start(bf16[1024,3072]{1,0:T(8,128)(2,1)} %convolution_convert_fusion.7), channel_id=1, source_target_pairs={{0,4},{4,0},{8,12},{12,8},{16,20},{20,16},{24,28},{28,24},{1,5},{5... | collective-permute-start | bytes 18874376 | tf_op jit(solution)/shard_map/ppermute | solution.py:38
  843.5 185.8 %collective-permute-start.57 = (bf16[280,2048]{1,0:T(8,128)(2,1)}, bf16[280,2048]{1,0:T(8,128)(2,1)}, u32[]{:S(2)}, u32[]{:S(2)}) collective-permute-start(bf16[280,2048]{1,0:T(8,128)(2,1)} %get-tuple-element.307), channel_id=1, source_target_pairs={{0,1},{1,2},{2,3},{3,0},{4,5},{5,6},{6,7},{7,4},{8,9},{9,10},{10,1... | collective-permute-start | bytes 3440648 | tf_op jit(solution)/shard_map/ppermute | solution.py:133
  843.7 244.2 %collective-permute-start.56 = (bf16[280,2048]{1,0:T(8,128)(2,1)}, bf16[280,2048]{1,0:T(8,128)(2,1)}, u32[]{:S(2)}, u32[]{:S(2)}) collective-permute-start(bf16[280,2048]{1,0:T(8,128)(2,1)} %get-tuple-element.308), channel_id=1, source_target_pairs={{0,2},{1,3},{2,0},{3,1},{4,6},{5,7},{6,4},{7,5},{8,10},{9,11},{10,... | collective-permute-start | bytes 3440648 | tf_op jit(solution)/shard_map/ppermute | solution.py:133
  867.4 59.0 %collective-permute-start.60 = (bf16[256,3072]{1,0:T(8,128)(2,1)}, bf16[256,3072]{1,0:T(8,128)(2,1)}, u32[]{:S(2)}, u32[]{:S(2)}) collective-permute-start(bf16[256,3072]{1,0:T(8,128)(2,1)} %pad_maximum_fusion.5), channel_id=1, source_target_pairs={{0,16},{4,20},{8,24},{12,28},{16,0},{20,4},{24,8},{28,12},{1,17},{... | collective-permute-start | bytes 4718600 | tf_op jit(solution)/shard_map/ppermute | solution.py:122
  868.9 74.3 %collective-permute-start.48 = (bf16[384,2560]{1,0:T(8,128)(2,1)}, bf16[384,2560]{1,0:T(8,128)(2,1)}, u32[]{:S(2)}, u32[]{:S(2)}) collective-permute-start(bf16[384,2560]{1,0:T(8,128)(2,1)} %pad_maximum_fusion.2), channel_id=1, source_target_pairs={{0,8},{4,12},{8,0},{12,4},{16,24},{20,28},{24,16},{28,20},{1,9},{5... | collective-permute-start | bytes 5898248 | tf_op jit(solution)/shard_map/ppermute | solution.py:122
  879.9 101.4 %collective-permute-start.50 = (bf16[400,2560]{1,0:T(8,128)(2,1)S(1)}, bf16[400,2560]{1,0:T(8,128)(2,1)S(1)}, u32[]{:S(2)}, u32[]{:S(2)}) collective-permute-start(bf16[400,2560]{1,0:T(8,128)(2,1)S(1)} %pad_maximum_fusion), channel_id=1, source_target_pairs={{0,16},{4,20},{8,24},{12,28},{16,0},{20,4},{24,8},{28,12},{1,17},{... | collective-permute-start | bytes 6144008 | tf_op jit(solution)/shard_map/ppermute | solution.py:122
  926.4 55.4 %collective-permute-start.58 = (bf16[256,3072]{1,0:T(8,128)(2,1)S(1)}, bf16[256,3072]{1,0:T(8,128)(2,1)S(1)}, u32[]{:S(2)}, u32[]{:S(2)}) collective-permute-start(bf16[256,3072]{1,0:T(8,128)(2,1)S(1)} %pad_maximum_fusion.4), channel_id=1, source_target_pairs={{0,8},{4,12},{8,0},{12,4},{16,24},{20,28},{24,16},{28,20},{1,9},{5... | collective-permute-start | bytes 4718600 | tf_op jit(solution)/shard_map/ppermute | solution.py:122
  943.2 53.2 %collective-permute-start.61 = (bf16[128,3072]{1,0:T(8,128)(2,1)S(1)}, bf16[128,3072]{1,0:T(8,128)(2,1)S(1)}, u32[]{:S(2)}, u32[]{:S(2)}) collective-permute-start(bf16[128,3072]{1,0:T(8,128)(2,1)S(1)} %fusion.44), channel_id=1, source_target_pairs={{0,8},{4,12},{8,0},{12,4},{16,24},{20,28},{24,16},{28,20},{1,9},{5... | collective-permute-start | bytes 2359304 | tf_op jit(solution)/shard_map/ppermute | solution.py:122
  981.8 106.0 %collective-permute-start.55 = (bf16[280,2048]{1,0:T(8,128)(2,1)S(1)}, bf16[280,2048]{1,0:T(8,128)(2,1)}, u32[]{:S(2)}, u32[]{:S(2)}) collective-permute-start(bf16[280,2048]{1,0:T(8,128)(2,1)S(1)} %copy-done.68), channel_id=1, source_target_pairs={{0,3},{1,0},{2,1},{3,2},{4,7},{5,4},{6,5},{7,6},{8,11},{9,8},{10,9... | collective-permute-start | bytes 3440648 | tf_op jit(solution)/shard_map/ppermute | solution.py:133
  1029.3 56.6 %collective-permute-start.63 = (bf16[64,3072]{1,0:T(8,128)(2,1)S(1)}, bf16[64,3072]{1,0:T(8,128)(2,1)S(1)}, u32[]{:S(2)}, u32[]{:S(2)}) collective-permute-start(bf16[64,3072]{1,0:T(8,128)(2,1)S(1)} %get-tuple-element.335), channel_id=1, source_target_pairs={{0,2},{1,3},{2,0},{3,1},{4,6},{5,7},{6,4},{7,5},{8,10},{9,11},{10,... | collective-permute-start | bytes 1179656 | tf_op jit(solution)/shard_map/ppermute | solution.py:133
  1029.3 56.6 %collective-permute-start.64 = (bf16[64,3072]{1,0:T(8,128)(2,1)S(1)}, bf16[64,3072]{1,0:T(8,128)(2,1)S(1)}, u32[]{:S(2)}, u32[]{:S(2)}) collective-permute-start(bf16[64,3072]{1,0:T(8,128)(2,1)S(1)} %get-tuple-element.336), channel_id=1, source_target_pairs={{0,1},{1,2},{2,3},{3,0},{4,5},{5,6},{6,7},{7,4},{8,9},{9,10},{10,1... | collective-permute-start | bytes 1179656 | tf_op jit(solution)/shard_map/ppermute | solution.py:133
  1038.9 49.0 %collective-permute-start.54 = (bf16[97,2560]{1,0:T(8,128)(2,1)}, bf16[97,2560]{1,0:T(8,128)(2,1)}, u32[]{:S(2)}, u32[]{:S(2)}) collective-permute-start(bf16[97,2560]{1,0:T(8,128)(2,1)} %pad_maximum_fusion.18), channel_id=1, source_target_pairs={{0,1},{1,2},{2,3},{3,0},{4,5},{5,6},{6,7},{7,4},{8,9},{9,10},{10,1... | collective-permute-start | bytes 1489928 | tf_op jit(solution)/shard_map/ppermute | solution.py:133
  (181 other events, 2848.7 us)
Sparse Core Ops, SparseCore 0:
  11.1 74.8 all-gather.6
  87.9 155.5 all-gather.4
  245.4 106.8 all-gather.8
  354.1 89.8 all-gather.10
  450.6 89.6 reduce-scatter.4
  553.7 113.2 reduce-scatter.6
  670.6 115.9 reduce-scatter.8
  790.1 160.6 reduce-scatter.10
